TPU v7x, 256 devices: a whole 4x4x8 slice. The times are simulated.
256 devices in a mesh: grp: 2 (over y_hi), sub: 128 (over y_lo, x, z, core).
Axes of the slice: x: 4, y: 4 (y_hi: 2, y_lo: 2; y = y_hi * 2 + y_lo), z: 8, core: 2. Of those that a mesh axis runs over, the one named last changes fastest.
Arguments:
- fluid_state: float32 [5, 64, 262144], P(None, None, ('grp', 'sub')), may hold values from -6 to 6
- flux_jacobian: float32 [3, 5, 5], replicated, may hold values from -1.5 to 1.5
- solid_temp: float32 [256, 256, 256], P(None, 'sub', 'grp'), may hold values from -6 to 6
- iface_elem: int32 [32768], P(('grp', 'sub')), may hold values from 0 to 1023, as said below
- iface_owner: int32 [32768, 1], P(('grp', 'sub')), may hold values from 0 to 127; in each aligned block of 128 rows (0 to 127, 128 to 255, ...) at most 2 rows name the same one
- iface_patch: int32 [32768], P(('grp', 'sub')), may hold values from 0 to 15
Outputs:
- fluid_out: float32 [5, 64, 262144], P(None, None, ('grp', 'sub'))
- solid_out: float32 [256, 256, 256], P(None, 'sub', 'grp')
Inputs may be any that keep to these rules, and one draw needn't show every extreme that they name: `iface_elem`: within the 128 entries of one device the elements are distinct. `iface_owner`: among the 128 rows of one device no owner appears more than 2 times; in every draw some owner appears exactly 2 times.
All inputs are finite; a program needn't handle non-finite values.
Results may differ from a plain program's by a relative error of at most 0.0003.
Values sent between devices are 32-bit elements; how exact they have to be, the bound alone decides.
No kernel may reach another device: no remote copies, remote signals or barrier semaphores. Data moves between devices by JAX's collectives and lax.ppermute only.
A program may use at most 64 MiB of HBM per device.

v0:
```python
import jax
import jax.numpy as jnp
import numpy as np
from jax import lax
from jax.sharding import Mesh, PartitionSpec as P

ALL = ("g", "yl", "x", "z", "c")
SUB = ("yl", "x", "z", "c")
SAME_CORE = ("g", "yl", "x", "z")
N = 256
HALF = 128
DT = 0.05
VISC = 0.05
GAIN = 0.3
HIGH = lax.Precision.HIGH
F32 = jnp.float32


def sine_table(length):
    numbers = np.arange(length) + 1
    phases = numbers[:, None] * numbers[None, :] % (2 * (length + 1))
    return np.sqrt(2.0 / (length + 1)) * np.sin(np.pi * phases / (length + 1))


def rates(length):
    return 2.0 - 2.0 * np.cos(np.pi * (np.arange(length) + 1) / (length + 1))


SINE = sine_table(N)
RATES = rates(N)
MODE_ORDER = np.array([2 * q + k for k in range(2) for q in range(HALF)])
X_ORDER = np.array([4 * j + 2 * k + i for i in range(2) for k in range(2) for j in range(64)])


def surface_response():
    total = np.zeros((N, N))
    for c in range(N):
        total += SINE[0, c] ** 2 / (1.0 + 64.0 * (RATES[c] + RATES[:, None] + RATES[None, :]))
    return total


Q = SINE.astype(np.float32)
RESPONSE = surface_response()[MODE_ORDER].astype(np.float32)
Q_MODES = Q[MODE_ORDER]
Q_X = Q[:, X_ORDER]


def lobatto_derivative():
    points = np.array([-1.0, -1.0 / np.sqrt(5.0), 1.0 / np.sqrt(5.0), 1.0])
    weights = np.array(
        [1.0 / np.prod([points[j] - points[k] for k in range(4) if k != j]) for j in range(4)]
    )
    deriv = np.zeros((4, 4))
    for i in range(4):
        for j in range(4):
            if i != j:
                deriv[i, j] = weights[j] / weights[i] / (points[i] - points[j])
        deriv[i, i] = -np.sum(deriv[i])
    return deriv


def operator_parts():
    deriv, eye = lobatto_derivative(), np.eye(4)
    along = [
        np.kron(eye, np.kron(eye, deriv)),
        np.kron(eye, np.kron(deriv, eye)),
        np.kron(deriv, np.kron(eye, eye)),
    ]
    second = sum(d @ d for d in along)
    pick = np.zeros((4, 4, 4, 4))
    for i in range(4):
        for j in range(4):
            pick[i, j, i, j] = 1.0
    eye16 = np.eye(16)
    right, left = np.kron(eye16, pick[3, 3]), np.kron(eye16, pick[0, 0])
    right_from, left_from = np.kron(eye16, pick[3, 0]), np.kron(eye16, pick[0, 3])
    fixed = np.kron(np.eye(5), np.eye(64) - 0.15 * right - 0.15 * left)
    fixed = fixed + DT * VISC * np.kron(np.diag([0.0, 1.0, 1.0, 1.0, 1.0]), second)
    by_x = -DT * along[0] + 0.15 * right - 0.15 * left
    return [
        np.asarray(a, np.float32)
        for a in (
            fixed,
            by_x,
            -DT * along[1],
            -DT * along[2],
            np.kron(np.eye(5), 0.15 * right_from),
            -0.15 * right_from,
            np.kron(np.eye(5), 0.15 * left_from),
            0.15 * left_from,
        )
    ]


FIXED, BY_X, BY_Y, BY_Z, NEXT_FIXED, NEXT_X, PREV_FIXED, PREV_X = operator_parts()


def mm(a, b):
    return lax.dot_general(a, b, (((1,), (0,)), ((), ())), precision=HIGH)


def mm_nt(a, b):
    return lax.dot_general(a, b, (((1,), (1,)), ((), ())), precision=HIGH)


def mm_tn(a, b):
    return lax.dot_general(a, b, (((0,), (0,)), ((), ())), precision=HIGH)


def step_matrices(flux_jacobian):
    own = (
        FIXED
        + jnp.kron(flux_jacobian[0], BY_X)
        + jnp.kron(flux_jacobian[1], BY_Y)
        + jnp.kron(flux_jacobian[2], BY_Z)
    )
    following = NEXT_FIXED + jnp.kron(flux_jacobian[0], NEXT_X)
    preceding = PREV_FIXED + jnp.kron(flux_jacobian[0], PREV_X)
    return own, following, preceding


def chain_halo(fluid):
    last, first = fluid[:, -1:], fluid[:, :1]
    before = lax.ppermute(last, ALL, [(i, i + 1) for i in range(255)])
    after = lax.ppermute(first, ALL, [(i + 1, i) for i in range(255)])
    return before, after


def fluid_step(fluid, matrices, halo):
    own, following, preceding = matrices
    before, after = halo
    shifted_next = jnp.concatenate([fluid[:, 1:], after], axis=1)
    shifted_prev = jnp.concatenate([before, fluid[:, :-1]], axis=1)
    return mm(own, fluid) + mm(following, shifted_next) + mm(preceding, shifted_prev)


def wall(fluid):
    return fluid[256:272] - fluid[0:16]


def patch_values(surface_t, x_hot, chunk_hot, fold):
    return mm(fold, mm(surface_t, x_hot) * chunk_hot)


def on_device(fluid_state, flux_jacobian, solid_temp, iface_elem, iface_owner, iface_patch):
    me = lax.axis_index(ALL)
    group, core = me // HALF, me % 2
    sine = jnp.asarray(Q)
    sine_half = lax.dynamic_slice(sine, (0, group * HALF), (N, HALF))

    pay1 = jnp.concatenate([mm_nt(sine_half, solid_temp[:, i, :]) for i in range(2)], axis=1)
    got1 = lax.all_to_all(pay1, ALL, split_axis=0, concat_axis=0, tiled=True)

    fluid0 = fluid_state.reshape(320, -1)
    matrices = step_matrices(flux_jacobian)
    fluid1 = fluid_step(fluid0, matrices, chain_halo(fluid0))
    elem_hot = (iface_elem[:, None] == jnp.arange(fluid0.shape[1])[None, :]).astype(F32)
    wall0, wall1 = wall(fluid0), wall(fluid1)
    slot_values = mm_nt(jnp.concatenate([wall0, wall1 - GAIN * wall0], axis=0), elem_hot)
    trace0 = slot_values[:16]

    owners = iface_owner[:, 0]
    patch = iface_patch
    same = (owners[:, None] == owners[None, :]) & (
        jnp.arange(HALF)[:, None] < jnp.arange(HALF)[None, :]
    )
    place = jnp.sum(same.astype(jnp.int32), axis=0)
    sent = jnp.concatenate(
        [slot_values, (patch + 1).astype(F32)[None, :], jnp.zeros((31, HALF), F32)], axis=0
    )
    lanes = []
    for i in range(2):
        hot = (jnp.arange(HALF)[:, None] == owners[None, :]) & (place == i)[None, :]
        lanes.append(mm_nt(hot.astype(F32), sent))
    got_fluid = lax.all_to_all(
        jnp.concatenate(lanes, axis=1), SUB, split_axis=0, concat_axis=0, tiled=True
    )

    lane = np.arange(HALF)
    spread = np.zeros((2, HALF, 2 * HALF), np.float32)
    for i in range(2):
        for f in range(2):
            spread[i, i * 64 + f * 16 + lane % 16, f * HALF + lane] = 1.0
    sums = [[0.0, 0.0], [0.0, 0.0]]
    counts = [0.0, 0.0]
    count_lanes = 0.0
    for i in range(2):
        ids = got_fluid[:, i * 64 + 32 : i * 64 + 33] - 1.0
        values = mm(got_fluid, spread[i])
        count_lanes = count_lanes + jnp.sum((ids == lane).astype(F32), axis=0, keepdims=True)
        for xl in range(2):
            mask = ids == (xl * 8 + lane // 16)
            counts[xl] = counts[xl] + jnp.sum(mask.astype(F32), axis=0, keepdims=True)
            for f in range(2):
                part = jnp.where(mask, values[:, f * HALF : (f + 1) * HALF], 0.0)
                sums[f][xl] = sums[f][xl] + jnp.sum(part, axis=0, keepdims=True)
    heat0 = [sums[0][xl] - counts[xl] * solid_temp[0, xl : xl + 1, :] for xl in range(2)]
    later = jnp.concatenate(sums[1], axis=0)

    sine_surface = sine[0:1]
    modes = 0.0
    for i in range(2):
        by_z = mm_nt(sine, got1[:, i * N : (i + 1) * N])
        modes = modes + mm(by_z, np.concatenate([Q[:, i::2].T] * 2, axis=0))
    own_rate = lax.dynamic_slice(jnp.asarray(RATES, F32), (me,), (1,))
    z_x_rates = (1.0 + 64.0 * (RATES[:, None] + RATES[None, :])).astype(np.float32)
    decay = 1.0 / (z_x_rates + 64.0 * own_rate[0])
    once = decay * modes
    surface_row = mm(sine_surface, once)

    sine_modes = jnp.asarray(Q_MODES)
    modes_half = lax.dynamic_slice(sine_modes, (0, group * HALF), (N, HALF))
    later_modes = mm_nt(modes_half, later)
    shared = jnp.concatenate([surface_row, heat0[0], heat0[1]], axis=1)
    tail = jnp.concatenate(
        [
            jnp.broadcast_to(count_lanes[:, :16], (HALF, 16)),
            later_modes[:HALF],
            later_modes[HALF:],
            jnp.zeros((HALF, 108), F32),
        ],
        axis=1,
    )
    pay2 = jnp.concatenate([jnp.broadcast_to(shared, (HALF, 512)), tail], axis=1)
    got2 = lax.all_to_all(pay2, SAME_CORE, split_axis=0, concat_axis=0, tiled=True)
    other = lax.ppermute(got2, "c", [(0, 1), (1, 0)])
    first = core == 0
    gathered = jnp.concatenate(
        [jnp.where(first, got2, other), jnp.where(first, other, got2)], axis=0
    )

    def block(g, lo, hi):
        return jnp.concatenate(
            [gathered[k * HALF + g * 64 : k * HALF + g * 64 + 64, lo:hi] for k in range(2)], axis=0
        )

    heat_modes = 0.0
    for xl in range(2):
        by_y = 0.0
        for g in range(2):
            by_y = by_y + mm_nt(
                Q_MODES[:, g * HALF : (g + 1) * HALF],
                block(g, N + xl * HALF, N + (xl + 1) * HALF),
            )
        heat_modes = heat_modes + mm(by_y, Q_X[:, xl * HALF : (xl + 1) * HALF].T)
    surface1_modes = gathered[:, :N] + RESPONSE * heat_modes
    surface1 = mm(mm(Q_MODES.T, surface1_modes), Q_X)
    tails = [block(g, 512, 640) for g in range(2)]
    expand = [
        (lane[None, :] == (xl * 8 + lane // 16)[:, None]).astype(np.float32) for xl in range(2)
    ]
    count_t = jnp.concatenate(
        [
            jnp.concatenate([mm_nt(expand[xl], tails[g]) for xl in range(2)], axis=1)
            for g in range(2)
        ],
        axis=0,
    )
    own_sine = lax.dynamic_slice(sine, (me, 0), (1, N))
    reduced = mm(own_sine, count_t * surface1)
    tail_sum = tails[0] + tails[1]
    later_row = jnp.concatenate(
        [
            mm_nt((lane[None, :] == 16 + 2 * core + xl).astype(F32), tail_sum)
            for xl in range(2)
        ],
        axis=1,
    )
    heat1_modes = mm(later_row - 0.7 * reduced, Q_X.T)
    heat0_modes = lax.dynamic_slice(heat_modes, (core * HALF + me // 2, 0), (1, N))
    surface_column = jnp.asarray(Q[0][:, None])
    final = decay * (decay * (modes + surface_column * heat0_modes) + surface_column * heat1_modes)
    final_row = mm(sine_surface, final)

    back = [mm(mm_nt(Q[:, xl::2].T, final), sine) for xl in range(2)]
    pay3 = jnp.concatenate(back + [jnp.broadcast_to(final_row, (HALF, N))], axis=1)
    got3 = lax.all_to_all(
        jnp.concatenate([pay3, pay3], axis=0), ALL, split_axis=0, concat_axis=0, tiled=True
    )

    x_of_slot = patch // 8 * HALF + owners % 2 * 64 + owners // 2
    x_hot = (jnp.arange(N)[:, None] == x_of_slot[None, :]).astype(F32)
    chunk_hot = ((lane // 16)[:, None] == (patch % 8)[None, :]).astype(F32)
    fold = (np.arange(16)[:, None] == (lane % 16)[None, :]).astype(np.float32)
    own_surface1 = lax.dynamic_slice(surface1, (group * HALF, 0), (HALF, N))
    patch1 = patch_values(own_surface1, x_hot, chunk_hot, fold)
    source0 = GAIN * mm(patch1 - trace0, elem_hot)
    fluid1 = jnp.concatenate([fluid1[:256], fluid1[256:272] + source0, fluid1[272:]], axis=0)
    trace1 = mm_nt(wall(fluid1), elem_hot)
    fluid2 = fluid_step(fluid1, matrices, chain_halo(fluid1))

    sine_back = sine_half.T
    solid_out = jnp.stack(
        [mm_tn(got3[:, xl * N : (xl + 1) * N], sine_half) for xl in range(2)], axis=1
    )
    surface2 = mm(mm(sine_back, got3[:, 512:]), Q_X)
    patch2 = patch_values(surface2, x_hot, chunk_hot, fold)
    source1 = GAIN * mm(patch2 - trace1, elem_hot)
    fluid2 = jnp.concatenate([fluid2[:256], fluid2[256:272] + source1, fluid2[272:]], axis=0)
    return fluid2.reshape(fluid_state.shape), solid_out


def solution(mesh):
    fine = Mesh(mesh.devices.reshape(2, 2, 4, 8, 2), ALL)
    placed = (
        P(None, None, ALL),
        P(),
        P(None, SUB, "g"),
        P(ALL),
        P(ALL, None),
        P(ALL),
    )
    return jax.shard_map(
        on_device,
        mesh=fine,
        in_specs=placed,
        out_specs=(P(None, None, ALL), P(None, SUB, "g")),
        check_vma=False,
    )
```

profile of v0, /device:TPU:1, one launch (start us, length us, event | category | flops | bytes accessed | tf_op | source)
XLA Modules:
  0.0 167.1 jit_solution(14009839738026281149)
XLA Ops:
  0.6 1.8 %fusion.153 = (f32[320,1]{1,0:T(8,128)}, f32[320,1]{1,0:T(8,128)}) fusion(f32[320,1024]{1,0:T(8,128)} %bitcast.145), kind=kLoop, calls=%fused_computation.239 | loop fusion | bytes 5120 | tf_op jit(solution)/shard_map/slice | solution.py:123
  2.4 5.1 %collective-permute-start = (f32[320,1]{1,0:T(8,128)}, f32[320,1]{1,0:T(8,128)}, u32[]{:S(2)}, u32[]{:S(2)}) collective-permute-start(f32[320,1]{1,0:T(8,128)} %get-tuple-element.43), channel_id=1, source_target_pairs={{1,0},{2,1},{3,2},{4,3},{5,4},{6,5},{7,6},{8,7},{9,8},{10,9},{11,1... | collective-permute-start | bytes 3848 | tf_op jit(solution)/shard_map/ppermute | solution.py:125
  7.7 2.1 %collective-permute-start.1 = (f32[320,1]{1,0:T(8,128)}, f32[320,1]{1,0:T(8,128)}, u32[]{:S(2)}, u32[]{:S(2)}) collective-permute-start(f32[320,1]{1,0:T(8,128)} %get-tuple-element.42), channel_id=1, source_target_pairs={{0,1},{1,2},{2,3},{3,4},{4,5},{5,6},{6,7},{7,8},{8,9},{9,10},{10,1... | collective-permute-start | bytes 3848 | tf_op jit(solution)/shard_map/ppermute | solution.py:124
  9.7 3.9 %fusion.154 = (f32[320,1023]{1,0:T(8,128)}, f32[320,1023]{1,0:T(8,128)}) fusion(f32[320,1024]{1,0:T(8,128)} %bitcast.146), kind=kLoop, calls=%fused_computation.240 | loop fusion | bytes 5237760 | tf_op jit(solution)/shard_map/slice | solution.py:133
  13.7 3.8 %multiply_add_fusion = (f32[5,64,5,64]{3,2,1,0:T(8,128)S(1)}, f32[5,64,5,64]{3,2,1,0:T(8,128)}, f32[5,64,5,64]{3,2,1,0:T(8,128)}) fusion(f32[5,64,5,64]{3,2,1,0:T(8,128)} %constant.242, f32[64,64]{1,0:T(8,128)S(1)} %copy-done.38, f32[5,5]{1,0:T(8,128)S(1)} %bitcast.160, f32[5,64,5,64]{3,2,1,0:T(8,128)} %constant.241, f32[64,64]{1,0:T(8,128)S(1)} %copy-done.37, ...), kind=kLoop, calls=%fused_computation.19 | loop fusion | flops 1024000 | bytes 2539820 | tf_op jit(solution)/shard_map/add | solution.py:118
  17.5 1.6 reshape.232
  19.2 2.3 %fusion.160 = f32[320,1024]{1,0:T(8,128)} fusion(f32[320,320]{1,0:T(8,128)S(1)} %reshape.232, f32[320,1024]{1,0:T(8,128)S(1)} %bitcast.147), kind=kOutput, calls=%fused_computation.246 | convolution fusion | flops 629145600 | bytes 3031040 | tf_op jit(solution)/shard_map/dot_general | solution.py:99
  21.6 1.9 %fusion.157 = (f32[256,1,128]{2,1,0:T(1,128)S(1)}, f32[256,1,128]{2,1,0:T(1,128)}) fusion(f32[256,2,128]{2,1,0:T(2,128)} %param.48), kind=kLoop, calls=%fused_computation.243 | loop fusion | bytes 524288 | tf_op jit(solution)/shard_map/slice | solution.py:151
  23.5 1.9 %fusion.18 = f32[256,256]{0,1:T(8,128)} fusion(f32[256,128]{1,0:T(8,128)} %bitcast.159, f32[256,256]{1,0:T(8,128)S(1)} %copy-done.1, s32[]{:T(128)S(6)} %select_n.86), kind=kOutput, calls=%fused_computation.46 | convolution fusion | flops 50331648 | bytes 524292 | tf_op jit(solution)/shard_map/dot_general | solution.py:103
  26.4 2.3 %reshape.228 = f32[320,320]{1,0:T(8,128)} reshape(f32[5,64,5,64]{3,2,1,0:T(8,128)} %get-tuple-element.68) | data formatting | bytes 819200 | tf_op jit(solution)/shard_map/add | solution.py:117
  29.9 3.3 %convolution_add_fusion.3 = f32[320,1024]{1,0:T(8,128)S(1)} fusion(f32[320,1024]{1,0:T(8,128)} %fusion.160, f32[320,320]{1,0:T(8,128)} %reshape.228, f32[320,1]{1,0:T(8,128)} %collective-permute-done, f32[320,1023]{1,0:T(8,128)} %get-tuple-element.45), kind=kOutput, calls=%fused_computation.3 | convolution fusion | flops 629800960 | bytes 4341760 | tf_op jit(solution)/shard_map/dot_general | solution.py:99
  33.3 2.3 %convolution_add_fusion.2 = f32[320,1024]{1,0:T(8,128)S(1)} fusion(f32[320,1024]{1,0:T(8,128)S(1)} %convolution_add_fusion.3, f32[320,320]{1,0:T(8,128)S(1)} %copy-done.3, f32[320,1023]{1,0:T(8,128)S(1)} %copy-done.2, f32[320,1]{1,0:T(8,128)} %collective-permute-done.1), kind=kOutput, calls=%fused_computation.2 | convolution fusion | flops 629800960 | bytes 4341760 | tf_op jit(solution)/shard_map/dot_general | solution.py:99
  37.1 15.3 %all-to-all-start.1 = ((f32[128,1,128]{2,1,0:T(1,128)}), f32[128,1,128]{2,1,0:T(1,128)S(1)}, u32[]{:S(2)}, u32[]{:S(2)}) async-start(f32[128,1,128]{2,1,0:T(1,128)} %copy.90), calls=%async_computation.1 | async-start | bytes 131072 | tf_op jit(solution)/shard_map/all_to_all | solution.py:175
  52.5 1.1 maximum_bitcast_fusion.1
  55.9 7.2 %all-to-all-done.1 = f32[128,1,128]{2,1,0:T(1,128)S(1)} async-done(((f32[128,1,128]{2,1,0:T(1,128)}), f32[128,1,128]{2,1,0:T(1,128)S(1)}, u32[]{:S(2)}, u32[]{:S(2)}) %all-to-all-start.1) | async-done | bytes 65568 | tf_op jit(solution)/shard_map/all_to_all | solution.py:175
  63.1 5.8 %all-to-all-start = ((f32[256,1,512]{2,1,0:T(1,128)}), f32[256,1,512]{2,1,0:T(1,128)S(1)}, u32[]{:S(2)}, u32[]{:S(2)}) async-start(f32[256,1,512]{2,1,0:T(1,128)} %copy.89), calls=%async_computation | async-start | bytes 1048576 | tf_op jit(solution)/shard_map/all_to_all | solution.py:152
  70.9 19.4 %all-to-all-done = f32[256,1,512]{2,1,0:T(1,128)S(1)} async-done(((f32[256,1,512]{2,1,0:T(1,128)}), f32[256,1,512]{2,1,0:T(1,128)S(1)}, u32[]{:S(2)}, u32[]{:S(2)}) %all-to-all-start) | async-done | bytes 524320 | tf_op jit(solution)/shard_map/all_to_all | solution.py:152
  93.0 21.1 %all_to_all.48 = f32[128,1,640]{2,1,0:T(1,128)S(1)} all-to-all(f32[128,1,640]{2,1,0:T(1,128)S(1)} %all_to_all.38), channel_id=1, replica_groups=mesh['g'=2,'yl'=2,'x'=4,'z'=8,'c'=2] {'g','yl','x','z'}, dimensions={0} | all-to-all | bytes 655360 | tf_op jit(solution)/shard_map/all_to_all | solution.py:225
  115.5 1.9 %collective-permute-start.2 = (f32[128,640]{1,0:T(8,128)}, f32[128,640]{1,0:T(8,128)}, u32[]{:S(2)}, u32[]{:S(2)}) collective-permute-start(f32[128,640]{1,0:T(8,128)} %bitcast.143), channel_id=1, source_target_pairs={{0,1},{1,0},{2,3},{3,2},{4,5},{5,4},{6,7},{7,6},{8,9},{9,8},{10,11... | collective-permute-start | bytes 983048 | tf_op jit(solution)/shard_map/ppermute | solution.py:226
  126.3 1.7 %copy.97 = f32[256,1,768]{2,1,0:T(1,128)} copy(f32[256,1,768]{2,0,1:T(8,128)S(1)} %maximum_bitcast_fusion) | data formatting | bytes 1572864 | tf_op jit(solution)/shard_map/all_to_all | solution.py:277
  128.0 7.0 %all-to-all-start.3 = ((f32[256,1,768]{2,1,0:T(1,128)}), f32[256,1,768]{2,1,0:T(1,128)}, u32[]{:S(2)}, u32[]{:S(2)}) async-start(f32[256,1,768]{2,1,0:T(1,128)} %copy.97), calls=%async_computation.3 | async-start | bytes 1572864 | tf_op jit(solution)/shard_map/all_to_all | solution.py:277
  135.0 1.1 convolution_select_fusion.1
  136.7 4.5 %collective-permute-start.3 = (f32[320,1]{1,0:T(8,128)S(1)}, f32[320,1]{1,0:T(8,128)S(1)}, u32[]{:S(2)}, u32[]{:S(2)}) collective-permute-start(f32[320,1]{1,0:T(8,128)S(1)} %get-tuple-element.39), channel_id=1, source_target_pairs={{1,0},{2,1},{3,2},{4,3},{5,4},{6,5},{7,6},{8,7},{9,8},{10,9},{11,1... | collective-permute-start | bytes 3848 | tf_op jit(solution)/shard_map/ppermute | solution.py:125
  141.8 1.2 fusion.151
  143.1 1.9 %collective-permute-start.4 = (f32[320,1]{1,0:T(8,128)S(1)}, f32[320,1]{1,0:T(8,128)S(1)}, u32[]{:S(2)}, u32[]{:S(2)}) collective-permute-start(f32[320,1]{1,0:T(8,128)S(1)} %get-tuple-element.38), channel_id=1, source_target_pairs={{0,1},{1,2},{2,3},{3,4},{4,5},{5,6},{6,7},{7,8},{8,9},{9,10},{10,1... | collective-permute-start | bytes 3848 | tf_op jit(solution)/shard_map/ppermute | solution.py:124
  145.0 9.1 %collective-permute-done.3 = f32[320,1]{1,0:T(8,128)S(1)} collective-permute-done((f32[320,1]{1,0:T(8,128)S(1)}, f32[320,1]{1,0:T(8,128)S(1)}, u32[]{:S(2)}, u32[]{:S(2)}) %collective-permute-start.3) | collective-permute-done | bytes 1312 | tf_op jit(solution)/shard_map/ppermute | solution.py:125
  154.1 1.3 convolution_add_fusion.1
  155.4 1.4 convolution_add_fusion
  156.8 1.0 slice.252
  157.9 3.7 %all-to-all-done.3 = f32[256,1,768]{2,1,0:T(1,128)} async-done(((f32[256,1,768]{2,1,0:T(1,128)}), f32[256,1,768]{2,1,0:T(1,128)}, u32[]{:S(2)}, u32[]{:S(2)}) %all-to-all-start.3) | async-done | bytes 786464 | tf_op jit(solution)/shard_map/all_to_all | solution.py:277
  161.5 1.2 copy.119
  166.0 1.1 pad_maximum_fusion.1
  (198 shorter events, 24.4 us)
Async XLA Ops:
  2.4 27.5 %collective-permute-start = (f32[320,1]{1,0:T(8,128)}, f32[320,1]{1,0:T(8,128)}, u32[]{:S(2)}, u32[]{:S(2)}) collective-permute-start(f32[320,1]{1,0:T(8,128)} %get-tuple-element.43), channel_id=1, source_target_pairs={{1,0},{2,1},{3,2},{4,3},{5,4},{6,5},{7,6},{8,7},{9,8},{10,9},{11,1... | collective-permute-start | bytes 3848 | tf_op jit(solution)/shard_map/ppermute | solution.py:125
  7.6 6.0 %copy-start.40 = (f32[3,5,5]{2,0,1:T(4,128)S(1)}, f32[3,5,5]{2,0,1:T(4,128)}, u32[]{:S(2)}) copy-start(f32[3,5,5]{2,0,1:T(4,128)} %param.47) | copy-start | bytes 904
  7.6 6.0 %copy-start.11 = (f32[5,64,5,64]{3,2,1,0:T(8,128)S(1)}, f32[5,64,5,64]{3,2,1,0:T(8,128)}, u32[]{:S(2)}) copy-start(f32[5,64,5,64]{3,2,1,0:T(8,128)} %constant.240) | copy-start | bytes 1228804
  7.6 6.0 %copy-start.34 = (f32[64,64]{1,0:T(8,128)S(1)}, f32[64,64]{1,0:T(8,128)}, u32[]{:S(2)}) copy-start(f32[64,64]{1,0:T(8,128)} %constant.197.clone) | copy-start | bytes 49156
  7.6 6.0 %copy-start.35 = (f32[64,64]{1,0:T(8,128)S(1)}, f32[64,64]{1,0:T(8,128)}, u32[]{:S(2)}) copy-start(f32[64,64]{1,0:T(8,128)} %constant.199.clone) | copy-start | bytes 49156
  7.6 6.0 %copy-start.36 = (f32[64,64]{1,0:T(8,128)S(1)}, f32[64,64]{1,0:T(8,128)}, u32[]{:S(2)}) copy-start(f32[64,64]{1,0:T(8,128)} %constant.200.clone) | copy-start | bytes 49156
  7.6 6.0 %copy-start.37 = (f32[64,64]{1,0:T(8,128)S(1)}, f32[64,64]{1,0:T(8,128)}, u32[]{:S(2)}) copy-start(f32[64,64]{1,0:T(8,128)} %constant.201.clone) | copy-start | bytes 49156
  7.6 6.0 %copy-start.38 = (f32[64,64]{1,0:T(8,128)S(1)}, f32[64,64]{1,0:T(8,128)}, u32[]{:S(2)}) copy-start(f32[64,64]{1,0:T(8,128)} %constant.203.clone) | copy-start | bytes 49156
  7.7 25.6 %collective-permute-start.1 = (f32[320,1]{1,0:T(8,128)}, f32[320,1]{1,0:T(8,128)}, u32[]{:S(2)}, u32[]{:S(2)}) collective-permute-start(f32[320,1]{1,0:T(8,128)} %get-tuple-element.42), channel_id=1, source_target_pairs={{0,1},{1,2},{2,3},{3,4},{4,5},{5,6},{6,7},{7,8},{8,9},{9,10},{10,1... | collective-permute-start | bytes 3848 | tf_op jit(solution)/shard_map/ppermute | solution.py:124
  19.2 4.3 %copy-start.1 = (f32[256,256]{1,0:T(8,128)S(1)}, f32[256,256]{1,0:T(8,128)}, u32[]{:S(2)}) copy-start(f32[256,256]{1,0:T(8,128)} %constant.196.clone) | copy-start | bytes 786436
  29.9 3.4 %copy-start.2 = (f32[320,1023]{1,0:T(8,128)S(1)}, f32[320,1023]{1,0:T(8,128)}, u32[]{:S(2)}) copy-start(f32[320,1023]{1,0:T(8,128)} %get-tuple-element.44) | copy-start | bytes 3928324
  29.9 3.4 %copy-start.3 = (f32[320,320]{1,0:T(8,128)S(1)}, f32[320,320]{1,0:T(8,128)}, u32[]{:S(2)}) copy-start(f32[320,320]{1,0:T(8,128)} %reshape.230) | copy-start | bytes 1228804
  36.0 18.7 %copy-start.50 = (f32[256]{0:T(256)S(1)}, f32[256]{0:T(256)}, u32[]{:S(2)}) copy-start(f32[256]{0:T(256)} %constant.211.clone) | copy-start | bytes 3076
  37.1 26.0 %all-to-all-start.1 = ((f32[128,1,128]{2,1,0:T(1,128)}), f32[128,1,128]{2,1,0:T(1,128)S(1)}, u32[]{:S(2)}, u32[]{:S(2)}) async-start(f32[128,1,128]{2,1,0:T(1,128)} %copy.90), calls=%async_computation.1 | async-start | bytes 131072 | tf_op jit(solution)/shard_map/all_to_all | solution.py:175
  53.5 15.5 %copy-start.28 = (f32[128,256]{1,0:T(8,128)S(1)}, f32[128,256]{1,0:T(8,128)}, u32[]{:S(2)}) copy-start(f32[128,256]{1,0:T(8,128)} %constant.205.clone) | copy-start | bytes 393220
  53.6 15.7 %copy-start.27 = (f32[128,256]{1,0:T(8,128)S(1)}, f32[128,256]{1,0:T(8,128)}, u32[]{:S(2)}) copy-start(f32[128,256]{1,0:T(8,128)} %constant.208.clone) | copy-start | bytes 393220
  53.6 15.9 %copy-start.45 = (f32[128]{0:T(128)S(1)}, f32[128]{0:T(128)}, u32[]{:S(2)}) copy-start(f32[128]{0:T(128)} %constant.237) | copy-start | bytes 1540
  53.6 15.9 %copy-start.46 = (f32[128]{0:T(128)S(1)}, f32[128]{0:T(128)}, u32[]{:S(2)}) copy-start(f32[128]{0:T(128)} %constant.238) | copy-start | bytes 1540
  54.6 15.1 %copy-start.33 = (f32[256,256]{1,0:T(8,128)S(1)}, f32[256,256]{1,0:T(8,128)}, u32[]{:S(2)}) copy-start(f32[256,256]{1,0:T(8,128)} %constant.213.clone) | copy-start | bytes 786436
  63.1 27.2 %all-to-all-start = ((f32[256,1,512]{2,1,0:T(1,128)}), f32[256,1,512]{2,1,0:T(1,128)S(1)}, u32[]{:S(2)}, u32[]{:S(2)}) async-start(f32[256,1,512]{2,1,0:T(1,128)} %copy.89), calls=%async_computation | async-start | bytes 1048576 | tf_op jit(solution)/shard_map/all_to_all | solution.py:152
  70.9 20.2 %copy-start.18 = (f32[256,256]{1,0:T(8,128)S(1)}, f32[256,256]{1,0:T(8,128)}, u32[]{:S(2)}) copy-start(f32[256,256]{1,0:T(8,128)} %constant.209.clone) | copy-start | bytes 786436
  115.5 3.5 %collective-permute-start.2 = (f32[128,640]{1,0:T(8,128)}, f32[128,640]{1,0:T(8,128)}, u32[]{:S(2)}, u32[]{:S(2)}) collective-permute-start(f32[128,640]{1,0:T(8,128)} %bitcast.143), channel_id=1, source_target_pairs={{0,1},{1,0},{2,3},{3,2},{4,5},{5,4},{6,7},{7,6},{8,9},{9,8},{10,11... | collective-permute-start | bytes 983048 | tf_op jit(solution)/shard_map/ppermute | solution.py:226
  117.5 2.8 %copy-start.19 = (f32[128,128]{1,0:T(8,128)S(1)}, f32[128,128]{1,0:T(8,128)}, u32[]{:S(2)}) copy-start(f32[128,128]{1,0:T(8,128)} %constant.222.clone) | copy-start | bytes 196612
  118.2 2.8 %copy-start.42 = (s32[1,128]{1,0:T(1,128)S(1)}, s32[1,128]{1,0:T(1,128)}, u32[]{:S(2)}) copy-start(s32[1,128]{1,0:T(1,128)} %constant.223.clone) | copy-start | bytes 1540
  118.2 3.1 %copy-start.17 = (f32[256,128]{1,0:T(8,128)S(1)}, f32[256,128]{1,0:T(8,128)}, u32[]{:S(2)}) copy-start(f32[256,128]{1,0:T(8,128)} %constant.215.clone) | copy-start | bytes 393220
  126.3 8.8 %copy-start.41 = (s32[128]{0:T(128)S(1)}, s32[128]{0:T(128)}, u32[]{:S(2)}) copy-start(s32[128]{0:T(128)} %constant.234) | copy-start | bytes 1540
  126.3 9.9 %copy-start.39 = (f32[16,128]{1,0:T(8,128)S(1)}, f32[16,128]{1,0:T(8,128)}, u32[]{:S(2)}) copy-start(f32[16,128]{1,0:T(8,128)} %constant.229.clone) | copy-start | bytes 24580
  128.0 8.6 %copy-start.7 = (f32[48,1024]{1,0:T(8,128)S(1)}, f32[48,1024]{1,0:T(8,128)}, u32[]{:S(2)}) copy-start(f32[48,1024]{1,0:T(8,128)} %slice.249) | copy-start | bytes 589828
  128.0 33.5 %all-to-all-start.3 = ((f32[256,1,768]{2,1,0:T(1,128)}), f32[256,1,768]{2,1,0:T(1,128)}, u32[]{:S(2)}, u32[]{:S(2)}) async-start(f32[256,1,768]{2,1,0:T(1,128)} %copy.97), calls=%async_computation.3 | async-start | bytes 1572864 | tf_op jit(solution)/shard_map/all_to_all | solution.py:277
  136.7 17.4 %collective-permute-start.3 = (f32[320,1]{1,0:T(8,128)S(1)}, f32[320,1]{1,0:T(8,128)S(1)}, u32[]{:S(2)}, u32[]{:S(2)}) collective-permute-start(f32[320,1]{1,0:T(8,128)S(1)} %get-tuple-element.39), channel_id=1, source_target_pairs={{1,0},{2,1},{3,2},{4,3},{5,4},{6,5},{7,6},{8,7},{9,8},{10,9},{11,1... | collective-permute-start | bytes 3848 | tf_op jit(solution)/shard_map/ppermute | solution.py:125
  141.8 12.3 %copy-start.5 = (f32[320,320]{1,0:T(8,128)S(1)}, f32[320,320]{1,0:T(8,128)}, u32[]{:S(2)}) copy-start(f32[320,320]{1,0:T(8,128)} %reshape.228) | copy-start | bytes 1228804
  143.1 12.3 %collective-permute-start.4 = (f32[320,1]{1,0:T(8,128)S(1)}, f32[320,1]{1,0:T(8,128)S(1)}, u32[]{:S(2)}, u32[]{:S(2)}) collective-permute-start(f32[320,1]{1,0:T(8,128)S(1)} %get-tuple-element.38), channel_id=1, source_target_pairs={{0,1},{1,2},{2,3},{3,4},{4,5},{5,6},{6,7},{7,8},{8,9},{9,10},{10,1... | collective-permute-start | bytes 3848 | tf_op jit(solution)/shard_map/ppermute | solution.py:124
  (27 other events, 43.1 us)
where the time goes:
time: 168 us; the launch traced here: 167 us
  starting transfers between devices  43.6 us (26%)
  waiting for transfers between devices  40.1 us (24%)
  matrix products  26.6 us (16%)
  local copies, waits for them, and re-layouts  24.6 us (15%)
  blocking collectives  21.1 us (13%)
  other arithmetic  8.77 us (5%)
  between operations  2.46 us (1%)
    all_to_all x1, blocking collectives, on_device(): lax.all_to_all(pay2, SAME_CORE, split_axis=0, concat_axis=0, tiled=True)  21.1 us
    all_to_all x1, waiting for transfers between devices, on_device(): got1 = lax.all_to_all(pay1, ALL, split_axis=0, concat_axis=0, tiled=True)  19.4 us
    dot_general x28, matrix products, mm(): return lax.dot_general(a, b, (((1,), (0,)), ((), ())), precision=HIGH)  18.4 us
    all_to_all x1, starting transfers between devices, on_device(): lax.all_to_all(jnp.concatenate(lanes, axis=1), SUB, split_axis=0, concat_...  15.3 us
    ppermute x2, starting transfers between devices, chain_halo(): after = lax.ppermute(first, ALL, [(i + 1, i) for i in range(255)])  9.62 us
    ppermute x2, waiting for transfers between devices, chain_halo(): after = lax.ppermute(first, ALL, [(i + 1, i) for i in range(255)])  9.09 us
    dot_general x21, matrix products, mm_nt(): return lax.dot_general(a, b, (((1,), (1,)), ((), ())), precision=HIGH)  7.41 us
    all_to_all x1, waiting for transfers between devices, on_device(): lax.all_to_all(jnp.concatenate(lanes, axis=1), SUB, split_axis=0, concat_...  7.19 us
  transfers between devices with their start and end apart: 8, of which 5 were waited for; matrix products, arithmetic and copies ran while one was open for 21% of the time, Pallas kernels for 0%

commit v1 on v0

v1 whole, which is shorter than its diff:
```python
import jax
import jax.numpy as jnp
import ml_dtypes
import numpy as np
from jax import lax
from jax.experimental import pallas as pl
from jax.experimental.pallas import tpu as pltpu
from jax.sharding import Mesh, PartitionSpec as P

ALL = ("g", "yl", "x", "z", "c")
SUB = ("yl", "x", "z", "c")
SAME_CORE = ("g", "yl", "x", "z")
N = 256
HALF = 128
DT = 0.05
VISC = 0.05
GAIN = 0.3
F32 = jnp.float32
BF16 = jnp.bfloat16
NN = ((1,), (0,))
NT = ((1,), (1,))
TN = ((0,), (0,))


def sine_table(length):
    numbers = np.arange(length) + 1
    phases = numbers[:, None] * numbers[None, :] % (2 * (length + 1))
    return np.sqrt(2.0 / (length + 1)) * np.sin(np.pi * phases / (length + 1))


def rates(length):
    return 2.0 - 2.0 * np.cos(np.pi * (np.arange(length) + 1) / (length + 1))


SINE = sine_table(N)
RATES = rates(N)
MODE_ORDER = np.array([2 * q + k for k in range(2) for q in range(HALF)])
X_ORDER = np.array([4 * j + 2 * k + i for i in range(2) for k in range(2) for j in range(64)])


def surface_response():
    total = np.zeros((N, N))
    for c in range(N):
        total += SINE[0, c] ** 2 / (1.0 + 64.0 * (RATES[c] + RATES[:, None] + RATES[None, :]))
    return total


Q = SINE.astype(np.float32)
RESPONSE = surface_response()[MODE_ORDER].astype(np.float32)
Q_MODES = Q[MODE_ORDER]
Q_X = Q[:, X_ORDER]


def lobatto_derivative():
    points = np.array([-1.0, -1.0 / np.sqrt(5.0), 1.0 / np.sqrt(5.0), 1.0])
    weights = np.array(
        [1.0 / np.prod([points[j] - points[k] for k in range(4) if k != j]) for j in range(4)]
    )
    deriv = np.zeros((4, 4))
    for i in range(4):
        for j in range(4):
            if i != j:
                deriv[i, j] = weights[j] / weights[i] / (points[i] - points[j])
        deriv[i, i] = -np.sum(deriv[i])
    return deriv


def operator_parts():
    deriv, eye = lobatto_derivative(), np.eye(4)
    along = [
        np.kron(eye, np.kron(eye, deriv)),
        np.kron(eye, np.kron(deriv, eye)),
        np.kron(deriv, np.kron(eye, eye)),
    ]
    second = sum(d @ d for d in along)
    pick = np.zeros((4, 4, 4, 4))
    for i in range(4):
        for j in range(4):
            pick[i, j, i, j] = 1.0
    eye16 = np.eye(16)
    right, left = np.kron(eye16, pick[3, 3]), np.kron(eye16, pick[0, 0])
    right_from, left_from = np.kron(eye16, pick[3, 0]), np.kron(eye16, pick[0, 3])
    fixed = np.kron(np.eye(5), np.eye(64) - 0.15 * right - 0.15 * left)
    fixed = fixed + DT * VISC * np.kron(np.diag([0.0, 1.0, 1.0, 1.0, 1.0]), second)
    by_x = -DT * along[0] + 0.15 * right - 0.15 * left
    return [
        np.asarray(a, np.float32)
        for a in (
            fixed,
            by_x,
            -DT * along[1],
            -DT * along[2],
            np.kron(np.eye(5), 0.15 * right_from),
            -0.15 * right_from,
            np.kron(np.eye(5), 0.15 * left_from),
            0.15 * left_from,
        )
    ]


FIXED, BY_X, BY_Y, BY_Z, NEXT_FIXED, NEXT_X, PREV_FIXED, PREV_X = operator_parts()


def pair(table):
    high = np.asarray(table, np.float32).astype(ml_dtypes.bfloat16)
    low = (np.asarray(table, np.float32) - high.astype(np.float32)).astype(ml_dtypes.bfloat16)
    return np.stack([high, low])


SINE_PAIR = pair(Q)
SINE_BLOCKS = np.ascontiguousarray(
    pair(Q).reshape(2, 2, HALF, 2, HALF).transpose(0, 1, 3, 2, 4)
)
X_SPLIT = np.stack([pair(Q[i::2]) for i in range(2)])
MODES_PAIR = pair(Q_MODES)
MODES_PAIR_T = pair(Q_MODES.T)
X_PAIR = pair(Q_X)
X_PAIR_T = pair(Q_X.T)
Y_HALVES = np.stack([pair(Q[:, :HALF]), pair(Q[:, HALF:])])
Y_HALVES_T = np.stack([pair(Q[:HALF]), pair(Q[HALF:])])
MODES_HALVES = np.stack([pair(Q_MODES[:, :HALF]), pair(Q_MODES[:, HALF:])])
RATE_TABLE = (1.0 + 64.0 * (RATES[:, None] + RATES[None, :])).astype(np.float32)
SURFACE_ROW = np.broadcast_to(Q[:1], (8, N)).copy()
SURFACE_COLUMN = Q[:, :1].copy()
FIELD_ROWS = np.kron(np.eye(5), np.ones((64, 1))).astype(np.float32)
FIELD_HOT = np.pad(FIELD_ROWS, ((0, 0), (0, 123))).astype(ml_dtypes.bfloat16)
BY_TILES = np.stack([np.tile(t, (5, 5)) for t in (BY_X, BY_Y, BY_Z)])
NEXT_TILE, PREV_TILE = np.tile(NEXT_X, (5, 5)), np.tile(PREV_X, (5, 5))


def split(value):
    high = value.astype(BF16)
    return high, (value - high.astype(F32)).astype(BF16)


def dot(a, b, dims=NN):
    return lax.dot_general(a, b, (dims, ((), ())), preferred_element_type=F32)


def dot3(a, b, dims=NN):
    a = split(a) if not isinstance(a, tuple) else a
    b = split(b) if not isinstance(b, tuple) else b
    return dot(a[0], b[0], dims) + (dot(a[0], b[1], dims) + dot(a[1], b[0], dims))


def hot_dot(hot, b, dims=NN):
    high, low = split(b)
    return dot(hot, high, dims) + dot(hot, low, dims)


def dot_hot(a, hot, dims=NN):
    high, low = split(a)
    return dot(high, hot, dims) + dot(low, hot, dims)


def hot_of(condition):
    return jnp.where(condition, 1.0, 0.0).astype(BF16)


def iota(shape, dim):
    return lax.broadcasted_iota(jnp.int32, shape, dim)


def both(ref):
    return ref[0], ref[1]


def rows(ref, first, count, stride):
    return ref[pl.ds(first, count, stride), :]


def edges_kernel(left_ref, right_ref, first_ref, last_ref):
    first_ref[...] = left_ref[...].T[0:1]
    last_ref[...] = right_ref[...].T[HALF - 1 : HALF]


def matrices_kernel(
    fluid_ref, jac_ref, hot_ref, fixed_ref, tiles_ref, nf_ref, nt_ref, pf_ref, pt_ref, out_ref, wall_ref
):
    spread = []
    for d in range(3):
        by_row = hot_dot(hot_ref[...], jac_ref[d])
        spread.append(dot_hot(by_row, hot_ref[...], NT))
    own = fixed_ref[...]
    for d in range(3):
        own = own + spread[d] * tiles_ref[d]
    parts = [own, nf_ref[...] + spread[0] * nt_ref[...], pf_ref[...] + spread[0] * pt_ref[...]]
    for i, part in enumerate(parts):
        out_ref[pl.ds(320 * i, 320), :] = part
    moved = jnp.concatenate([part[256:272] - part[0:16] for part in parts], axis=0)
    wall_ref[0:48] = dot3(moved, fluid_ref[...])
    wall_ref[48:64] = fluid_ref[256:272] - fluid_ref[0:16]


def with_halo(own, following, preceding, after, before):
    lane = iota(own.shape, 1)
    count = own.shape[1]
    following = jnp.where(lane == count - 1, after, pltpu.roll(following, count - 1, 1))
    preceding = jnp.where(lane == 0, before, pltpu.roll(preceding, 1, 1))
    return own + following + preceding


def first_kernel(
    where_ref, solid_ref, far_ref, wall_ref, matrix_ref, before_ref, after_ref, elem_ref,
    owner_col_ref, owner_ref, patch_ref, blocks_ref, out_ref, trace_ref
):
    group = where_ref[0]
    near, far = [
        (blocks_ref[0, group, h], blocks_ref[1, group, h]) for h in (group, 1 - group)
    ]
    for i in range(2):
        modes = dot3(near, rows(solid_ref, i, N, 2), NT) + dot3(far, rows(far_ref, i, N, 2), NT)
        for h in range(2):
            out_ref[pl.ds(2 * i + h, HALF, 5), :] = modes[:, h * HALF : (h + 1) * HALF]

    def halo(part, row):
        start = 320 * part
        moved = matrix_ref[pl.ds(start + 256, 16), :] - matrix_ref[pl.ds(start, 16), :]
        return jnp.sum(moved * row, axis=1, keepdims=True)

    later = with_halo(
        wall_ref[0:16], wall_ref[16:32], wall_ref[32:48],
        halo(1, after_ref[...]), halo(2, before_ref[...]),
    )
    wall0 = wall_ref[48:64]
    elem_hot = hot_of(elem_ref[...] == iota((HALF, wall0.shape[1]), 1))
    values = dot_hot(jnp.concatenate([wall0, later - GAIN * wall0], axis=0), elem_hot, NT)
    trace_ref[...] = values[:16]
    owner = owner_ref[...]
    square = (HALF, HALF)
    same = (owner_col_ref[...] == owner) & (iota(square, 0) < iota(square, 1))
    place = jnp.sum(jnp.where(same, 1.0, 0.0), axis=0, keepdims=True)
    ids = jnp.broadcast_to((patch_ref[...] + 1).astype(F32), (8, HALF))
    filler = jnp.zeros((24, HALF), F32)
    sent = jnp.concatenate([values, ids, filler], axis=0)
    none = jnp.zeros((64, HALF), F32)
    arranged = 0.0
    for i in range(2):
        hot = hot_of((iota(square, 0) == owner) & (place == float(i)))
        padded = jnp.concatenate([sent, none] if i == 0 else [none, sent], axis=0)
        arranged = arranged + hot_dot(hot, padded, NT)
    out_ref[pl.ds(4, HALF, 5), :] = arranged


def modes_kernel(
    where_ref, rate_ref, got_ref, surface_ref, sine_ref, x_ref, table_ref, row_ref, halves_ref,
    modes_ref, out_ref
):
    group = where_ref[0]
    sine = both(sine_ref)
    modes = 0.0
    for i in range(2):
        part = jnp.concatenate([rows(got_ref, 2 * i + h, HALF, 5) for h in range(2)], axis=1)
        by_z = dot3(sine, part, NT)
        modes = modes + dot3(by_z, (x_ref[i, 0], x_ref[i, 1]))
    modes_ref[...] = modes
    once = modes / (table_ref[...] + 64.0 * rate_ref[0])
    surface_row = dot3(row_ref[...], once)[0:1]

    fluid = rows(got_ref, 4, HALF, 5)
    square = (HALF, HALF)
    lane = iota(square, 1)
    fluid_pair = split(fluid)
    sums = [[0.0, 0.0], [0.0, 0.0]]
    counts = [0.0, 0.0]
    count_lanes = 0.0
    for i in range(2):
        ids = fluid[:, i * 64 + 32 : i * 64 + 33].astype(jnp.int32) - 1
        count_lanes = count_lanes + jnp.sum(jnp.where(ids == lane, 1.0, 0.0), axis=0, keepdims=True)
        for f in range(2):
            pick = hot_of(iota(square, 0) == i * 64 + f * 16 + lane % 16)
            values = dot(fluid_pair[0], pick) + dot(fluid_pair[1], pick)
            for xl in range(2):
                mask = ids == xl * 8 + lane // 16
                sums[f][xl] = sums[f][xl] + jnp.sum(
                    jnp.where(mask, values, 0.0), axis=0, keepdims=True
                )
                if f == 0:
                    counts[xl] = counts[xl] + jnp.sum(
                        jnp.where(mask, 1.0, 0.0), axis=0, keepdims=True
                    )
    heat = [sums[0][xl] - counts[xl] * surface_ref[xl : xl + 1, :] for xl in range(2)]
    by_modes = (halves_ref[group, 0], halves_ref[group, 1])
    tail = jnp.where(lane < 16, count_lanes, 0.0)
    for xl in range(2):
        column = dot3(by_modes, jnp.broadcast_to(sums[1][xl], (8, HALF)), NT)[:, 0:1]
        for k in range(2):
            tail = jnp.where(lane == 16 + 2 * k + xl, column[k * HALF : (k + 1) * HALF], tail)
    shared = [surface_row[:, :HALF], surface_row[:, HALF:], heat[0], heat[1]]
    for r in range(4):
        out_ref[pl.ds(r, HALF, 5), :] = jnp.broadcast_to(shared[r], square)
    out_ref[pl.ds(4, HALF, 5), :] = tail


def solve_kernel(
    where_ref, rate_ref, got_ref, other_ref, modes_ref, response_ref, by_modes_ref, from_modes_ref,
    x_ref, xt_ref, sine_ref, full_ref, x_split_ref, table_ref, row_ref, column_ref,
    surface_ref, out_ref, heat_ref
):
    group, core, me = where_ref[0], where_ref[1], where_ref[2]
    first = jnp.full((HALF, HALF), core, jnp.int32) == 0
    ordered = []
    for r in range(5):
        mine, theirs = rows(got_ref, r, HALF, 5), rows(other_ref, r, HALF, 5)
        ordered.append((jnp.where(first, mine, theirs), jnp.where(first, theirs, mine)))

    def block(g, r):
        return jnp.concatenate([ordered[r][k][g * 64 : (g + 1) * 64] for k in range(2)], axis=0)

    heat_modes = 0.0
    for xl in range(2):
        by_y = 0.0
        for g in range(2):
            halves = (by_modes_ref[g, 0], by_modes_ref[g, 1])
            by_y = by_y + dot3(halves, block(g, 2 + xl), NT)
        at = pl.ds(xl * HALF, HALF)
        heat_modes = heat_modes + dot3(by_y, (xt_ref[0, at, :], xt_ref[1, at, :]))
    heat_ref[...] = heat_modes
    given = jnp.concatenate(
        [jnp.concatenate([ordered[h][k] for h in range(2)], axis=1) for k in range(2)], axis=0
    )
    x_pair = both(x_ref)
    surface = dot3(both(from_modes_ref), given + response_ref[...] * heat_modes)
    surface = dot3(surface, x_pair)
    heat_ref[...] = surface
    surface_ref[...] = heat_ref[pl.ds(pl.multiple_of(group * HALF, HALF), HALF), :]
    heat_ref[...] = heat_modes
    square = (HALF, HALF)
    tails = [block(g, 4) for g in range(2)]
    tail_pairs = [tail.astype(BF16) for tail in tails]
    expand = [hot_of(iota(square, 1) == xl * 8 + iota(square, 0) // 16) for xl in range(2)]
    count = jnp.concatenate(
        [
            jnp.concatenate([dot(expand[xl], tail_pairs[g], NT) for xl in range(2)], axis=1)
            for g in range(2)
        ],
        axis=0,
    )
    own_sine = jnp.broadcast_to(full_ref[pl.ds(me, 1), :], (8, N))
    reduced = dot3(own_sine, count * surface)
    tail_sum = tails[0] + tails[1]
    lane8 = iota((8, HALF), 1)
    later = jnp.concatenate(
        [hot_dot(hot_of(lane8 == 16 + 2 * core + xl), tail_sum, NT) for xl in range(2)], axis=1
    )
    heat1 = dot3(later - 0.7 * reduced, both(xt_ref))[0:1]
    heat0 = heat_ref[pl.ds(core * HALF + me // 2, 1), :]
    decay = 1.0 / (table_ref[...] + 64.0 * rate_ref[0])
    column = column_ref[...]
    final = decay * (decay * (modes_ref[...] + column * heat0) + column * heat1)
    final_row = dot3(row_ref[...], final)[0:1]
    final = split(final)
    sine = both(sine_ref)
    for xl in range(2):
        by_x = dot3((x_split_ref[xl, 0], x_split_ref[xl, 1]), final, NT)
        back = dot3(by_x, sine)
        for g in range(2):
            for h in range(2):
                out_ref[pl.ds(g * 768 + 2 * xl + h, HALF, 6), :] = back[:, h * HALF : (h + 1) * HALF]
    for h in range(2):
        out_ref[pl.ds(4 + h, N, 6), :] = jnp.broadcast_to(
            final_row[:, h * HALF : (h + 1) * HALF], (N, HALF)
        )


def patch_values(surface, owner, patch):
    x_of_slot = patch // 8 * HALF + owner % 2 * 64 + owner // 2
    square = (HALF, HALF)
    x_hot = hot_of(iota((N, HALF), 0) == x_of_slot)
    met = dot_hot(surface, x_hot)
    met = jnp.where(iota(square, 0) // 16 == patch % 8, met, 0.0)
    fold = hot_of(iota((16, HALF), 0) == iota((16, HALF), 1) % 16)
    return hot_dot(fold, met)


def source_kernel(
    fluid_ref, surface_ref, trace_ref, elem_ref, owner_ref, patch_ref,
    out_ref, later_ref, first_ref, last_ref
):
    count = fluid_ref.shape[1]
    elem_hot = hot_of(elem_ref[...] == iota((HALF, count), 1))
    met = patch_values(surface_ref[...], owner_ref[...], patch_ref[...])
    source = GAIN * dot_hot(met - trace_ref[...], elem_hot)
    out_ref[...] = fluid_ref[...]
    walls = fluid_ref[256:272] + source
    out_ref[256:272] = walls
    later_ref[...] = dot_hot(walls - fluid_ref[0:16], elem_hot, NT)
    first_ref[...] = out_ref[:, 0:HALF].T[0:1]
    last_ref[...] = out_ref[:, count - HALF : count].T[HALF - 1 : HALF]


def step_kernel(fluid_ref, matrix_ref, before_ref, after_ref, out_ref):
    fluid = split(fluid_ref[...])
    after, before = [
        jnp.sum(matrix_ref[pl.ds(320 * part, 320), :] * row, axis=1, keepdims=True)
        for part, row in ((1, after_ref[...]), (2, before_ref[...]))
    ]
    parts = [dot3(matrix_ref[pl.ds(320 * i, 320), :], fluid) for i in range(3)]
    out_ref[...] = with_halo(*parts, after, before)


def last_kernel(
    where_ref, got_ref, y_ref, yt_ref, x_ref, later_ref, elem_ref, owner_ref, patch_ref, fluid_ref,
    solid_ref, out_ref
):
    group = where_ref[0]
    by_y = (y_ref[group, 0], y_ref[group, 1])
    for xl in range(2):
        for h in range(2):
            part = rows(got_ref, 2 * xl + h, N, 6)
            solid_ref[pl.ds(h * N + xl, HALF, 2), :] = dot3(part, by_y, TN)
    given = jnp.concatenate([rows(got_ref, 4 + h, N, 6) for h in range(2)], axis=1)
    surface = dot3(dot3((yt_ref[group, 0], yt_ref[group, 1]), given), both(x_ref))
    met = patch_values(surface, owner_ref[...], patch_ref[...])
    elem_hot = hot_of(elem_ref[...] == iota((HALF, fluid_ref.shape[1]), 1))
    out_ref[...] = fluid_ref[...] + GAIN * dot_hot(met - later_ref[...], elem_hot)


def call(kernel, outs, args, scalars=0, scratch=(), aliases=None, specs=None, out_specs=None, cost=None):
    whole = pl.BlockSpec(memory_space=pltpu.VMEM)
    given = [pl.BlockSpec(memory_space=pltpu.SMEM)] * scalars + [whole] * (len(args) - scalars)
    return pl.pallas_call(
        kernel,
        out_shape=[jax.ShapeDtypeStruct(shape, F32) for shape in outs],
        in_specs=specs or given,
        out_specs=out_specs or [whole] * len(outs),
        scratch_shapes=list(scratch),
        input_output_aliases=aliases or {},
        cost_estimate=pl.CostEstimate(flops=int(cost or 1e8), bytes_accessed=1 << 20, transcendentals=0),
        compiler_params=pltpu.CompilerParams(vmem_limit_bytes=40 << 20),
    )(*args)


def chain_halo(first, last):
    before = lax.ppermute(last, ALL, [(i, i + 1) for i in range(255)])
    after = lax.ppermute(first, ALL, [(i + 1, i) for i in range(255)])
    return before, after


def on_device(fluid_state, flux_jacobian, solid_temp, iface_elem, iface_owner, iface_patch):
    me = lax.axis_index(ALL)
    where = jnp.stack([me // HALF, me % 2, me]).astype(jnp.int32)
    rate = lax.dynamic_slice(jnp.asarray(RATES, F32), (me,), (1,))
    fluid0 = fluid_state.reshape(320, -1)
    count = fluid0.shape[1]
    solid = solid_temp.reshape(2 * N, HALF)
    elem = iface_elem[:, None]
    owner, patch = iface_owner.reshape(1, HALF), iface_patch[None, :]

    far = lax.ppermute(solid, "g", [(0, 1), (1, 0)])
    first, last = pl.pallas_call(
        edges_kernel,
        grid=(1,),
        out_shape=[jax.ShapeDtypeStruct((1, 320), F32)] * 2,
        in_specs=[
            pl.BlockSpec((320, HALF), lambda i: (0, 0)),
            pl.BlockSpec((320, HALF), lambda i: (0, count // HALF - 1)),
        ],
        out_specs=[pl.BlockSpec((1, 320), lambda i: (0, 0))] * 2,
    )(fluid0, fluid0)
    before, after = chain_halo(first, last)
    jacobian = jnp.pad(flux_jacobian, ((0, 0), (0, 123), (0, 123)))
    matrix, walls = call(
        matrices_kernel,
        [(960, 320), (64, count)],
        [fluid0, jacobian, FIELD_HOT, FIXED, BY_TILES, NEXT_FIXED, NEXT_TILE, PREV_FIXED, PREV_TILE],
    )
    pay1, trace0 = call(
        first_kernel,
        [(5 * HALF, HALF), (16, HALF)],
        [where, solid, far, walls, matrix, before, after, elem, iface_owner, owner, patch, SINE_BLOCKS],
        scalars=1,
    )
    got1 = lax.all_to_all(pay1, SUB, split_axis=0, concat_axis=0, tiled=True)
    (fluid1,) = call(step_kernel, [(320, count)], [fluid0, matrix, before, after], cost=2e9)
    modes, pay2 = call(
        modes_kernel,
        [(N, N), (5 * HALF, HALF)],
        [where, rate, got1, solid[:2], SINE_PAIR, X_SPLIT, RATE_TABLE, SURFACE_ROW, MODES_HALVES],
        scalars=2,
    )
    got2 = lax.all_to_all(pay2, SAME_CORE, split_axis=0, concat_axis=0, tiled=True)
    other = lax.ppermute(got2, "c", [(0, 1), (1, 0)])
    surface1, pay3 = call(
        solve_kernel,
        [(HALF, N), (6 * N, HALF)],
        [where, rate, got2, other, modes, RESPONSE, MODES_HALVES, MODES_PAIR_T, X_PAIR, X_PAIR_T,
         SINE_PAIR, Q, X_SPLIT, RATE_TABLE, SURFACE_ROW, SURFACE_COLUMN],
        scalars=2,
        scratch=[pltpu.VMEM((N, N), F32)],
    )
    got3 = lax.all_to_all(pay3, ALL, split_axis=0, concat_axis=0, tiled=True)
    fluid1, trace1, first, last = call(
        source_kernel,
        [(320, count), (16, HALF), (1, 320), (1, 320)],
        [fluid1, surface1, trace0, elem, owner, patch],
    )
    before, after = chain_halo(first, last)
    (fluid2,) = call(step_kernel, [(320, count)], [fluid1, matrix, before, after], cost=2e9)
    solid_out, fluid2 = pl.pallas_call(
        last_kernel,
        grid=(1,),
        out_shape=[
            jax.ShapeDtypeStruct((2 * N, HALF), F32),
            jax.ShapeDtypeStruct((320, count), F32),
        ],
        in_specs=[pl.BlockSpec(memory_space=pltpu.SMEM)]
        + [pl.BlockSpec(memory_space=pltpu.VMEM)] * 8
        + [pl.BlockSpec((16, count), lambda i: (16, 0))],
        out_specs=[
            pl.BlockSpec((2 * N, HALF), lambda i: (0, 0)),
            pl.BlockSpec((16, count), lambda i: (16, 0)),
        ],
        input_output_aliases={9: 1},
        compiler_params=pltpu.CompilerParams(vmem_limit_bytes=40 << 20),
    )(where, got3, Y_HALVES, Y_HALVES_T, X_PAIR, trace1, elem, owner, patch, fluid2)
    return fluid2.reshape(fluid_state.shape), solid_out.reshape(solid_temp.shape)


def solution(mesh):
    fine = Mesh(mesh.devices.reshape(2, 2, 4, 8, 2), ALL)
    placed = (
        P(None, None, ALL),
        P(),
        P(None, SUB, "g"),
        P(ALL),
        P(ALL, None),
        P(ALL),
    )
    return jax.shard_map(
        on_device,
        mesh=fine,
        in_specs=placed,
        out_specs=(P(None, None, ALL), P(None, SUB, "g")),
        check_vma=False,
    )
```

time: 168 us -> 155 us (0.923)
  matrix products: 26.6 us -> 0 us
  Pallas kernels: 0 us -> 23.6 us
  other arithmetic: 8.77 us -> 0.08 us
  blocking collectives: 21.1 us -> 27.1 us
  waiting for transfers between devices: 40.1 us -> 36 us
  starting transfers between devices: 43.6 us -> 40 us
    dot_general x51 -> x0, matrix products: 26.6 us -> none  [the longest x28 18.4 us: mm(): return lax.dot_general(a, b, (((1,), (0,)), ((), ())), precision=HIGH)]
    pallas_call x0 -> x9, Pallas kernels: none -> 23.6 us  [the longest x7 19.1 us: call(): pl.pallas_call(kernel, out_shape=[jax.ShapeDtypeStruct(shape, F32) for sh...]
    unnamed x107 -> x92, local copies, waits for them, and re-layouts: 4.81 us -> 18 us
    slice x14 -> x1, local copies, waits for them, and re-layouts: 10.2 us -> 0.01 us  [on_device(): solid[:2]]
    all_to_all x3 -> x2, waiting for transfers between devices: 30.2 us -> 22 us  [the longest x1 17.5 us: on_device(): got1 = lax.all_to_all(pay1, SUB, split_axis=0, concat_axis=0, tiled=True)]
    all_to_all x3 -> x2, starting transfers between devices: 28.1 us -> 21.4 us  [the longest x1 14.3 us: on_device(): got1 = lax.all_to_all(pay1, SUB, split_axis=0, concat_axis=0, tiled=True)]
    all_to_all x1, blocking collectives: 21.1 us -> 27.1 us  [on_device(): lax.all_to_all(pay2, SAME_CORE, split_axis=0, concat_axis=0, tiled=True)]
    ppermute x2, starting transfers between devices: 9.62 us -> 3.85 us  [chain_halo(): after = lax.ppermute(first, ALL, [(i + 1, i) for i in range(255)])]
  transfers between devices with their start and end apart: 8 -> 8, of which waited for: 5 -> 5; matrix products, arithmetic and copies ran while one was open for 21% -> 1% of each run, Pallas kernels for 0% -> 8%
where the time goes in v1:
time: 155 us; the launch traced here: 154 us
  starting transfers between devices  40 us (26%)
  waiting for transfers between devices  36 us (23%)
  blocking collectives  27.1 us (17%)
  local copies, waits for them, and re-layouts  26.2 us (17%)
  Pallas kernels  23.6 us (15%)
    all_to_all x1, blocking collectives, on_device(): lax.all_to_all(pay2, SAME_CORE, split_axis=0, concat_axis=0, tiled=True)  27.1 us
    pallas_call x7, Pallas kernels, call(): pl.pallas_call(kernel, out_shape=[jax.ShapeDtypeStruct(shape, F32) for sh...  19.1 us
    unnamed x92, local copies, waits for them, and re-layouts  18 us
    all_to_all x1, waiting for transfers between devices, on_device(): got1 = lax.all_to_all(pay1, SUB, split_axis=0, concat_axis=0, tiled=True)  17.5 us
    all_to_all x1, starting transfers between devices, on_device(): got1 = lax.all_to_all(pay1, SUB, split_axis=0, concat_axis=0, tiled=True)  14.3 us
    ppermute x2, waiting for transfers between devices, chain_halo(): after = lax.ppermute(first, ALL, [(i + 1, i) for i in range(255)])  11.3 us
    ppermute x2, starting transfers between devices, chain_halo(): before = lax.ppermute(last, ALL, [(i, i + 1) for i in range(255)])  8.16 us
    all_to_all x1, starting transfers between devices, on_device(): got3 = lax.all_to_all(pay3, ALL, split_axis=0, concat_axis=0, tiled=True)  7.16 us
  transfers between devices with their start and end apart: 8, of which 5 were waited for; matrix products, arithmetic and copies ran while one was open for 1% of the time, Pallas kernels for 8%

profile of v1, /device:TPU:1, one launch (start us, length us, event | category | flops | bytes accessed | tf_op | source)
XLA Modules:
  0.0 154.0 jit_solution(14492343854602630950)
XLA Ops:
  0.6 3.8 %collective-permute-start = (f32[512,128]{1,0:T(8,128)}, f32[512,128]{1,0:T(8,128)}, u32[]{:S(2)}, u32[]{:S(2)}) collective-permute-start(f32[512,128]{1,0:T(8,128)} %bitcast.16), channel_id=1, source_target_pairs={{0,128},{128,0},{1,129},{129,1},{2,130},{130,2},{3,131},{131,3},{4... | collective-permute-start | bytes 786440 | tf_op jit(solution)/shard_map/ppermute | solution.py:450
  4.5 1.9 %shard_map.276 = (f32[1,320]{1,0:T(1,128)}, f32[1,320]{1,0:T(1,128)}) custom-call(f32[320,1024]{1,0:T(8,128)} %bitcast.12, f32[320,1024]{1,0:T(8,128)} %bitcast.13), custom_call_target="tpu_custom_call" | custom-call | tf_op jit(solution)/shard_map/pallas_call | solution.py:451
  6.4 4.4 %collective-permute-start.1 = (f32[1,320]{1,0:T(1,128)}, f32[1,320]{1,0:T(1,128)S(1)}, u32[]{:S(2)}, u32[]{:S(2)}) collective-permute-start(f32[1,320]{1,0:T(1,128)} %get-tuple-element.20), channel_id=1, source_target_pairs={{0,1},{1,2},{2,3},{3,4},{4,5},{5,6},{6,7},{7,8},{8,9},{9,10},{10,1... | collective-permute-start | bytes 3848 | tf_op jit(solution)/shard_map/ppermute | solution.py:435
  10.7 1.9 %collective-permute-start.2 = (f32[1,320]{1,0:T(1,128)}, f32[1,320]{1,0:T(1,128)S(1)}, u32[]{:S(2)}, u32[]{:S(2)}) collective-permute-start(f32[1,320]{1,0:T(1,128)} %get-tuple-element.21), channel_id=1, source_target_pairs={{1,0},{2,1},{3,2},{4,3},{5,4},{6,5},{7,6},{8,7},{9,8},{10,9},{11,1... | collective-permute-start | bytes 3848 | tf_op jit(solution)/shard_map/ppermute | solution.py:436
  14.5 1.0 copy-done.12
  15.6 1.0 copy-done.13
  16.6 1.0 copy-done.14
  17.6 1.0 copy-done.15
  18.7 1.5 shard_map.275
  20.2 1.1 copy-done.2
  22.9 1.4 copy-done.3
  25.9 1.8 %shard_map.277 = (f32[640,128]{1,0:T(8,128)S(1)}, f32[16,128]{1,0:T(8,128)S(1)}) custom-call(s32[3]{0:T(128)S(1)} %pad_add_fusion.where_ref, f32[512,128]{1,0:T(8,128)S(1)} %bitcast.17, f32[512,128]{1,0:T(8,128)} %collective-permute-done.far_ref, f32[64,1024]{1,0:T(8,128)S(1)} %copy-done.27, f32[960,320]{1,0:T(8,128)S(1)} %copy-done.3, ...), custom_call_target="tpu_custom_call" | custom-call | flops 100000000 | bytes 1048576 | tf_op jit(solution)/shard_map/pallas_call | solution.py:422
  29.2 14.3 %all-to-all-start = ((f32[128,5,128]{2,1,0:T(8,128)}), f32[128,5,128]{2,1,0:T(8,128)}, u32[]{:S(2)}, u32[]{:S(2)}) async-start(f32[128,5,128]{2,1,0:T(8,128)} %all_to_all.21), calls=%async_computation | async-start | bytes 1048576 | tf_op jit(solution)/shard_map/all_to_all | solution.py:474
  44.1 17.5 %all-to-all-done = f32[128,5,128]{2,1,0:T(8,128)} async-done(((f32[128,5,128]{2,1,0:T(8,128)}), f32[128,5,128]{2,1,0:T(8,128)}, u32[]{:S(2)}, u32[]{:S(2)}) %all-to-all-start) | async-done | bytes 327712 | tf_op jit(solution)/shard_map/all_to_all | solution.py:474
  61.5 1.1 all_to_all.23.got_ref
  62.7 2.9 %shard_map.278 = (f32[256,256]{1,0:T(8,128)S(1)}, f32[640,128]{1,0:T(8,128)S(1)}) custom-call(s32[3]{0:T(128)S(1)} %pad_add_fusion.where_ref, f32[1]{0:T(128)} %dynamic_slice.3.rate_ref, f32[640,128]{1,0:T(8,128)S(1)} %all_to_all.23.got_ref, f32[2,128]{1,0:T(2,128)S(1)} %slice_bitcast_fusion.surface_ref, bf16[2,256,256]{2,1,0:T(8,128)(2,1)S(1)} %copy-done.9, ...), custom_call_target="tpu_custom_call" | custom-call | flops 100000000 | bytes 1048576 | tf_op jit(solution)/shard_map/pallas_call | solution.py:422
  67.2 27.1 %all_to_all.33 = f32[128,5,128]{2,1,0:T(8,128)} all-to-all(f32[128,5,128]{2,1,0:T(8,128)} %all_to_all.24), channel_id=1, replica_groups=mesh['g'=2,'yl'=2,'x'=4,'z'=8,'c'=2] {'g','yl','x','z'}, dimensions={0} | all-to-all | bytes 655360 | tf_op jit(solution)/shard_map/all_to_all | solution.py:482
  94.2 1.1 all_to_all.26.got_ref
  95.3 2.7 %collective-permute-start.3 = (f32[640,128]{1,0:T(8,128)S(1)}, f32[640,128]{1,0:T(8,128)S(1)}, u32[]{:S(2)}, u32[]{:S(2)}) collective-permute-start(f32[640,128]{1,0:T(8,128)S(1)} %all_to_all.26.got_ref), channel_id=1, source_target_pairs={{0,1},{1,0},{2,3},{3,2},{4,5},{5,4},{6,7},{7,6},{8,9},{9,8},{10,11... | collective-permute-start | bytes 983048 | tf_op jit(solution)/shard_map/ppermute | solution.py:483
  98.1 1.3 collective-permute-done.3.other_ref
  103.1 4.3 %shard_map.279 = (f32[128,256]{1,0:T(8,128)S(1)}, f32[1536,128]{1,0:T(8,128)S(1)}) custom-call(s32[3]{0:T(128)S(1)} %pad_add_fusion.where_ref, f32[1]{0:T(128)} %dynamic_slice.3.rate_ref, f32[640,128]{1,0:T(8,128)S(1)} %all_to_all.26.got_ref, f32[640,128]{1,0:T(8,128)S(1)} %collective-permute-done.3.other_ref, f32[256,256]{1,0:T(8,128)S(1)} %copy-done.25, ...), custom_call_target="tpu_custom_call" | custom-call | flops 100000000 | bytes 1048576 | tf_op jit(solution)/shard_map/pallas_call | solution.py:422
  108.9 2.2 %all_to_all.27 = f32[256,6,128]{2,1,0:T(8,128)} reshape(f32[1536,128]{1,0:T(8,128)} %copy-done.10) | data formatting | bytes 1572864 | tf_op jit(solution)/shard_map/all_to_all | solution.py:492
  111.1 7.2 %all-to-all-start.2 = ((f32[256,6,128]{2,1,0:T(8,128)}), f32[256,6,128]{2,1,0:T(8,128)}, u32[]{:S(2)}, u32[]{:S(2)}) async-start(f32[256,6,128]{2,1,0:T(8,128)} %all_to_all.27), calls=%async_computation.2 | async-start | bytes 2097152 | tf_op jit(solution)/shard_map/all_to_all | solution.py:492
  118.4 3.4 %shard_map.280.fluid_ref = f32[320,1024]{1,0:T(8,128)S(1)} custom-call(f32[320,1024]{1,0:T(8,128)S(1)} %bitcast.15, f32[960,320]{1,0:T(8,128)S(1)} %copy-done.4, f32[1,320]{1,0:T(1,128)S(1)} %copy-done.39, f32[1,320]{1,0:T(1,128)S(1)} %copy-done.42), custom_call_target="tpu_custom_call" | custom-call | flops 2000000000 | bytes 1048576 | tf_op jit(solution)/shard_map/pallas_call | solution.py:422
  122.6 3.8 %collective-permute-start.4 = (f32[1,320]{1,0:T(1,128)S(1)}, f32[1,320]{1,0:T(1,128)S(1)}, u32[]{:S(2)}, u32[]{:S(2)}) collective-permute-start(f32[1,320]{1,0:T(1,128)S(1)} %get-tuple-element.30), channel_id=1, source_target_pairs={{0,1},{1,2},{2,3},{3,4},{4,5},{5,6},{6,7},{7,8},{8,9},{9,10},{10,1... | collective-permute-start | bytes 3848 | tf_op jit(solution)/shard_map/ppermute | solution.py:435
  126.4 1.9 %collective-permute-start.5 = (f32[1,320]{1,0:T(1,128)S(1)}, f32[1,320]{1,0:T(1,128)S(1)}, u32[]{:S(2)}, u32[]{:S(2)}) collective-permute-start(f32[1,320]{1,0:T(1,128)S(1)} %get-tuple-element.31), channel_id=1, source_target_pairs={{1,0},{2,1},{3,2},{4,3},{5,4},{6,5},{7,6},{8,7},{9,8},{10,9},{11,1... | collective-permute-start | bytes 3848 | tf_op jit(solution)/shard_map/ppermute | solution.py:436
  128.3 1.5 collective-permute-done.4.before_ref
  129.8 11.3 %collective-permute-done.5.after_ref = f32[1,320]{1,0:T(1,128)S(1)} collective-permute-done((f32[1,320]{1,0:T(1,128)S(1)}, f32[1,320]{1,0:T(1,128)S(1)}, u32[]{:S(2)}, u32[]{:S(2)}) %collective-permute-start.5) | collective-permute-done | bytes 1312 | tf_op jit(solution)/shard_map/ppermute | solution.py:436
  141.1 4.4 %shard_map.282.fluid_ref = f32[320,1024]{1,0:T(8,128)} custom-call(f32[320,1024]{1,0:T(8,128)S(1)} %get-tuple-element.29.fluid_ref, f32[960,320]{1,0:T(8,128)S(1)} %copy-done.4, f32[1,320]{1,0:T(1,128)S(1)} %collective-permute-done.4.before_ref, f32[1,320]{1,0:T(1,128)S(1)} %collective-permute-done.5.after_ref), custom_call_target="tpu_custom_call" | custom-call | flops 2000000000 | bytes 1048576 | tf_op jit(solution)/shard_map/pallas_call | solution.py:422
  145.5 4.5 %all-to-all-done.2 = f32[256,6,128]{2,1,0:T(8,128)} async-done(((f32[256,6,128]{2,1,0:T(8,128)}), f32[256,6,128]{2,1,0:T(8,128)}, u32[]{:S(2)}, u32[]{:S(2)}) %all-to-all-start.2) | async-done | bytes 786464 | tf_op jit(solution)/shard_map/all_to_all | solution.py:492
  150.0 1.3 all_to_all.29.got_ref
  151.3 2.7 %shard_map.283 = (f32[512,128]{1,0:T(8,128)}, f32[320,1024]{1,0:T(8,128)}) custom-call(s32[3]{0:T(128)S(1)} %pad_add_fusion.where_ref, f32[1536,128]{1,0:T(8,128)S(1)} %all_to_all.29.got_ref, bf16[2,2,256,128]{3,2,1,0:T(8,128)(2,1)S(1)} %copy-done.18, bf16[2,2,128,256]{3,2,1,0:T(8,128)(2,1)S(1)} %copy-done.17, ...), custom_call_target="tpu_custom_call", output_to_operand_aliasing={{1}: (9, {})} | custom-call | tf_op jit(solution)/shard_map/pallas_call | solution.py:500
  (97 shorter events, 14.7 us)
Async XLA Ops:
  0.6 21.7 %collective-permute-start = (f32[512,128]{1,0:T(8,128)}, f32[512,128]{1,0:T(8,128)}, u32[]{:S(2)}, u32[]{:S(2)}) collective-permute-start(f32[512,128]{1,0:T(8,128)} %bitcast.16), channel_id=1, source_target_pairs={{0,128},{128,0},{1,129},{129,1},{2,130},{130,2},{3,131},{131,3},{4... | collective-permute-start | bytes 786440 | tf_op jit(solution)/shard_map/ppermute | solution.py:450
  4.5 9.0 %copy-start = (f32[5,64,1024]{2,1,0:T(8,128)S(1)}, f32[5,64,1024]{2,1,0:T(8,128)}, u32[]{:S(2)}) copy-start(f32[5,64,1024]{2,1,0:T(8,128)} %param.28) | copy-start | bytes 3932164
  4.5 9.0 %copy-start.1 = (f32[3,320,320]{2,1,0:T(8,128)S(1)}, f32[3,320,320]{2,1,0:T(8,128)}, u32[]{:S(2)}) copy-start(f32[3,320,320]{2,1,0:T(8,128)} %constant.105.clone.tiles_ref) | copy-start | bytes 3686404
  4.5 9.0 %copy-start.31 = (bf16[320,128]{1,0:T(8,128)(2,1)S(1)}, bf16[320,128]{1,0:T(8,128)(2,1)}, u32[]{:S(2)}) copy-start(bf16[320,128]{1,0:T(8,128)(2,1)} %constant.103.clone.hot_ref) | copy-start | bytes 245764
  6.4 15.9 %collective-permute-start.1 = (f32[1,320]{1,0:T(1,128)}, f32[1,320]{1,0:T(1,128)S(1)}, u32[]{:S(2)}, u32[]{:S(2)}) collective-permute-start(f32[1,320]{1,0:T(1,128)} %get-tuple-element.20), channel_id=1, source_target_pairs={{0,1},{1,2},{2,3},{3,4},{4,5},{5,6},{6,7},{7,8},{8,9},{9,10},{10,1... | collective-permute-start | bytes 3848 | tf_op jit(solution)/shard_map/ppermute | solution.py:435
  10.7 11.5 %collective-permute-start.2 = (f32[1,320]{1,0:T(1,128)}, f32[1,320]{1,0:T(1,128)S(1)}, u32[]{:S(2)}, u32[]{:S(2)}) collective-permute-start(f32[1,320]{1,0:T(1,128)} %get-tuple-element.21), channel_id=1, source_target_pairs={{1,0},{2,1},{3,2},{4,3},{5,4},{6,5},{7,6},{8,7},{9,8},{10,9},{11,1... | collective-permute-start | bytes 3848 | tf_op jit(solution)/shard_map/ppermute | solution.py:436
  18.7 3.5 %copy-start.33 = (s32[128,1]{0,1:T(1,128)S(1)}, s32[128,1]{0,1:T(1,128)}, u32[]{:S(2)}) copy-start(s32[128,1]{0,1:T(1,128)} %param.32) | copy-start | bytes 1540
  18.7 4.2 %copy-start.16 = (f32[256,2,128]{2,1,0:T(2,128)S(1)}, f32[256,2,128]{2,1,0:T(2,128)}, u32[]{:S(2)}) copy-start(f32[256,2,128]{2,1,0:T(2,128)} %param.30) | copy-start | bytes 786436
  18.7 4.2 %copy-start.23 = (bf16[2,2,2,128,128]{4,3,2,1,0:T(8,128)(2,1)S(1)}, bf16[2,2,2,128,128]{4,3,2,1,0:T(8,128)(2,1)}, u32[]{:S(2)}) copy-start(bf16[2,2,2,128,128]{4,3,2,1,0:T(8,128)(2,1)} %constant.110.clone.blocks_ref) | copy-start | bytes 786436
  18.7 4.2 %copy-start.36 = (s32[128]{0:T(128)S(1)}, s32[128]{0:T(128)}, u32[]{:S(2)}) copy-start(s32[128]{0:T(128)} %param.33) | copy-start | bytes 1540
  22.3 5.4 %copy-start.38 = (f32[1,320]{1,0:T(1,128)}, f32[1,320]{1,0:T(1,128)S(1)}, u32[]{:S(2)}) copy-start(f32[1,320]{1,0:T(1,128)S(1)} %collective-permute-done.1.before_ref) | copy-start | bytes 3844
  28.3 15.2 %copy-start.44 = (f32[256]{0:T(256)S(1)}, f32[256]{0:T(256)}, u32[]{:S(2)}) copy-start(f32[256]{0:T(256)} %constant.102.clone) | copy-start | bytes 3076
  28.3 34.4 %copy-start.6 = (bf16[2,2,256,128]{3,2,1,0:T(8,128)(2,1)S(1)}, bf16[2,2,256,128]{3,2,1,0:T(8,128)(2,1)}, u32[]{:S(2)}) copy-start(bf16[2,2,256,128]{3,2,1,0:T(8,128)(2,1)} %constant.115.clone.halves_ref.by_modes_ref) | copy-start | bytes 786436
  28.3 34.4 %copy-start.7 = (f32[256,256]{1,0:T(8,128)S(1)}, f32[256,256]{1,0:T(8,128)}, u32[]{:S(2)}) copy-start(f32[256,256]{1,0:T(8,128)} %constant.113.clone.table_ref) | copy-start | bytes 786436
  28.3 34.4 %copy-start.8 = (bf16[2,2,128,256]{3,2,1,0:T(8,128)(2,1)S(1)}, bf16[2,2,128,256]{3,2,1,0:T(8,128)(2,1)}, u32[]{:S(2)}) copy-start(bf16[2,2,128,256]{3,2,1,0:T(8,128)(2,1)} %constant.112.clone.x_ref.x_split_ref) | copy-start | bytes 786436
  28.3 34.4 %copy-start.9 = (bf16[2,256,256]{2,1,0:T(8,128)(2,1)S(1)}, bf16[2,256,256]{2,1,0:T(8,128)(2,1)}, u32[]{:S(2)}) copy-start(bf16[2,256,256]{2,1,0:T(8,128)(2,1)} %constant.111.clone.sine_ref) | copy-start | bytes 786436
  28.3 34.4 %copy-start.32 = (f32[8,256]{1,0:T(8,128)S(1)}, f32[8,256]{1,0:T(8,128)}, u32[]{:S(2)}) copy-start(f32[8,256]{1,0:T(8,128)} %constant.114.clone.row_ref) | copy-start | bytes 24580
  29.2 32.4 %all-to-all-start = ((f32[128,5,128]{2,1,0:T(8,128)}), f32[128,5,128]{2,1,0:T(8,128)}, u32[]{:S(2)}, u32[]{:S(2)}) async-start(f32[128,5,128]{2,1,0:T(8,128)} %all_to_all.21), calls=%async_computation | async-start | bytes 1048576 | tf_op jit(solution)/shard_map/all_to_all | solution.py:474
  66.3 33.0 %copy-start.5 = (bf16[2,256,256]{2,1,0:T(8,128)(2,1)S(1)}, bf16[2,256,256]{2,1,0:T(8,128)(2,1)}, u32[]{:S(2)}) copy-start(bf16[2,256,256]{2,1,0:T(8,128)(2,1)} %constant.118.clone.x_ref) | copy-start | bytes 786436
  67.2 32.2 %copy-start.19 = (f32[256,256]{1,0:T(8,128)S(1)}, f32[256,256]{1,0:T(8,128)}, u32[]{:S(2)}) copy-start(f32[256,256]{1,0:T(8,128)} %constant.120.clone.full_ref) | copy-start | bytes 786436
  67.2 32.2 %copy-start.20 = (bf16[2,256,256]{2,1,0:T(8,128)(2,1)S(1)}, bf16[2,256,256]{2,1,0:T(8,128)(2,1)}, u32[]{:S(2)}) copy-start(bf16[2,256,256]{2,1,0:T(8,128)(2,1)} %constant.119.clone.xt_ref) | copy-start | bytes 786436
  95.3 4.0 %collective-permute-start.3 = (f32[640,128]{1,0:T(8,128)S(1)}, f32[640,128]{1,0:T(8,128)S(1)}, u32[]{:S(2)}, u32[]{:S(2)}) collective-permute-start(f32[640,128]{1,0:T(8,128)S(1)} %all_to_all.26.got_ref), channel_id=1, source_target_pairs={{0,1},{1,0},{2,3},{3,2},{4,5},{5,4},{6,7},{7,6},{8,9},{9,8},{10,11... | collective-permute-start | bytes 983048 | tf_op jit(solution)/shard_map/ppermute | solution.py:483
  111.1 7.2 %copy-start.4 = (f32[960,320]{1,0:T(8,128)S(1)}, f32[960,320]{1,0:T(8,128)}, u32[]{:S(2)}) copy-start(f32[960,320]{1,0:T(8,128)} %copy-done.2) | copy-start | bytes 3686404
  111.1 7.2 %copy-start.39 = (f32[1,320]{1,0:T(1,128)S(1)}, f32[1,320]{1,0:T(1,128)}, u32[]{:S(2)}) copy-start(f32[1,320]{1,0:T(1,128)} %copy-done.38) | copy-start | bytes 3844
  111.1 7.2 %copy-start.42 = (f32[1,320]{1,0:T(1,128)S(1)}, f32[1,320]{1,0:T(1,128)}, u32[]{:S(2)}) copy-start(f32[1,320]{1,0:T(1,128)} %copy-done.40) | copy-start | bytes 3844
  111.1 38.9 %all-to-all-start.2 = ((f32[256,6,128]{2,1,0:T(8,128)}), f32[256,6,128]{2,1,0:T(8,128)}, u32[]{:S(2)}, u32[]{:S(2)}) async-start(f32[256,6,128]{2,1,0:T(8,128)} %all_to_all.27), calls=%async_computation.2 | async-start | bytes 2097152 | tf_op jit(solution)/shard_map/all_to_all | solution.py:492
  118.3 3.4 %copy-start.30 = (f32[128,256]{1,0:T(8,128)S(1)}, f32[128,256]{1,0:T(8,128)}, u32[]{:S(2)}) copy-start(f32[128,256]{1,0:T(8,128)} %copy-done.29) | copy-start | bytes 393220
  118.3 3.4 %copy-start.35 = (f32[16,128]{1,0:T(8,128)S(1)}, f32[16,128]{1,0:T(8,128)}, u32[]{:S(2)}) copy-start(f32[16,128]{1,0:T(8,128)} %copy-done.34) | copy-start | bytes 24580
  122.6 7.2 %collective-permute-start.4 = (f32[1,320]{1,0:T(1,128)S(1)}, f32[1,320]{1,0:T(1,128)S(1)}, u32[]{:S(2)}, u32[]{:S(2)}) collective-permute-start(f32[1,320]{1,0:T(1,128)S(1)} %get-tuple-element.30), channel_id=1, source_target_pairs={{0,1},{1,2},{2,3},{3,4},{4,5},{5,6},{6,7},{7,8},{8,9},{9,10},{10,1... | collective-permute-start | bytes 3848 | tf_op jit(solution)/shard_map/ppermute | solution.py:435
  126.4 14.7 %collective-permute-start.5 = (f32[1,320]{1,0:T(1,128)S(1)}, f32[1,320]{1,0:T(1,128)S(1)}, u32[]{:S(2)}, u32[]{:S(2)}) collective-permute-start(f32[1,320]{1,0:T(1,128)S(1)} %get-tuple-element.31), channel_id=1, source_target_pairs={{1,0},{2,1},{3,2},{4,3},{5,4},{6,5},{7,6},{8,7},{9,8},{10,9},{11,1... | collective-permute-start | bytes 3848 | tf_op jit(solution)/shard_map/ppermute | solution.py:436
  145.5 5.8 %copy-start.17 = (bf16[2,2,128,256]{3,2,1,0:T(8,128)(2,1)S(1)}, bf16[2,2,128,256]{3,2,1,0:T(8,128)(2,1)}, u32[]{:S(2)}) copy-start(bf16[2,2,128,256]{3,2,1,0:T(8,128)(2,1)} %constant.123.clone.yt_ref) | copy-start | bytes 786436
  145.5 5.8 %copy-start.18 = (bf16[2,2,256,128]{3,2,1,0:T(8,128)(2,1)S(1)}, bf16[2,2,256,128]{3,2,1,0:T(8,128)(2,1)}, u32[]{:S(2)}) copy-start(bf16[2,2,256,128]{3,2,1,0:T(8,128)(2,1)} %constant.122.clone.y_ref) | copy-start | bytes 786436
  (21 other events, 23.9 us)

commit v2 on v1

v2 whole, which is shorter than its diff:
```python
import functools

import jax
import jax.numpy as jnp
import ml_dtypes
import numpy as np
from jax import lax
from jax.experimental import pallas as pl
from jax.experimental.pallas import tpu as pltpu
from jax.sharding import Mesh, PartitionSpec as P

ALL = ("g", "yl", "x", "z", "c")
SUB = ("yl", "x", "z", "c")
SAME_CORE = ("g", "yl", "x", "z")
N = 256
HALF = 128
DT = 0.05
VISC = 0.05
GAIN = 0.3
F32 = jnp.float32
BF16 = jnp.bfloat16
NN = ((1,), (0,))
NT = ((1,), (1,))
TN = ((0,), (0,))


def sine_table(length):
    numbers = np.arange(length) + 1
    phases = numbers[:, None] * numbers[None, :] % (2 * (length + 1))
    return np.sqrt(2.0 / (length + 1)) * np.sin(np.pi * phases / (length + 1))


def rates(length):
    return 2.0 - 2.0 * np.cos(np.pi * (np.arange(length) + 1) / (length + 1))


SINE = sine_table(N)
RATES = rates(N)
MODE_ORDER = np.array([2 * q + k for k in range(2) for q in range(HALF)])


def surface_response():
    total = np.zeros((N, N))
    for c in range(N):
        total += SINE[0, c] ** 2 / (1.0 + 64.0 * (RATES[c] + RATES[:, None] + RATES[None, :]))
    return total


Q = SINE.astype(np.float32)
Q_HALVES = np.concatenate([Q[:, :HALF], Q[:, HALF:]], axis=0)
RESPONSE = surface_response()[MODE_ORDER].astype(np.float32)


def lobatto_derivative():
    points = np.array([-1.0, -1.0 / np.sqrt(5.0), 1.0 / np.sqrt(5.0), 1.0])
    weights = np.array(
        [1.0 / np.prod([points[j] - points[k] for k in range(4) if k != j]) for j in range(4)]
    )
    deriv = np.zeros((4, 4))
    for i in range(4):
        for j in range(4):
            if i != j:
                deriv[i, j] = weights[j] / weights[i] / (points[i] - points[j])
        deriv[i, i] = -np.sum(deriv[i])
    return deriv


def operator_parts():
    deriv, eye = lobatto_derivative(), np.eye(4)
    along = [
        np.kron(eye, np.kron(eye, deriv)),
        np.kron(eye, np.kron(deriv, eye)),
        np.kron(deriv, np.kron(eye, eye)),
    ]
    second = sum(d @ d for d in along)
    pick = np.zeros((4, 4, 4, 4))
    for i in range(4):
        for j in range(4):
            pick[i, j, i, j] = 1.0
    eye16 = np.eye(16)
    right, left = np.kron(eye16, pick[3, 3]), np.kron(eye16, pick[0, 0])
    right_from, left_from = np.kron(eye16, pick[3, 0]), np.kron(eye16, pick[0, 3])
    fixed = np.kron(np.eye(5), np.eye(64) - 0.15 * right - 0.15 * left)
    fixed = fixed + DT * VISC * np.kron(np.diag([0.0, 1.0, 1.0, 1.0, 1.0]), second)
    by_x = -DT * along[0] + 0.15 * right - 0.15 * left
    return [
        np.asarray(a, np.float32)
        for a in (
            fixed,
            by_x,
            -DT * along[1],
            -DT * along[2],
            np.kron(np.eye(5), 0.15 * right_from),
            -0.15 * right_from,
            np.kron(np.eye(5), 0.15 * left_from),
            0.15 * left_from,
        )
    ]


FIXED, BY_X, BY_Y, BY_Z, NEXT_FIXED, NEXT_X, PREV_FIXED, PREV_X = operator_parts()


def wall_tables():
    groups = []
    for fixed, tables in ((FIXED, (BY_X, BY_Y, BY_Z)), (NEXT_FIXED, (NEXT_X,)), (PREV_FIXED, (PREV_X,))):
        groups.append(fixed[256:272] - fixed[0:16])
        groups += [np.tile(t[:16], (1, 5)) for t in tables]
    return np.stack(groups).astype(np.float32)


WALL_TABLES = wall_tables()
RATE_LIST = RATES.astype(np.float32)
RATE_ROW = (1.0 + 64.0 * RATES)[None, :].astype(np.float32)
RATE_COLUMN = (64.0 * RATES)[:, None].astype(np.float32)
SURFACE_ROW = np.broadcast_to(Q[:1], (8, N)).copy()
SURFACE_COLUMN = Q[:, :1].copy()
FIELD_HOT = np.pad(np.kron(np.eye(5), np.ones((64, 1))), ((0, 0), (0, 3))).astype(ml_dtypes.bfloat16)
TILE_HOT = np.kron(np.ones((5, 1)), np.eye(64)).astype(ml_dtypes.bfloat16)
OPERATORS = np.stack([BY_X, BY_Y, BY_Z, NEXT_X, PREV_X])


def split(value):
    high = value.astype(BF16)
    return high, (value - high.astype(F32)).astype(BF16)


def dot(a, b, dims=NN):
    return lax.dot_general(a, b, (dims, ((), ())), preferred_element_type=F32)


def dot3(a, b, dims=NN):
    a = split(a) if not isinstance(a, tuple) else a
    b = split(b) if not isinstance(b, tuple) else b
    return dot(a[0], b[0], dims) + (dot(a[0], b[1], dims) + dot(a[1], b[0], dims))


def hot_dot(hot, b, dims=NN):
    high, low = split(b)
    return dot(hot, high, dims) + dot(hot, low, dims)


def dot_hot(a, hot, dims=NN):
    high, low = split(a)
    return dot(high, hot, dims) + dot(low, hot, dims)


def hot_of(condition):
    return jnp.where(condition, 1.0, 0.0).astype(BF16)


def iota(shape, dim):
    return lax.broadcasted_iota(jnp.int32, shape, dim)


def rows(ref, first, count, stride):
    return ref[pl.ds(first, count, stride) if stride > 1 else pl.ds(first, count), :]


def sine_rows(ref, first, count, stride):
    return jnp.concatenate([rows(ref, h * N + first, count, stride) for h in range(2)], axis=1)


def x_ordered(sine_ref):
    blocks = [sine_rows(sine_ref, 2 * k + i, 64, 4) for i in range(2) for k in range(2)]
    return split(jnp.concatenate(blocks, axis=0))


def mode_ordered(sine_ref):
    return jnp.concatenate([sine_rows(sine_ref, k, HALF, 2) for k in range(2)], axis=0)


def edges_kernel(left_ref, right_ref, elem_ref, owner_ref, patch_ref, first_ref, last_ref, *, count):
    lane = iota((1, 384), 1)
    gap = jnp.zeros((1, 64), F32)
    for ref, block, at, out, element in (
        (left_ref, left_ref[...], (0, 1), first_ref, 0),
        (right_ref, right_ref[...], (HALF - 1, HALF - 2), last_ref, count - 1),
    ):
        turned = block.T
        met = elem_ref[...] == element
        owner = jnp.sum(jnp.where(met, owner_ref[...] + 1, 0).astype(F32), axis=1, keepdims=True)
        patch = jnp.sum(jnp.where(met, patch_ref[...], 0).astype(F32), axis=1, keepdims=True)
        slot = jnp.where(lane == 0, owner, jnp.where(lane == 1, patch, 0.0))
        out[0:1] = jnp.concatenate([turned[at[0] : at[0] + 1], gap], axis=1)
        out[1:2] = jnp.concatenate([turned[at[1] : at[1] + 1], gap], axis=1)
        out[2:3] = slot
        out[3:8] = jnp.zeros((5, 384), F32)


def walls_kernel(jac_ref, fluid_ref, table_ref, out_ref, matrix_ref):
    @pl.when(pl.program_id(0) == 0)
    def _():
        field = iota((1, 320), 1) // 64
        coefficients = []
        for d in range(3):
            row = jnp.zeros((1, 320), F32)
            for f in range(5):
                row = jnp.where(field == f, jac_ref[d, 4, f] - jac_ref[d, 0, f], row)
            coefficients.append(row)
        own = table_ref[0]
        for d in range(3):
            own = own + coefficients[d] * table_ref[1 + d]
        matrix_ref[0:16] = own
        matrix_ref[16:32] = table_ref[4] + coefficients[0] * table_ref[5]
        matrix_ref[32:48] = table_ref[6] + coefficients[0] * table_ref[7]

    out_ref[0:48] = dot3(matrix_ref[...], fluid_ref[...])
    out_ref[48:64] = fluid_ref[256:272] - fluid_ref[0:16]


def matrices_kernel(jac_ref, field_ref, tile_ref, fixed_ref, operators_ref, out_ref):
    field, tile = field_ref[...], tile_ref[...]

    def spread(d):
        return dot_hot(hot_dot(field, jac_ref[d]), field, NT)

    def tiled(d):
        return dot_hot(hot_dot(tile, operators_ref[d]), tile, NT)

    by_x = spread(0)
    own = by_x * tiled(0) + spread(1) * tiled(1) + spread(2) * tiled(2)
    out_ref[0:320] = fixed_ref[0] + own
    out_ref[320:640] = fixed_ref[1] + by_x * tiled(3)
    out_ref[640:960] = fixed_ref[2] + by_x * tiled(4)


def first_kernel(
    where_ref, solid_ref, far_ref, wall_ref, matrix_ref, before_ref, after_ref, elem_ref,
    owner_col_ref, owner_ref, patch_ref, sine_ref, out_ref, trace_ref, surface_ref
):
    group = where_ref[0]
    near, far = [
        split(sine_ref[pl.ds(pl.multiple_of(half * N + group * HALF, HALF), HALF), :])
        for half in (group, 1 - group)
    ]
    for i in range(2):
        modes = dot3(near, rows(solid_ref, i, N, 2), NT) + dot3(far, rows(far_ref, i, N, 2), NT)
        for h in range(2):
            out_ref[pl.ds(2 * i + h, HALF, 5), :] = modes[:, h * HALF : (h + 1) * HALF]
    surface_ref[...] = solid_ref[0:2]

    def halo(part, ref):
        return jnp.sum(matrix_ref[16 * part : 16 * part + 16] * ref[0:1, 0:320], axis=1, keepdims=True)

    wall0, own = wall_ref[48:64], wall_ref[0:16]
    count = own.shape[1]
    lane = iota(own.shape, 1)
    following = pltpu.roll(wall_ref[16:32], count - 1, 1)
    preceding = pltpu.roll(wall_ref[32:48], 1, 1)
    later = own + jnp.where(lane == count - 1, halo(1, after_ref), following)
    later = later + jnp.where(lane == 0, halo(2, before_ref), preceding)
    elem_hot = hot_of(elem_ref[...] == iota((HALF, count), 1))
    values = dot_hot(jnp.concatenate([wall0, later - GAIN * wall0], axis=0), elem_hot, NT)
    trace_ref[...] = values[:16]
    owner = owner_ref[...]
    square = (HALF, HALF)
    same = (owner_col_ref[...] == owner) & (iota(square, 0) < iota(square, 1))
    place = jnp.sum(jnp.where(same, 1.0, 0.0), axis=0, keepdims=True)
    ids = jnp.broadcast_to((patch_ref[...] + 1).astype(F32), (8, HALF))
    filler = jnp.zeros((24, HALF), F32)
    sent = jnp.concatenate([values, ids, filler], axis=0)
    none = jnp.zeros((64, HALF), F32)
    arranged = 0.0
    for i in range(2):
        hot = hot_of((iota(square, 0) == owner) & (place == float(i)))
        padded = jnp.concatenate([sent, none] if i == 0 else [none, sent], axis=0)
        arranged = arranged + hot_dot(hot, padded, NT)
    out_ref[pl.ds(4, HALF, 5), :] = arranged


def modes_kernel(
    where_ref, rate_ref, got_ref, surface_ref, sine_ref, rate_row_ref, rate_col_ref, row_ref,
    modes_ref, out_ref
):
    group, me = where_ref[0], where_ref[2]
    sine = split(sine_rows(sine_ref, 0, N, 1))
    modes = 0.0
    for i in range(2):
        part = jnp.concatenate([rows(got_ref, 2 * i + h, HALF, 5) for h in range(2)], axis=1)
        by_z = dot3(sine, part, NT)
        modes = modes + dot3(by_z, sine_rows(sine_ref, i, HALF, 2))
    modes_ref[...] = modes
    once = modes / (rate_col_ref[...] + (rate_row_ref[...] + 64.0 * rate_ref[me]))
    surface_row = dot3(row_ref[...], once)[0:1]

    fluid = rows(got_ref, 4, HALF, 5)
    square = (HALF, HALF)
    lane = iota(square, 1)
    fluid_pair = split(fluid)
    sums = [[0.0, 0.0], [0.0, 0.0]]
    counts = [0.0, 0.0]
    count_lanes = 0.0
    for i in range(2):
        ids = fluid[:, i * 64 + 32 : i * 64 + 33].astype(jnp.int32) - 1
        count_lanes = count_lanes + jnp.sum(jnp.where(ids == lane, 1.0, 0.0), axis=0, keepdims=True)
        for f in range(2):
            pick = hot_of(iota(square, 0) == i * 64 + f * 16 + lane % 16)
            values = dot(fluid_pair[0], pick) + dot(fluid_pair[1], pick)
            for xl in range(2):
                mask = ids == xl * 8 + lane // 16
                sums[f][xl] = sums[f][xl] + jnp.sum(
                    jnp.where(mask, values, 0.0), axis=0, keepdims=True
                )
                if f == 0:
                    counts[xl] = counts[xl] + jnp.sum(
                        jnp.where(mask, 1.0, 0.0), axis=0, keepdims=True
                    )
    heat = [sums[0][xl] - counts[xl] * surface_ref[xl : xl + 1, :] for xl in range(2)]
    tail = jnp.where(lane < 16, count_lanes, 0.0)
    for k in range(2):
        by_modes = split(sine_ref[pl.ds(group * N + k, HALF, 2), :])
        for xl in range(2):
            column = dot3(by_modes, jnp.broadcast_to(sums[1][xl], (8, HALF)), NT)[:, 0:1]
            tail = jnp.where(lane == 16 + 2 * k + xl, column, tail)
    shared = [surface_row[:, :HALF], surface_row[:, HALF:], heat[0], heat[1]]
    for r in range(4):
        out_ref[pl.ds(r, HALF, 5), :] = jnp.broadcast_to(shared[r], square)
    out_ref[pl.ds(4, HALF, 5), :] = tail


def solve_kernel(
    where_ref, rate_ref, got_ref, other_ref, modes_ref, response_ref, sine_ref, rate_row_ref,
    rate_col_ref, row_ref, column_ref, surface_ref, out_ref, heat_ref
):
    core, me = where_ref[1], where_ref[2]
    first = jnp.full((HALF, HALF), core, jnp.int32) == 0
    ordered = []
    for r in range(5):
        mine, theirs = rows(got_ref, r, HALF, 5), rows(other_ref, r, HALF, 5)
        ordered.append((jnp.where(first, mine, theirs), jnp.where(first, theirs, mine)))

    def block(g, r):
        return jnp.concatenate([ordered[r][k][g * 64 : (g + 1) * 64] for k in range(2)], axis=0)

    by_modes = mode_ordered(sine_ref)
    halves = [split(by_modes[:, g * HALF : (g + 1) * HALF]) for g in range(2)]
    by_x = x_ordered(sine_ref)
    heat_modes = 0.0
    for xl in range(2):
        by_y = 0.0
        for g in range(2):
            by_y = by_y + dot3(halves[g], block(g, 2 + xl), NT)
        at = slice(xl * HALF, (xl + 1) * HALF)
        heat_modes = heat_modes + dot3(by_y, (by_x[0][at], by_x[1][at]))
    heat_ref[...] = heat_modes
    given = jnp.concatenate(
        [jnp.concatenate([ordered[h][k] for h in range(2)], axis=1) for k in range(2)], axis=0
    )
    surface = dot3(split(by_modes.T), given + response_ref[...] * heat_modes)
    surface = dot3(surface, by_x, NT)
    surface_ref[...] = surface
    square = (HALF, HALF)
    tails = [block(g, 4) for g in range(2)]
    tail_pairs = [tail.astype(BF16) for tail in tails]
    expand = [hot_of(iota(square, 1) == xl * 8 + iota(square, 0) // 16) for xl in range(2)]
    count = jnp.concatenate(
        [
            jnp.concatenate([dot(expand[xl], tail_pairs[g], NT) for xl in range(2)], axis=1)
            for g in range(2)
        ],
        axis=0,
    )
    own_sine = jnp.broadcast_to(sine_rows(sine_ref, me, 1, 1), (8, N))
    reduced = dot3(own_sine, count * surface)
    tail_sum = tails[0] + tails[1]
    lane8 = iota((8, HALF), 1)
    later = jnp.concatenate(
        [hot_dot(hot_of(lane8 == 16 + 2 * core + xl), tail_sum, NT) for xl in range(2)], axis=1
    )
    heat1 = dot3(later - 0.7 * reduced, by_x)[0:1]
    heat0 = heat_ref[pl.ds(core * HALF + me // 2, 1), :]
    decay = 1.0 / (rate_col_ref[...] + (rate_row_ref[...] + 64.0 * rate_ref[me]))
    column = column_ref[...]
    final = decay * (decay * (modes_ref[...] + column * heat0) + column * heat1)
    final_row = dot3(row_ref[...], final)[0:1]
    final = split(final)
    sine = split(sine_rows(sine_ref, 0, N, 1))
    for xl in range(2):
        back = dot3(dot3(sine_rows(sine_ref, xl, HALF, 2), final, NT), sine)
        for g in range(2):
            for h in range(2):
                out_ref[pl.ds(g * 768 + 2 * xl + h, HALF, 6), :] = back[:, h * HALF : (h + 1) * HALF]
    for h in range(2):
        out_ref[pl.ds(4 + h, N, 6), :] = jnp.broadcast_to(
            final_row[:, h * HALF : (h + 1) * HALF], (N, HALF)
        )


def met_values(surface, owner, patch):
    x_of_slot = patch // 8 * HALF + owner % 2 * 64 + owner // 2
    x_hot = hot_of(iota((N, HALF), 0) == x_of_slot)
    met = dot_hot(surface, x_hot)
    return jnp.where(iota((HALF, HALF), 0) // 16 == patch % 8, met, 0.0)


def folded(met):
    fold = hot_of(iota((16, HALF), 0) == iota((16, HALF), 1) % 16)
    return hot_dot(fold, met)


def stepped(extended, matrix_ref):
    fluid = split(extended)
    width = extended.shape[1]
    own, following, preceding = [
        dot3(matrix_ref[pl.ds(320 * i, 320), :], fluid) for i in range(3)
    ]
    return own + pltpu.roll(following, width - 1, 1) + pltpu.roll(preceding, 1, 1)


def step_kernel(where_ref, fluid_ref, matrix_ref, before_ref, after_ref, out_ref):
    count = fluid_ref.shape[1]
    me = where_ref[2]
    lane = iota((320, HALF), 1)
    following, preceding = after_ref[...].T[0:320], before_ref[...].T[0:320]
    halo = jnp.zeros((320, HALF), F32)
    for at, column in (
        (0, following[:, 0:1]),
        (1, following[:, 1:2]),
        (HALF - 1, preceding[:, 0:1]),
        (HALF - 2, preceding[:, 1:2]),
    ):
        halo = jnp.where(lane == at, column, halo)
    result = stepped(jnp.concatenate([fluid_ref[...], halo], axis=1), matrix_ref)
    edge = result[:, count:]
    beyond = ((lane == 0) & (me == 255)) | ((lane == HALF - 1) & (me == 0))
    out_ref[:, :count] = result[:, :count]
    out_ref[:, count:] = jnp.where(beyond, 0.0, edge)


def second_kernel(
    where_ref, fluid_ref, surface_ref, trace_ref, matrix_ref, before_ref, after_ref, elem_ref,
    owner_ref, patch_ref, out_ref, later_ref
):
    group, me = where_ref[0], where_ref[2]
    width = fluid_ref.shape[1]
    count = width - HALF
    own_surface = surface_ref[pl.ds(pl.multiple_of(group * HALF, HALF), HALF), :]
    elem_hot = hot_of(elem_ref[...] == iota((HALF, count), 1))
    met = folded(met_values(own_surface, owner_ref[...], patch_ref[...]))
    source = GAIN * dot_hot(met - trace_ref[...], elem_hot)
    square = (16, HALF)
    edge = jnp.zeros(square, F32)
    for ref, at, device in ((after_ref, 0, me + 1), (before_ref, HALF - 1, me - 1)):
        owner = ref[2:3, 0:1].astype(jnp.int32) - 1
        patch = ref[2:3, 1:2].astype(jnp.int32)
        side = jnp.clip(device, 0, 255) // HALF
        near = surface_ref[pl.ds(pl.multiple_of(side * HALF, HALF), HALF), :]
        lanes = jnp.zeros((1, HALF), jnp.int32)
        value = folded(met_values(near, owner + lanes, patch + lanes))
        column = ref[...].T
        value = GAIN * (value - (column[256:272, 0:1] - column[0:16, 0:1]))
        used = (iota(square, 1) == at) & (owner >= 0)
        edge = jnp.where(used, value, edge)
    walls = fluid_ref[256:272] + jnp.concatenate([source, edge], axis=1)
    later_ref[...] = dot_hot(walls[:, :count] - fluid_ref[0:16, :count], elem_hot, NT)
    extended = jnp.concatenate([fluid_ref[0:256], walls, fluid_ref[272:320]], axis=0)
    out_ref[...] = stepped(extended, matrix_ref)[:, :count]


def last_kernel(
    where_ref, got_ref, sine_ref, later_ref, elem_ref, owner_ref, patch_ref, fluid_ref,
    solid_ref, out_ref
):
    group = where_ref[0]
    by_y = split(sine_ref[pl.ds(pl.multiple_of(group * N, N), N), :])
    for xl in range(2):
        for h in range(2):
            part = rows(got_ref, 2 * xl + h, N, 6)
            solid_ref[pl.ds(h * N + xl, HALF, 2), :] = dot3(part, by_y, TN)
    given = jnp.concatenate([rows(got_ref, 4 + h, N, 6) for h in range(2)], axis=1)
    own_rows = sine_rows(sine_ref, pl.multiple_of(group * HALF, HALF), HALF, 1)
    surface = dot3(dot3(own_rows, given), x_ordered(sine_ref), NT)
    met = folded(met_values(surface, owner_ref[...], patch_ref[...]))
    elem_hot = hot_of(elem_ref[...] == iota((HALF, fluid_ref.shape[1]), 1))
    out_ref[...] = fluid_ref[...] + GAIN * dot_hot(met - later_ref[...], elem_hot)


def call(kernel, outs, args, scalars=0, scratch=(), aliases=None, specs=None, out_specs=None, cost=None):
    whole = pl.BlockSpec(memory_space=pltpu.VMEM)
    given = [pl.BlockSpec(memory_space=pltpu.SMEM)] * scalars + [whole] * (len(args) - scalars)
    return pl.pallas_call(
        kernel,
        out_shape=[jax.ShapeDtypeStruct(shape, F32) for shape in outs],
        in_specs=specs or given,
        out_specs=out_specs or [whole] * len(outs),
        scratch_shapes=list(scratch),
        input_output_aliases=aliases or {},
        cost_estimate=pl.CostEstimate(flops=int(cost or 1e8), bytes_accessed=1 << 20, transcendentals=0),
        compiler_params=pltpu.CompilerParams(vmem_limit_bytes=40 << 20),
    )(*args)


def exchange(payload, axes):
    chunks = payload.reshape(payload.shape[0], 1, HALF)
    return lax.all_to_all(chunks, axes, split_axis=0, concat_axis=0, tiled=True).reshape(payload.shape)


def on_device(fluid_state, flux_jacobian, solid_temp, iface_elem, iface_owner, iface_patch):
    me = lax.axis_index(ALL)
    where = jnp.stack([me // HALF, me % 2, me]).astype(jnp.int32)
    fluid0 = fluid_state.reshape(320, -1)
    count = fluid0.shape[1]
    solid = solid_temp.reshape(2 * N, HALF)
    elem = iface_elem[:, None]
    owner, patch = iface_owner.reshape(1, HALF), iface_patch[None, :]
    smem = pl.BlockSpec(memory_space=pltpu.SMEM)

    far = lax.ppermute(solid, "g", [(0, 1), (1, 0)])
    row_spec = pl.BlockSpec((1, HALF), lambda i: (0, 0))
    first, last = pl.pallas_call(
        functools.partial(edges_kernel, count=count),
        grid=(1,),
        out_shape=[jax.ShapeDtypeStruct((8, 384), F32)] * 2,
        in_specs=[
            pl.BlockSpec((320, HALF), lambda i: (0, 0)),
            pl.BlockSpec((320, HALF), lambda i: (0, count // HALF - 1)),
        ]
        + [row_spec] * 3,
        out_specs=[pl.BlockSpec((8, 384), lambda i: (0, 0))] * 2,
    )(fluid0, fluid0, iface_elem[None, :], owner, patch)
    before = lax.ppermute(last, ALL, [(i, i + 1) for i in range(255)])
    after = lax.ppermute(first, ALL, [(i + 1, i) for i in range(255)])
    walls, wall_matrix = pl.pallas_call(
        walls_kernel,
        grid=(4,),
        out_shape=[jax.ShapeDtypeStruct((64, count), F32), jax.ShapeDtypeStruct((48, 320), F32)],
        in_specs=[
            smem,
            pl.BlockSpec((320, count // 4), lambda i: (0, i)),
            pl.BlockSpec((8, 16, 320), lambda i: (0, 0, 0)),
        ],
        out_specs=[
            pl.BlockSpec((64, count // 4), lambda i: (0, i)),
            pl.BlockSpec((48, 320), lambda i: (0, 0)),
        ],
    )(flux_jacobian, fluid0, WALL_TABLES)
    pay1, trace0, surface0 = call(
        first_kernel,
        [(5 * HALF, HALF), (16, HALF), (2, HALF)],
        [where, solid, far, walls, wall_matrix, before, after, elem, iface_owner, owner, patch, Q_HALVES],
        scalars=1,
    )
    got1 = exchange(pay1, SUB)
    jacobian = jnp.pad(flux_jacobian, ((0, 0), (0, 3), (0, 3)))
    (matrix,) = call(
        matrices_kernel,
        [(960, 320)],
        [jacobian, FIELD_HOT, TILE_HOT, np.stack([FIXED, NEXT_FIXED, PREV_FIXED]), OPERATORS],
    )
    (fluid1,) = call(
        step_kernel,
        [(320, count + HALF)],
        [where, fluid0, matrix, before, after],
        scalars=1,
        cost=2e9,
    )
    modes, pay2 = call(
        modes_kernel,
        [(N, N), (5 * HALF, HALF)],
        [where, RATE_LIST, got1, surface0, Q_HALVES, RATE_ROW, RATE_COLUMN, SURFACE_ROW],
        scalars=2,
    )
    got2 = exchange(pay2, SAME_CORE)
    other = lax.ppermute(got2, "c", [(0, 1), (1, 0)])
    surface1, pay3 = call(
        solve_kernel,
        [(N, N), (6 * N, HALF)],
        [where, RATE_LIST, got2, other, modes, RESPONSE, Q_HALVES, RATE_ROW, RATE_COLUMN, SURFACE_ROW,
         SURFACE_COLUMN],
        scalars=2,
        scratch=[pltpu.VMEM((N, N), F32)],
    )
    got3 = exchange(pay3, ALL)
    fluid2, trace1 = call(
        second_kernel,
        [(320, count), (16, HALF)],
        [where, fluid1, surface1, trace0, matrix, before, after, elem, owner, patch],
        scalars=1,
        cost=2e9,
    )
    solid_out, fluid2 = pl.pallas_call(
        last_kernel,
        grid=(1,),
        out_shape=[
            jax.ShapeDtypeStruct((2 * N, HALF), F32),
            jax.ShapeDtypeStruct((320, count), F32),
        ],
        in_specs=[smem]
        + [pl.BlockSpec(memory_space=pltpu.VMEM)] * 6
        + [pl.BlockSpec((16, count), lambda i: (16, 0))],
        out_specs=[
            pl.BlockSpec((2 * N, HALF), lambda i: (0, 0)),
            pl.BlockSpec((16, count), lambda i: (16, 0)),
        ],
        input_output_aliases={7: 1},
        compiler_params=pltpu.CompilerParams(vmem_limit_bytes=40 << 20),
    )(where, got3, Q_HALVES, trace1, elem, owner, patch, fluid2)
    return fluid2.reshape(fluid_state.shape), solid_out.reshape(solid_temp.shape)


def solution(mesh):
    fine = Mesh(mesh.devices.reshape(2, 2, 4, 8, 2), ALL)
    placed = (
        P(None, None, ALL),
        P(),
        P(None, SUB, "g"),
        P(ALL),
        P(ALL, None),
        P(ALL),
    )
    return jax.shard_map(
        on_device,
        mesh=fine,
        in_specs=placed,
        out_specs=(P(None, None, ALL), P(None, SUB, "g")),
        check_vma=False,
    )
```

time: 155 us -> 118 us (0.76)
  blocking collectives: 27.1 us -> 50.6 us
  local copies, waits for them, and re-layouts: 26.2 us -> 2.75 us
  starting transfers between devices: 40 us -> 18.1 us
  waiting for transfers between devices: 36 us -> 15.1 us
  Pallas kernels: 23.6 us -> 29.7 us
    all_to_all x1 -> x2, blocking collectives: 27.1 us -> 50.6 us  [exchange(): lax.all_to_all(chunks, axes, split_axis=0, concat_axis=0, tiled=True)]
    all_to_all x2 -> x1, starting transfers between devices: 21.4 us -> 5.41 us  [exchange(): lax.all_to_all(chunks, axes, split_axis=0, concat_axis=0, tiled=True)]
    unnamed x92 -> x42, local copies, waits for them, and re-layouts: 18 us -> 2.63 us
    ppermute x4 -> x2, waiting for transfers between devices: 12.8 us -> 0.01 us  [the longest x1 0.01 us: on_device(): before = lax.ppermute(last, ALL, [(i, i + 1) for i in range(255)])]
    all_to_all x2 -> x1, waiting for transfers between devices: 22 us -> 13.8 us  [exchange(): lax.all_to_all(chunks, axes, split_axis=0, concat_axis=0, tiled=True)]
    all_to_all x6 -> x0, local copies, waits for them, and re-layouts: 7.37 us -> none  [the longest x2 3.51 us: on_device(): got3 = lax.all_to_all(pay3, ALL, split_axis=0, concat_axis=0, tiled=True)]
    ppermute x4 -> x2, starting transfers between devices: 12 us -> 6.44 us  [the longest x1 4.52 us: on_device(): before = lax.ppermute(last, ALL, [(i, i + 1) for i in range(255)])]
    pallas_call x1 -> x2, Pallas kernels: 1.9 us -> 5.6 us  [the longest x1 3.78 us: on_device(): pl.pallas_call(walls_kernel, grid=(4,), out_shape=[jax.ShapeDtypeStruct((...]
  transfers between devices with their start and end apart: 8 -> 5, of which waited for: 5 -> 2; matrix products, arithmetic and copies ran while one was open for 1% -> 1% of each run, Pallas kernels for 8% -> 16%
where the time goes in v2:
time: 118 us; the launch traced here: 117 us
  blocking collectives  50.6 us (43%)
  Pallas kernels  29.7 us (25%)
  starting transfers between devices  18.1 us (15%)
  waiting for transfers between devices  15.1 us (13%)
  local copies, waits for them, and re-layouts  2.75 us (2%)
    all_to_all x2, blocking collectives, exchange(): lax.all_to_all(chunks, axes, split_axis=0, concat_axis=0, tiled=True)  50.6 us
    pallas_call x6, Pallas kernels, call(): pl.pallas_call(kernel, out_shape=[jax.ShapeDtypeStruct(shape, F32) for sh...  21.4 us
    all_to_all x1, waiting for transfers between devices, exchange(): lax.all_to_all(chunks, axes, split_axis=0, concat_axis=0, tiled=True)  13.8 us
    all_to_all x1, starting transfers between devices, exchange(): lax.all_to_all(chunks, axes, split_axis=0, concat_axis=0, tiled=True)  5.41 us
    ppermute x1, starting transfers between devices, on_device(): before = lax.ppermute(last, ALL, [(i, i + 1) for i in range(255)])  4.52 us
    ppermute x1, starting transfers between devices, on_device(): far = lax.ppermute(solid, 'g', [(0, 1), (1, 0)])  3.83 us
    pallas_call x1, Pallas kernels, on_device(): pl.pallas_call(walls_kernel, grid=(4,), out_shape=[jax.ShapeDtypeStruct((...  3.78 us
    pallas_call x1, Pallas kernels, on_device(): pl.pallas_call(last_kernel, grid=(1,), out_shape=[jax.ShapeDtypeStruct((2...  2.71 us
  transfers between devices with their start and end apart: 5, of which 2 were waited for; matrix products, arithmetic and copies ran while one was open for 1% of the time, Pallas kernels for 16%

profile of v2, /device:TPU:1, one launch (start us, length us, event | category | flops | bytes accessed | tf_op | source)
XLA Modules:
  0.0 117.2 jit_solution(3350096226626942221)
XLA Ops:
  0.7 3.8 %collective-permute-start = (f32[512,128]{1,0:T(8,128)}, f32[512,128]{1,0:T(8,128)S(1)}, u32[]{:S(2)}, u32[]{:S(2)}) collective-permute-start(f32[512,128]{1,0:T(8,128)} %bitcast.33), channel_id=1, source_target_pairs={{0,128},{128,0},{1,129},{129,1},{2,130},{130,2},{3,131},{131,3},{4... | collective-permute-start | bytes 786440 | tf_op jit(solution)/shard_map/ppermute | solution.py:509
  4.5 1.8 %shard_map.186 = (f32[8,384]{1,0:T(8,128)}, f32[8,384]{1,0:T(8,128)}) custom-call(f32[320,1024]{1,0:T(8,128)} %bitcast.23, f32[320,1024]{1,0:T(8,128)} %bitcast.24, s32[1,128]{1,0:T(1,128)} %bitcast.44, s32[1,128]{1,0:T(1,128)} %bitcast.35, s32[1,128]{1,0:T(1,128)} %bitcast.39), custom_call_target="tpu_custom_call" | custom-call | tf_op jit(solution)/shard_map/pallas_call | solution.py:511
  6.3 4.5 %collective-permute-start.1 = (f32[8,384]{1,0:T(8,128)}, f32[8,384]{1,0:T(8,128)S(1)}, u32[]{:S(2)}, u32[]{:S(2)}) collective-permute-start(f32[8,384]{1,0:T(8,128)} %get-tuple-element.19), channel_id=1, source_target_pairs={{0,1},{1,2},{2,3},{3,4},{4,5},{5,6},{6,7},{7,8},{8,9},{9,10},{10,1... | collective-permute-start | bytes 36872 | tf_op jit(solution)/shard_map/ppermute | solution.py:522
  10.8 1.9 %collective-permute-start.2 = (f32[8,384]{1,0:T(8,128)}, f32[8,384]{1,0:T(8,128)S(1)}, u32[]{:S(2)}, u32[]{:S(2)}) collective-permute-start(f32[8,384]{1,0:T(8,128)} %get-tuple-element.20), channel_id=1, source_target_pairs={{1,0},{2,1},{3,2},{4,3},{5,4},{6,5},{7,6},{8,7},{9,8},{10,9},{11,1... | collective-permute-start | bytes 36872 | tf_op jit(solution)/shard_map/ppermute | solution.py:523
  12.8 0.1 pad_add_fusion.where_ref
  12.9 0.1 copy.29.owner_col_ref
  13.0 0.6 copy.27.jac_ref
  13.6 0.1 copy.28.elem_ref
  13.7 0.0 copy-start.12
  13.7 0.0 copy-start.15
  13.7 0.0 copy-start.16
  13.8 3.8 %shard_map.185 = (f32[64,1024]{1,0:T(8,128)}, f32[48,320]{1,0:T(8,128)}) custom-call(f32[3,5,5]{2,1,0:T(8,128)} %copy.27.jac_ref, f32[320,1024]{1,0:T(8,128)} %bitcast.25, f32[8,16,320]{2,1,0:T(8,128)} %constant.80.clone.table_ref), custom_call_target="tpu_custom_call" | custom-call | tf_op jit(solution)/shard_map/pallas_call | solution.py:524
  17.6 0.0 copy-start.6
  17.6 0.9 copy-done.6
  18.5 0.9 copy-done.11
  19.4 1.4 %shard_map.187 = (f32[640,128]{1,0:T(8,128)S(1)}, f32[16,128]{1,0:T(8,128)S(1)}, f32[2,128]{1,0:T(2,128)S(1)}) custom-call(s32[3]{0:T(128)S(1)} %pad_add_fusion.where_ref, f32[512,128]{1,0:T(8,128)S(1)} %bitcast.34, f32[512,128]{1,0:T(8,128)S(1)} %collective-permute-done.far_ref, f32[64,1024]{1,0:T(8,128)S(1)} %copy-done.6, f32[48,320]{1,0:T(8,128)S(1)} %copy-done.11, ...), custom_call_target="tpu_custom_call" | custom-call | flops 100000000 | bytes 1048576 | tf_op jit(solution)/shard_map/pallas_call | solution.py:482
  20.8 28.1 %all_to_all.15 = f32[640,1,128]{2,1,0:T(1,128)S(1)} all-to-all(f32[640,1,128]{2,1,0:T(1,128)S(1)} %bitcast.31), channel_id=1, replica_groups=mesh['g'=2,'yl'=2,'x'=4,'z'=8,'c'=2] {'yl','x','z','c'}, dimensions={0} | all-to-all | bytes 655360 | tf_op jit(solution)/shard_map/all_to_all | solution.py:496
  48.9 2.3 %shard_map.188 = (f32[256,256]{1,0:T(8,128)S(1)}, f32[640,128]{1,0:T(8,128)S(1)}) custom-call(s32[3]{0:T(128)S(1)} %pad_add_fusion.where_ref, f32[256]{0:T(256)S(1)} %copy-done.16, f32[640,128]{1,0:T(8,128)S(1)} %bitcast.28, f32[2,128]{1,0:T(2,128)S(1)} %get-tuple-element.22.surface_ref, f32[512,128]{1,0:T(8,128)S(1)} %copy-done.1, f32[1,256]{1,0:T(1,128)S(1)} %copy-done.15, ...), custom_call_target="tpu_custom_call" | custom-call | flops 100000000 | bytes 1048576 | tf_op jit(solution)/shard_map/pallas_call | solution.py:482
  51.2 22.6 %all_to_all.16 = f32[640,1,128]{2,1,0:T(1,128)S(1)} all-to-all(f32[640,1,128]{2,1,0:T(1,128)S(1)} %bitcast.32), channel_id=1, replica_groups=mesh['g'=2,'yl'=2,'x'=4,'z'=8,'c'=2] {'g','yl','x','z'}, dimensions={0} | all-to-all | bytes 655360 | tf_op jit(solution)/shard_map/all_to_all | solution.py:496
  73.8 2.4 %collective-permute-start.3 = (f32[640,128]{1,0:T(8,128)S(1)}, f32[640,128]{1,0:T(8,128)S(1)}, u32[]{:S(2)}, u32[]{:S(2)}) collective-permute-start(f32[640,128]{1,0:T(8,128)S(1)} %bitcast.29), channel_id=1, source_target_pairs={{0,1},{1,0},{2,3},{3,2},{4,5},{5,4},{6,7},{7,6},{8,9},{9,8},{10,11... | collective-permute-start | bytes 983048 | tf_op jit(solution)/shard_map/ppermute | solution.py:565
  76.2 1.3 %collective-permute-done.3.other_ref = f32[640,128]{1,0:T(8,128)S(1)} collective-permute-done((f32[640,128]{1,0:T(8,128)S(1)}, f32[640,128]{1,0:T(8,128)S(1)}, u32[]{:S(2)}, u32[]{:S(2)}) %collective-permute-start.3) | collective-permute-done | bytes 327712 | tf_op jit(solution)/shard_map/ppermute | solution.py:565
  77.4 0.0 copy-start.7
  77.4 0.0 copy-start.9
  77.5 0.0 copy-start.10
  77.5 4.6 %shard_map.189 = (f32[256,256]{1,0:T(8,128)S(1)}, f32[1536,128]{1,0:T(8,128)}) custom-call(s32[3]{0:T(128)S(1)} %pad_add_fusion.where_ref, f32[256]{0:T(256)S(1)} %copy-done.16, f32[640,128]{1,0:T(8,128)S(1)} %bitcast.30, f32[640,128]{1,0:T(8,128)S(1)} %collective-permute-done.3.other_ref, f32[256,256]{1,0:T(8,128)S(1)} %get-tuple-element.24.modes_ref, ...), custom_call_target="tpu_custom_call" | custom-call | flops 100000000 | bytes 1048576 | tf_op jit(solution)/shard_map/pallas_call | solution.py:482
  82.1 5.4 %all-to-all-start.2 = ((f32[1536,1,128]{2,1,0:T(1,128)}), f32[1536,1,128]{2,1,0:T(1,128)S(1)}, u32[]{:S(2)}, u32[]{:S(2)}) async-start(f32[1536,1,128]{2,1,0:T(1,128)} %bitcast.16), calls=%async_computation.2 | async-start | bytes 1572864 | tf_op jit(solution)/shard_map/all_to_all | solution.py:496
  87.5 0.0 copy-start
  87.6 2.4 %shard_map.190.matrix_ref = f32[960,320]{1,0:T(8,128)S(1)} custom-call(f32[3,8,8]{2,1,0:T(8,128)S(1)} %pad.4.jac_ref, bf16[320,8]{1,0:T(8,128)(2,1)S(1)} %copy-done.10, bf16[320,64]{1,0:T(8,128)(2,1)S(1)} %copy-done.9, f32[3,320,320]{2,1,0:T(8,128)S(1)} %copy-done.2, f32[5,64,64]{2,1,0:T(8,128)S(1)} %copy-done.7), custom_call_target="tpu_custom_call" | custom-call | flops 100000000 | bytes 1048576 | tf_op jit(solution)/shard_map/pallas_call | solution.py:482
  89.9 4.6 %shard_map.191.fluid_ref = f32[320,1152]{1,0:T(8,128)S(1)} custom-call(s32[3]{0:T(128)S(1)} %pad_add_fusion.where_ref, f32[320,1024]{1,0:T(8,128)S(1)} %bitcast.26, f32[960,320]{1,0:T(8,128)S(1)} %shard_map.190.matrix_ref, f32[8,384]{1,0:T(8,128)S(1)} %collective-permute-done.1.before_ref, f32[8,384]{1,0:T(8,128)S(1)} %collective-permute-done.2.after_ref), custom_call_target="tpu_custom_call" | custom-call | flops 2000000000 | bytes 1048576 | tf_op jit(solution)/shard_map/pallas_call | solution.py:482
  94.5 6.2 %shard_map.192 = (f32[320,1024]{1,0:T(8,128)}, f32[16,128]{1,0:T(8,128)S(1)}) custom-call(s32[3]{0:T(128)S(1)} %pad_add_fusion.where_ref, f32[320,1152]{1,0:T(8,128)S(1)} %shard_map.191.fluid_ref, f32[256,256]{1,0:T(8,128)S(1)} %get-tuple-element.26.surface_ref, f32[16,128]{1,0:T(8,128)S(1)} %get-tuple-element.27.trace_ref, ...), custom_call_target="tpu_custom_call" | custom-call | flops 2000000000 | bytes 1048576 | tf_op jit(solution)/shard_map/pallas_call | solution.py:482
  100.7 13.8 %all-to-all-done.2 = f32[1536,1,128]{2,1,0:T(1,128)S(1)} async-done(((f32[1536,1,128]{2,1,0:T(1,128)}), f32[1536,1,128]{2,1,0:T(1,128)S(1)}, u32[]{:S(2)}, u32[]{:S(2)}) %all-to-all-start.2) | async-done | bytes 786464 | tf_op jit(solution)/shard_map/all_to_all | solution.py:496
  114.5 2.7 %shard_map.193 = (f32[512,128]{1,0:T(8,128)}, f32[320,1024]{1,0:T(8,128)}) custom-call(s32[3]{0:T(128)S(1)} %pad_add_fusion.where_ref, f32[1536,128]{1,0:T(8,128)S(1)} %bitcast.27, f32[512,128]{1,0:T(8,128)S(1)} %copy-done.1, f32[16,128]{1,0:T(8,128)S(1)} %get-tuple-element.28.later_ref, ...), custom_call_target="tpu_custom_call", output_to_operand_aliasing={{1}: (7, {})} | custom-call | tf_op jit(solution)/shard_map/pallas_call | solution.py:582
  (34 shorter events, 0.1 us)
Async XLA Ops:
  0.6 12.3 %copy-start.13 = (s32[128,1]{0,1:T(1,128)S(1)}, s32[128,1]{0,1:T(1,128)}, u32[]{:S(2)}) copy-start(s32[128,1]{0,1:T(1,128)} %param.22) | copy-start | bytes 1540
  0.6 13.0 %copy-start.19 = (s32[128]{0:T(128)S(1)}, s32[128]{0:T(128)}, u32[]{:S(2)}) copy-start(s32[128]{0:T(128)} %param.21) | copy-start | bytes 1540
  0.7 12.3 %copy-start.18 = (f32[3,5,5]{2,0,1:T(4,128)S(1)}, f32[3,5,5]{2,0,1:T(4,128)}, u32[]{:S(2)}) copy-start(f32[3,5,5]{2,0,1:T(4,128)} %param.19) | copy-start | bytes 904
  0.7 16.9 %collective-permute-start = (f32[512,128]{1,0:T(8,128)}, f32[512,128]{1,0:T(8,128)S(1)}, u32[]{:S(2)}, u32[]{:S(2)}) collective-permute-start(f32[512,128]{1,0:T(8,128)} %bitcast.33), channel_id=1, source_target_pairs={{0,128},{128,0},{1,129},{129,1},{2,130},{130,2},{3,131},{131,3},{4... | collective-permute-start | bytes 786440 | tf_op jit(solution)/shard_map/ppermute | solution.py:509
  6.3 11.3 %copy-start.1 = (f32[512,128]{1,0:T(8,128)S(1)}, f32[512,128]{1,0:T(8,128)}, u32[]{:S(2)}) copy-start(f32[512,128]{1,0:T(8,128)} %constant.81.clone.sine_ref) | copy-start | bytes 786436
  6.3 11.3 %copy-start.5 = (f32[256,2,128]{2,1,0:T(2,128)S(1)}, f32[256,2,128]{2,1,0:T(2,128)}, u32[]{:S(2)}) copy-start(f32[256,2,128]{2,1,0:T(2,128)} %param.20) | copy-start | bytes 786436
  6.3 11.3 %copy-start.14 = (s32[128]{0:T(128)S(1)}, s32[128]{0:T(128)}, u32[]{:S(2)}) copy-start(s32[128]{0:T(128)} %param.23) | copy-start | bytes 1540
  6.3 11.2 %collective-permute-start.1 = (f32[8,384]{1,0:T(8,128)}, f32[8,384]{1,0:T(8,128)S(1)}, u32[]{:S(2)}, u32[]{:S(2)}) collective-permute-start(f32[8,384]{1,0:T(8,128)} %get-tuple-element.19), channel_id=1, source_target_pairs={{0,1},{1,2},{2,3},{3,4},{4,5},{5,6},{6,7},{7,8},{8,9},{9,10},{10,1... | collective-permute-start | bytes 36872 | tf_op jit(solution)/shard_map/ppermute | solution.py:522
  10.8 6.7 %collective-permute-start.2 = (f32[8,384]{1,0:T(8,128)}, f32[8,384]{1,0:T(8,128)S(1)}, u32[]{:S(2)}, u32[]{:S(2)}) collective-permute-start(f32[8,384]{1,0:T(8,128)} %get-tuple-element.20), channel_id=1, source_target_pairs={{1,0},{2,1},{3,2},{4,3},{5,4},{6,5},{7,6},{8,7},{9,8},{10,9},{11,1... | collective-permute-start | bytes 36872 | tf_op jit(solution)/shard_map/ppermute | solution.py:523
  13.7 35.2 %copy-start.3 = (f32[256,1]{1,0:T(8,128)S(1)}, f32[256,1]{1,0:T(8,128)}, u32[]{:S(2)}) copy-start(f32[256,1]{1,0:T(8,128)} %constant.88.clone.rate_col_ref) | copy-start | bytes 3076
  13.7 35.2 %copy-start.12 = (f32[8,256]{1,0:T(8,128)S(1)}, f32[8,256]{1,0:T(8,128)}, u32[]{:S(2)}) copy-start(f32[8,256]{1,0:T(8,128)} %constant.89.clone.row_ref) | copy-start | bytes 24580
  13.7 35.2 %copy-start.15 = (f32[1,256]{1,0:T(1,128)S(1)}, f32[1,256]{1,0:T(1,128)}, u32[]{:S(2)}) copy-start(f32[1,256]{1,0:T(1,128)} %constant.87.clone.rate_row_ref) | copy-start | bytes 3076
  13.7 35.1 %copy-start.16 = (f32[256]{0:T(256)S(1)}, f32[256]{0:T(256)}, u32[]{:S(2)}) copy-start(f32[256]{0:T(256)} %constant.86.clone.rate_ref) | copy-start | bytes 3076
  17.6 1.0 copy-start.6
  18.5 0.9 copy-start.11
  19.4 58.0 %copy-start.4 = (f32[256,256]{1,0:T(8,128)S(1)}, f32[256,256]{1,0:T(8,128)}, u32[]{:S(2)}) copy-start(f32[256,256]{1,0:T(8,128)} %constant.90.clone.response_ref) | copy-start | bytes 786436
  19.4 58.0 %copy-start.8 = (f32[256,1]{1,0:T(8,128)S(1)}, f32[256,1]{1,0:T(8,128)}, u32[]{:S(2)}) copy-start(f32[256,1]{1,0:T(8,128)} %constant.91.clone.column_ref) | copy-start | bytes 3076
  73.8 3.6 %collective-permute-start.3 = (f32[640,128]{1,0:T(8,128)S(1)}, f32[640,128]{1,0:T(8,128)S(1)}, u32[]{:S(2)}, u32[]{:S(2)}) collective-permute-start(f32[640,128]{1,0:T(8,128)S(1)} %bitcast.29), channel_id=1, source_target_pairs={{0,1},{1,0},{2,3},{3,2},{4,5},{5,4},{6,7},{7,6},{8,9},{9,8},{10,11... | collective-permute-start | bytes 983048 | tf_op jit(solution)/shard_map/ppermute | solution.py:565
  77.4 10.1 %copy-start.17 = (f32[3,5,5]{2,1,0:T(8,128)S(1)}, f32[3,5,5]{2,1,0:T(8,128)}, u32[]{:S(2)}) copy-start(f32[3,5,5]{2,1,0:T(8,128)} %copy.27.jac_ref) | copy-start | bytes 904
  77.4 10.1 %copy-start.2 = (f32[3,320,320]{2,1,0:T(8,128)S(1)}, f32[3,320,320]{2,1,0:T(8,128)}, u32[]{:S(2)}) copy-start(f32[3,320,320]{2,1,0:T(8,128)} %constant.84.clone.fixed_ref) | copy-start | bytes 3686404
  77.4 10.1 %copy-start.7 = (f32[5,64,64]{2,1,0:T(8,128)S(1)}, f32[5,64,64]{2,1,0:T(8,128)}, u32[]{:S(2)}) copy-start(f32[5,64,64]{2,1,0:T(8,128)} %constant.85.clone.operators_ref) | copy-start | bytes 245764
  77.4 10.1 %copy-start.9 = (bf16[320,64]{1,0:T(8,128)(2,1)S(1)}, bf16[320,64]{1,0:T(8,128)(2,1)}, u32[]{:S(2)}) copy-start(bf16[320,64]{1,0:T(8,128)(2,1)} %constant.83.clone.tile_ref) | copy-start | bytes 122884
  77.5 10.1 %copy-start.10 = (bf16[320,8]{1,0:T(8,128)(2,1)S(1)}, bf16[320,8]{1,0:T(8,128)(2,1)}, u32[]{:S(2)}) copy-start(bf16[320,8]{1,0:T(8,128)(2,1)} %constant.82.clone.field_ref) | copy-start | bytes 15364
  82.1 32.4 %all-to-all-start.2 = ((f32[1536,1,128]{2,1,0:T(1,128)}), f32[1536,1,128]{2,1,0:T(1,128)S(1)}, u32[]{:S(2)}, u32[]{:S(2)}) async-start(f32[1536,1,128]{2,1,0:T(1,128)} %bitcast.16), calls=%async_computation.2 | async-start | bytes 1572864 | tf_op jit(solution)/shard_map/all_to_all | solution.py:496
  87.5 2.4 %copy-start = (f32[5,64,1024]{2,1,0:T(8,128)S(1)}, f32[5,64,1024]{2,1,0:T(8,128)}, u32[]{:S(2)}) copy-start(f32[5,64,1024]{2,1,0:T(8,128)} %param.18) | copy-start | bytes 3932164

commit v3 on v2

--- a/solution.py
+++ b/solution.py
@@ -170,94 +170,90 @@
     return jnp.concatenate([sine_rows(sine_ref, k, HALF, 2) for k in range(2)], axis=0)
 
 
-def edges_kernel(left_ref, right_ref, elem_ref, owner_ref, patch_ref, first_ref, last_ref, *, count):
-    lane = iota((1, 384), 1)
-    gap = jnp.zeros((1, 64), F32)
-    for ref, block, at, out, element in (
-        (left_ref, left_ref[...], (0, 1), first_ref, 0),
-        (right_ref, right_ref[...], (HALF - 1, HALF - 2), last_ref, count - 1),
-    ):
-        turned = block.T
-        met = elem_ref[...] == element
-        owner = jnp.sum(jnp.where(met, owner_ref[...] + 1, 0).astype(F32), axis=1, keepdims=True)
-        patch = jnp.sum(jnp.where(met, patch_ref[...], 0).astype(F32), axis=1, keepdims=True)
-        slot = jnp.where(lane == 0, owner, jnp.where(lane == 1, patch, 0.0))
-        out[0:1] = jnp.concatenate([turned[at[0] : at[0] + 1], gap], axis=1)
-        out[1:2] = jnp.concatenate([turned[at[1] : at[1] + 1], gap], axis=1)
-        out[2:3] = slot
-        out[3:8] = jnp.zeros((5, 384), F32)
-
-
-def walls_kernel(jac_ref, fluid_ref, table_ref, out_ref, matrix_ref):
-    @pl.when(pl.program_id(0) == 0)
-    def _():
-        field = iota((1, 320), 1) // 64
-        coefficients = []
-        for d in range(3):
-            row = jnp.zeros((1, 320), F32)
-            for f in range(5):
-                row = jnp.where(field == f, jac_ref[d, 4, f] - jac_ref[d, 0, f], row)
-            coefficients.append(row)
-        own = table_ref[0]
-        for d in range(3):
-            own = own + coefficients[d] * table_ref[1 + d]
-        matrix_ref[0:16] = own
-        matrix_ref[16:32] = table_ref[4] + coefficients[0] * table_ref[5]
-        matrix_ref[32:48] = table_ref[6] + coefficients[0] * table_ref[7]
-
-    out_ref[0:48] = dot3(matrix_ref[...], fluid_ref[...])
-    out_ref[48:64] = fluid_ref[256:272] - fluid_ref[0:16]
-
-
-def matrices_kernel(jac_ref, field_ref, tile_ref, fixed_ref, operators_ref, out_ref):
-    field, tile = field_ref[...], tile_ref[...]
-
-    def spread(d):
-        return dot_hot(hot_dot(field, jac_ref[d]), field, NT)
-
-    def tiled(d):
-        return dot_hot(hot_dot(tile, operators_ref[d]), tile, NT)
-
-    by_x = spread(0)
-    own = by_x * tiled(0) + spread(1) * tiled(1) + spread(2) * tiled(2)
-    out_ref[0:320] = fixed_ref[0] + own
-    out_ref[320:640] = fixed_ref[1] + by_x * tiled(3)
-    out_ref[640:960] = fixed_ref[2] + by_x * tiled(4)
-
-
-def first_kernel(
-    where_ref, solid_ref, far_ref, wall_ref, matrix_ref, before_ref, after_ref, elem_ref,
-    owner_col_ref, owner_ref, patch_ref, sine_ref, out_ref, trace_ref, surface_ref
+def column_of(row):
+    return jnp.broadcast_to(row.astype(F32), (8, row.shape[1])).T[:, 0:1].astype(jnp.int32)
+
+
+def near_kernel(
+    where_ref, jac_hbm, fluid_hbm, solid_hbm, sine_hbm, table_ref, elem_ref, owner_ref, patch_ref,
+    out_ref, trace_ref, surface_ref, first_ref, last_ref, matrix_ref, far_table_ref,
+    jac_ref, fluid_ref, solid_ref, sine_ref, sems
 ):
     group = where_ref[0]
+    count = fluid_ref.shape[1]
+    copies = [
+        pltpu.make_async_copy(jac_hbm, jac_ref, sems.at[0]),
+        pltpu.make_async_copy(solid_hbm, solid_ref, sems.at[1]),
+        pltpu.make_async_copy(sine_hbm, sine_ref, sems.at[2]),
+    ]
+    for i in range(5):
+        at = pl.ds(64 * i, 64)
+        copies.append(pltpu.make_async_copy(fluid_hbm.at[at, :], fluid_ref.at[at, :], sems.at[3 + i]))
+    for copy in copies:
+        copy.start()
+    for copy in copies[:3]:
+        copy.wait()
+
     near, far = [
-        split(sine_ref[pl.ds(pl.multiple_of(half * N + group * HALF, HALF), HALF), :])
+        sine_ref[pl.ds(pl.multiple_of(half * N + group * HALF, HALF), HALF), :]
         for half in (group, 1 - group)
     ]
+    far_table_ref[...] = far
+    near = split(near)
     for i in range(2):
-        modes = dot3(near, rows(solid_ref, i, N, 2), NT) + dot3(far, rows(far_ref, i, N, 2), NT)
+        modes = dot3(near, rows(solid_ref, i, N, 2), NT)
         for h in range(2):
             out_ref[pl.ds(2 * i + h, HALF, 5), :] = modes[:, h * HALF : (h + 1) * HALF]
     surface_ref[...] = solid_ref[0:2]
 
-    def halo(part, ref):
-        return jnp.sum(matrix_ref[16 * part : 16 * part + 16] * ref[0:1, 0:320], axis=1, keepdims=True)
-
-    wall0, own = wall_ref[48:64], wall_ref[0:16]
-    count = own.shape[1]
-    lane = iota(own.shape, 1)
-    following = pltpu.roll(wall_ref[16:32], count - 1, 1)
-    preceding = pltpu.roll(wall_ref[32:48], 1, 1)
-    later = own + jnp.where(lane == count - 1, halo(1, after_ref), following)
-    later = later + jnp.where(lane == 0, halo(2, before_ref), preceding)
-    elem_hot = hot_of(elem_ref[...] == iota((HALF, count), 1))
+    field = iota((1, 320), 1) // 64
+    coefficients = []
+    for d in range(3):
+        change = jac_ref[d, 4:5, :] - jac_ref[d, 0:1, :]
+        row = jnp.zeros((1, 320), F32)
+        for f in range(5):
+            row = jnp.where(field == f, change[:, f : f + 1], row)
+        coefficients.append(row)
+    own = table_ref[0]
+    for d in range(3):
+        own = own + coefficients[d] * table_ref[1 + d]
+    matrix_ref[0:16] = own
+    matrix_ref[16:32] = table_ref[4] + coefficients[0] * table_ref[5]
+    matrix_ref[32:48] = table_ref[6] + coefficients[0] * table_ref[7]
+
+    owner, patch, elem = owner_ref[...], patch_ref[...], elem_ref[...]
+    square = (HALF, HALF)
+    same = (column_of(owner) == owner) & (iota(square, 0) < iota(square, 1))
+    place = jnp.sum(jnp.where(same, 1.0, 0.0), axis=0, keepdims=True)
+    elem_hot = hot_of(column_of(elem) == iota((HALF, count), 1))
+
+    for copy in copies[3:]:
+        copy.wait()
+    lane = iota((1, 384), 1)
+    gap = jnp.zeros((1, 64), F32)
+    for block, at, out, element in (
+        (fluid_ref[:, 0:HALF], (0, 1), first_ref, 0),
+        (fluid_ref[:, count - HALF : count], (HALF - 1, HALF - 2), last_ref, count - 1),
+    ):
+        turned = block.T
+        met = elem == element
+        edge_owner = jnp.sum(jnp.where(met, owner + 1, 0).astype(F32), axis=1, keepdims=True)
+        edge_patch = jnp.sum(jnp.where(met, patch, 0).astype(F32), axis=1, keepdims=True)
+        out[0:1] = jnp.concatenate([turned[at[0] : at[0] + 1], gap], axis=1)
+        out[1:2] = jnp.concatenate([turned[at[1] : at[1] + 1], gap], axis=1)
+        out[2:3] = jnp.where(lane == 0, edge_owner, jnp.where(lane == 1, edge_patch, 0.0))
+        out[3:8] = jnp.zeros((5, 384), F32)
+
+    walls = dot3(matrix_ref[...], fluid_ref[...])
+    wall0 = fluid_ref[256:272] - fluid_ref[0:16]
+    lane = iota(wall0.shape, 1)
+    following = pltpu.roll(walls[16:32], count - 1, 1)
+    preceding = pltpu.roll(walls[32:48], 1, 1)
+    later = walls[0:16] + jnp.where(lane == count - 1, 0.0, following)
+    later = later + jnp.where(lane == 0, 0.0, preceding)
     values = dot_hot(jnp.concatenate([wall0, later - GAIN * wall0], axis=0), elem_hot, NT)
     trace_ref[...] = values[:16]
-    owner = owner_ref[...]
-    square = (HALF, HALF)
-    same = (owner_col_ref[...] == owner) & (iota(square, 0) < iota(square, 1))
-    place = jnp.sum(jnp.where(same, 1.0, 0.0), axis=0, keepdims=True)
-    ids = jnp.broadcast_to((patch_ref[...] + 1).astype(F32), (8, HALF))
+    ids = jnp.broadcast_to((patch + 1).astype(F32), (8, HALF))
     filler = jnp.zeros((24, HALF), F32)
     sent = jnp.concatenate([values, ids, filler], axis=0)
     none = jnp.zeros((64, HALF), F32)
@@ -269,20 +265,63 @@
     out_ref[pl.ds(4, HALF, 5), :] = arranged
 
 
+def far_kernel(far_ref, table_ref, near_ref, out_ref):
+    table = split(table_ref[...])
+    out_ref[pl.ds(4, HALF, 5), :] = rows(near_ref, 4, HALF, 5)
+    for i in range(2):
+        modes = dot3(table, rows(far_ref, i, N, 2), NT)
+        for h in range(2):
+            part = modes[:, h * HALF : (h + 1) * HALF]
+            out_ref[pl.ds(2 * i + h, HALF, 5), :] = rows(near_ref, 2 * i + h, HALF, 5) + part
+
+
+def tables_kernel(
+    where_ref, rate_ref, sine_ref, rate_row_ref, rate_col_ref, order_ref,
+    sine_out, x_out, modes_out, modes_t_out, split_out, decay_out
+):
+    del order_ref
+    by_modes = mode_ordered(sine_ref)
+    for out, table in (
+        (sine_out, split(sine_rows(sine_ref, 0, N, 1))),
+        (x_out, x_ordered(sine_ref)),
+        (modes_out, split(by_modes)),
+        (modes_t_out, split(by_modes.T)),
+    ):
+        out[0], out[1] = table
+    for i in range(2):
+        split_out[2 * i], split_out[2 * i + 1] = split(sine_rows(sine_ref, i, HALF, 2))
+    decay_out[...] = 1.0 / (rate_col_ref[...] + (rate_row_ref[...] + 64.0 * rate_ref[where_ref[2]]))
+
+
+def matrices_kernel(jac_ref, field_ref, tile_ref, fixed_ref, operators_ref, out_ref):
+    field, tile = field_ref[...], tile_ref[...]
+
+    def spread(d):
+        return dot_hot(hot_dot(field, jac_ref[d]), field, NT)
+
+    def tiled(d):
+        return dot_hot(hot_dot(tile, operators_ref[d]), tile, NT)
+
+    by_x = spread(0)
+    own = by_x * tiled(0) + spread(1) * tiled(1) + spread(2) * tiled(2)
+    out_ref[0:320] = fixed_ref[0] + own
+    out_ref[320:640] = fixed_ref[1] + by_x * tiled(3)
+    out_ref[640:960] = fixed_ref[2] + by_x * tiled(4)
+
+
 def modes_kernel(
-    where_ref, rate_ref, got_ref, surface_ref, sine_ref, rate_row_ref, rate_col_ref, row_ref,
-    modes_ref, out_ref
+    where_ref, got_ref, surface_ref, sine_ref, split_ref, by_modes_ref, decay_ref, row_ref,
+    matrix_ref, before_ref, after_ref, elem_ref, owner_ref, patch_ref, modes_ref, out_ref, *, count
 ):
-    group, me = where_ref[0], where_ref[2]
-    sine = split(sine_rows(sine_ref, 0, N, 1))
+    group = where_ref[0]
+    sine = sine_ref[0], sine_ref[1]
     modes = 0.0
     for i in range(2):
         part = jnp.concatenate([rows(got_ref, 2 * i + h, HALF, 5) for h in range(2)], axis=1)
         by_z = dot3(sine, part, NT)
-        modes = modes + dot3(by_z, sine_rows(sine_ref, i, HALF, 2))
+        modes = modes + dot3(by_z, (split_ref[2 * i], split_ref[2 * i + 1]))
     modes_ref[...] = modes
-    once = modes / (rate_col_ref[...] + (rate_row_ref[...] + 64.0 * rate_ref[me]))
-    surface_row = dot3(row_ref[...], once)[0:1]
+    surface_row = dot3(row_ref[...], decay_ref[...] * modes)[0:1]
 
     fluid = rows(got_ref, 4, HALF, 5)
     square = (HALF, HALF)
@@ -308,11 +347,33 @@
                     )
     heat = [sums[0][xl] - counts[xl] * surface_ref[xl : xl + 1, :] for xl in range(2)]
     tail = jnp.where(lane < 16, count_lanes, 0.0)
+    edge_rows = []
+    for t, (part, ref, element) in enumerate(((2, before_ref, 0), (1, after_ref, count - 1))):
+        met = elem_ref[...] == element
+        owner, patch = [
+            jnp.sum(jnp.where(met, value, 0).astype(F32), axis=1, keepdims=True).astype(jnp.int32)
+            for value in (owner_ref[...] + 1, patch_ref[...])
+        ]
+        x_of_slot = patch // 8 * HALF + (owner - 1) % 2 * 64 + (owner - 1) // 2
+        tail = jnp.where(lane == 40 + t, jnp.where(owner > 0, x_of_slot + 1, 0).astype(F32), tail)
+        tables = matrix_ref[16 * part : 16 * part + 16]
+        column = jnp.sum(tables * ref[0:1, 0:320], axis=1, keepdims=True)
+        node, lane16 = iota((16, HALF), 0), iota((16, HALF), 1)
+        used = (lane16 % 16 == node) & (lane16 // 16 == patch % 8)
+        edge_rows.append(jnp.sum(jnp.where(used, column, 0.0), axis=0, keepdims=True))
     for k in range(2):
-        by_modes = split(sine_ref[pl.ds(group * N + k, HALF, 2), :])
+        by_modes = []
+        for part in range(2):
+            table = by_modes_ref[part, k * HALF : (k + 1) * HALF, :].astype(F32)
+            own = jnp.where(group == 0, table[:, :HALF], table[:, HALF:])
+            by_modes.append(own.astype(BF16))
+        by_modes = tuple(by_modes)
         for xl in range(2):
             column = dot3(by_modes, jnp.broadcast_to(sums[1][xl], (8, HALF)), NT)[:, 0:1]
             tail = jnp.where(lane == 16 + 2 * k + xl, column, tail)
+        for t in range(2):
+            column = dot3(by_modes, jnp.broadcast_to(edge_rows[t], (8, HALF)), NT)[:, 0:1]
+            tail = jnp.where(lane == 32 + 2 * t + k, column, tail)
     shared = [surface_row[:, :HALF], surface_row[:, HALF:], heat[0], heat[1]]
     for r in range(4):
         out_ref[pl.ds(r, HALF, 5), :] = jnp.broadcast_to(shared[r], square)
@@ -320,8 +381,8 @@
 
 
 def solve_kernel(
-    where_ref, rate_ref, got_ref, other_ref, modes_ref, response_ref, sine_ref, rate_row_ref,
-    rate_col_ref, row_ref, column_ref, surface_ref, out_ref, heat_ref
+    where_ref, got_ref, other_ref, modes_ref, response_ref, sine_ref, pair_ref, x_ref, by_modes_ref,
+    from_modes_ref, split_ref, decay_ref, row_ref, column_ref, surface_ref, out_ref, heat_ref
 ):
     core, me = where_ref[1], where_ref[2]
     first = jnp.full((HALF, HALF), core, jnp.int32) == 0
@@ -333,9 +394,11 @@
     def block(g, r):
         return jnp.concatenate([ordered[r][k][g * 64 : (g + 1) * 64] for k in range(2)], axis=0)
 
-    by_modes = mode_ordered(sine_ref)
-    halves = [split(by_modes[:, g * HALF : (g + 1) * HALF]) for g in range(2)]
-    by_x = x_ordered(sine_ref)
+    halves = [
+        tuple(by_modes_ref[part, :, g * HALF : (g + 1) * HALF] for part in range(2))
+        for g in range(2)
+    ]
+    by_x = x_ref[0], x_ref[1]
     heat_modes = 0.0
     for xl in range(2):
         by_y = 0.0
@@ -347,7 +410,7 @@
     given = jnp.concatenate(
         [jnp.concatenate([ordered[h][k] for h in range(2)], axis=1) for k in range(2)], axis=0
     )
-    surface = dot3(split(by_modes.T), given + response_ref[...] * heat_modes)
+    surface = dot3((from_modes_ref[0], from_modes_ref[1]), given + response_ref[...] * heat_modes)
     surface = dot3(surface, by_x, NT)
     surface_ref[...] = surface
     square = (HALF, HALF)
@@ -368,22 +431,29 @@
     later = jnp.concatenate(
         [hot_dot(hot_of(lane8 == 16 + 2 * core + xl), tail_sum, NT) for xl in range(2)], axis=1
     )
+    wide = iota((HALF, N), 1)
+    for k in range(2):
+        tail = ordered[4][k]
+        for t in range(2):
+            value = jnp.where(first[:, 0:1], tail[:, 32 + 2 * t : 33 + 2 * t], tail[:, 33 + 2 * t : 34 + 2 * t])
+            met = tail[:, 40 + t : 41 + t].astype(jnp.int32) - 1 == wide
+            later = later + jnp.sum(jnp.where(met, value, 0.0), axis=0, keepdims=True)
     heat1 = dot3(later - 0.7 * reduced, by_x)[0:1]
     heat0 = heat_ref[pl.ds(core * HALF + me // 2, 1), :]
-    decay = 1.0 / (rate_col_ref[...] + (rate_row_ref[...] + 64.0 * rate_ref[me]))
+    decay = decay_ref[...]
     column = column_ref[...]
     final = decay * (decay * (modes_ref[...] + column * heat0) + column * heat1)
     final_row = dot3(row_ref[...], final)[0:1]
     final = split(final)
-    sine = split(sine_rows(sine_ref, 0, N, 1))
+    sine = pair_ref[0], pair_ref[1]
     for xl in range(2):
-        back = dot3(dot3(sine_rows(sine_ref, xl, HALF, 2), final, NT), sine)
+        back = dot3(dot3((split_ref[2 * xl], split_ref[2 * xl + 1]), final, NT), sine)
         for g in range(2):
             for h in range(2):
-                out_ref[pl.ds(g * 768 + 2 * xl + h, HALF, 6), :] = back[:, h * HALF : (h + 1) * HALF]
-    for h in range(2):
-        out_ref[pl.ds(4 + h, N, 6), :] = jnp.broadcast_to(
-            final_row[:, h * HALF : (h + 1) * HALF], (N, HALF)
+                out_ref[pl.ds(g * 640 + 2 * xl + h, HALF, 5), :] = back[:, h * HALF : (h + 1) * HALF]
+    for k in range(2):
+        out_ref[pl.ds(4 + 5 * k, HALF, 10), :] = jnp.broadcast_to(
+            final_row[:, k * HALF : (k + 1) * HALF], (HALF, HALF)
         )
 
 
@@ -430,13 +500,13 @@
 
 def second_kernel(
     where_ref, fluid_ref, surface_ref, trace_ref, matrix_ref, before_ref, after_ref, elem_ref,
-    owner_ref, patch_ref, out_ref, later_ref
+    owner_ref, patch_ref, sine_ref, out_ref, later_ref, slots_ref
 ):
     group, me = where_ref[0], where_ref[2]
     width = fluid_ref.shape[1]
     count = width - HALF
     own_surface = surface_ref[pl.ds(pl.multiple_of(group * HALF, HALF), HALF), :]
-    elem_hot = hot_of(elem_ref[...] == iota((HALF, count), 1))
+    elem_hot = hot_of(column_of(elem_ref[...]) == iota((HALF, count), 1))
     met = folded(met_values(own_surface, owner_ref[...], patch_ref[...]))
     source = GAIN * dot_hot(met - trace_ref[...], elem_hot)
     square = (16, HALF)
@@ -452,27 +522,34 @@
         value = GAIN * (value - (column[256:272, 0:1] - column[0:16, 0:1]))
         used = (iota(square, 1) == at) & (owner >= 0)
         edge = jnp.where(used, value, edge)
+    slot_hot = hot_of(iota((N, HALF), 0) == 2 * owner_ref[...] + patch_ref[...] // 8)
+    slots_ref[...] = dot_hot(sine_rows(sine_ref, 0, N, 1), slot_hot)
     walls = fluid_ref[256:272] + jnp.concatenate([source, edge], axis=1)
     later_ref[...] = dot_hot(walls[:, :count] - fluid_ref[0:16, :count], elem_hot, NT)
     extended = jnp.concatenate([fluid_ref[0:256], walls, fluid_ref[272:320]], axis=0)
     out_ref[...] = stepped(extended, matrix_ref)[:, :count]
 
 
-def last_kernel(
-    where_ref, got_ref, sine_ref, later_ref, elem_ref, owner_ref, patch_ref, fluid_ref,
-    solid_ref, out_ref
-):
-    group = where_ref[0]
-    by_y = split(sine_ref[pl.ds(pl.multiple_of(group * N, N), N), :])
+def solid_kernel(where_ref, got_ref, sine_ref, solid_ref):
+    by_y = split(sine_ref[pl.ds(pl.multiple_of(where_ref[0] * N, N), N), :])
     for xl in range(2):
         for h in range(2):
-            part = rows(got_ref, 2 * xl + h, N, 6)
+            part = rows(got_ref, 2 * xl + h, N, 5)
             solid_ref[pl.ds(h * N + xl, HALF, 2), :] = dot3(part, by_y, TN)
-    given = jnp.concatenate([rows(got_ref, 4 + h, N, 6) for h in range(2)], axis=1)
+
+
+def last_kernel(
+    where_ref, mine_ref, other_ref, sine_ref, slots_ref, later_ref, elem_ref, patch_ref, fluid_ref,
+    out_ref
+):
+    group, core = where_ref[0], where_ref[1]
+    first = jnp.full((N, HALF), core, jnp.int32) == 0
+    mine, other = mine_ref[...], other_ref[...]
+    given = jnp.concatenate([jnp.where(first, mine, other), jnp.where(first, other, mine)], axis=1)
     own_rows = sine_rows(sine_ref, pl.multiple_of(group * HALF, HALF), HALF, 1)
-    surface = dot3(dot3(own_rows, given), x_ordered(sine_ref), NT)
-    met = folded(met_values(surface, owner_ref[...], patch_ref[...]))
-    elem_hot = hot_of(elem_ref[...] == iota((HALF, fluid_ref.shape[1]), 1))
+    met = dot3(own_rows, dot3(given, slots_ref[...]))
+    met = folded(jnp.where(iota((HALF, HALF), 0) // 16 == patch_ref[...] % 8, met, 0.0))
+    elem_hot = hot_of(column_of(elem_ref[...]) == iota((HALF, fluid_ref.shape[1]), 1))
     out_ref[...] = fluid_ref[...] + GAIN * dot_hot(met - later_ref[...], elem_hot)
 
 
@@ -481,7 +558,9 @@
     given = [pl.BlockSpec(memory_space=pltpu.SMEM)] * scalars + [whole] * (len(args) - scalars)
     return pl.pallas_call(
         kernel,
-        out_shape=[jax.ShapeDtypeStruct(shape, F32) for shape in outs],
+        out_shape=[
+            jax.ShapeDtypeStruct(*(out if isinstance(out[0], tuple) else (out, F32))) for out in outs
+        ],
         in_specs=specs or given,
         out_specs=out_specs or [whole] * len(outs),
         scratch_shapes=list(scratch),
@@ -502,46 +581,36 @@
     fluid0 = fluid_state.reshape(320, -1)
     count = fluid0.shape[1]
     solid = solid_temp.reshape(2 * N, HALF)
-    elem = iface_elem[:, None]
-    owner, patch = iface_owner.reshape(1, HALF), iface_patch[None, :]
+    elem, owner, patch = iface_elem[None, :], iface_owner.reshape(1, HALF), iface_patch[None, :]
     smem = pl.BlockSpec(memory_space=pltpu.SMEM)
+    vmem = pl.BlockSpec(memory_space=pltpu.VMEM)
+    anywhere = pl.BlockSpec(memory_space=pl.ANY)
 
     far = lax.ppermute(solid, "g", [(0, 1), (1, 0)])
-    row_spec = pl.BlockSpec((1, HALF), lambda i: (0, 0))
-    first, last = pl.pallas_call(
-        functools.partial(edges_kernel, count=count),
-        grid=(1,),
-        out_shape=[jax.ShapeDtypeStruct((8, 384), F32)] * 2,
-        in_specs=[
-            pl.BlockSpec((320, HALF), lambda i: (0, 0)),
-            pl.BlockSpec((320, HALF), lambda i: (0, count // HALF - 1)),
-        ]
-        + [row_spec] * 3,
-        out_specs=[pl.BlockSpec((8, 384), lambda i: (0, 0))] * 2,
-    )(fluid0, fluid0, iface_elem[None, :], owner, patch)
+    near, trace0, surface0, first, last, wall_matrix, far_table = call(
+        near_kernel,
+        [(5 * HALF, HALF), (16, HALF), (2, HALF), (8, 384), (8, 384), (48, 320), (HALF, HALF)],
+        [where, flux_jacobian, fluid0, solid, Q_HALVES, WALL_TABLES, elem, owner, patch],
+        specs=[smem] + [anywhere] * 4 + [vmem] * 4,
+        scratch=[
+            pltpu.VMEM(flux_jacobian.shape, F32),
+            pltpu.VMEM(fluid0.shape, F32),
+            pltpu.VMEM(solid.shape, F32),
+            pltpu.VMEM(Q_HALVES.shape, F32),
+            pltpu.SemaphoreType.DMA((8,)),
+        ],
+    )
     before = lax.ppermute(last, ALL, [(i, i + 1) for i in range(255)])
     after = lax.ppermute(first, ALL, [(i + 1, i) for i in range(255)])
-    walls, wall_matrix = pl.pallas_call(
-        walls_kernel,
-        grid=(4,),
-        out_shape=[jax.ShapeDtypeStruct((64, count), F32), jax.ShapeDtypeStruct((48, 320), F32)],
-        in_specs=[
-            smem,
-            pl.BlockSpec((320, count // 4), lambda i: (0, i)),
-            pl.BlockSpec((8, 16, 320), lambda i: (0, 0, 0)),
-        ],
-        out_specs=[
-            pl.BlockSpec((64, count // 4), lambda i: (0, i)),
-            pl.BlockSpec((48, 320), lambda i: (0, 0)),
-        ],
-    )(flux_jacobian, fluid0, WALL_TABLES)
-    pay1, trace0, surface0 = call(
-        first_kernel,
-        [(5 * HALF, HALF), (16, HALF), (2, HALF)],
-        [where, solid, far, walls, wall_matrix, before, after, elem, iface_owner, owner, patch, Q_HALVES],
-        scalars=1,
-    )
+    (pay1,) = call(far_kernel, [(5 * HALF, HALF)], [far, far_table, near])
     got1 = exchange(pay1, SUB)
+    tables = call(
+        tables_kernel,
+        [((2, N, N), BF16)] * 4 + [((4, HALF, N), BF16), (N, N)],
+        [where, RATE_LIST, Q_HALVES, RATE_ROW, RATE_COLUMN, surface0],
+        scalars=2,
+    )
+    sine_pair, x_pair, modes_pair, modes_t_pair, split_pair, decay = tables
     jacobian = jnp.pad(flux_jacobian, ((0, 0), (0, 3), (0, 3)))
     (matrix,) = call(
         matrices_kernel,
@@ -556,46 +625,44 @@
         cost=2e9,
     )
     modes, pay2 = call(
-        modes_kernel,
+        functools.partial(modes_kernel, count=count),
         [(N, N), (5 * HALF, HALF)],
-        [where, RATE_LIST, got1, surface0, Q_HALVES, RATE_ROW, RATE_COLUMN, SURFACE_ROW],
-        scalars=2,
+        [where, got1, surface0, sine_pair, split_pair, modes_pair, decay, SURFACE_ROW,
+         wall_matrix, before, after, elem, owner, patch],
+        scalars=1,
     )
     got2 = exchange(pay2, SAME_CORE)
     other = lax.ppermute(got2, "c", [(0, 1), (1, 0)])
     surface1, pay3 = call(
         solve_kernel,
-        [(N, N), (6 * N, HALF)],
-        [where, RATE_LIST, got2, other, modes, RESPONSE, Q_HALVES, RATE_ROW, RATE_COLUMN, SURFACE_ROW,
-         SURFACE_COLUMN],
-        scalars=2,
+        [(N, N), (5 * N, HALF)],
+        [where, got2, other, modes, RESPONSE, Q_HALVES, sine_pair, x_pair, modes_pair, modes_t_pair,
+         split_pair, decay, SURFACE_ROW, SURFACE_COLUMN],
+        scalars=1,
         scratch=[pltpu.VMEM((N, N), F32)],
     )
     got3 = exchange(pay3, ALL)
-    fluid2, trace1 = call(
+    fluid2, trace1, slots = call(
         second_kernel,
-        [(320, count), (16, HALF)],
-        [where, fluid1, surface1, trace0, matrix, before, after, elem, owner, patch],
+        [(320, count), (16, HALF), (N, HALF)],
+        [where, fluid1, surface1, trace0, matrix, before, after, elem, owner, patch, Q_HALVES],
         scalars=1,
         cost=2e9,
     )
-    solid_out, fluid2 = pl.pallas_call(
+    got3, fluid2, trace1, slots = lax.optimization_barrier((got3, fluid2, trace1, slots))
+    mine = got3.reshape(N, 5, 1, HALF)[:, 4].reshape(N, HALF)
+    far_row = lax.ppermute(mine, "c", [(0, 1), (1, 0)])
+    (solid_out,) = call(solid_kernel, [(2 * N, HALF)], [where, got3, Q_HALVES], scalars=1)
+    walls_spec = pl.BlockSpec((16, count), lambda i: (16, 0))
+    (fluid2,) = pl.pallas_call(
         last_kernel,
         grid=(1,),
-        out_shape=[
-            jax.ShapeDtypeStruct((2 * N, HALF), F32),
-            jax.ShapeDtypeStruct((320, count), F32),
-        ],
-        in_specs=[smem]
-        + [pl.BlockSpec(memory_space=pltpu.VMEM)] * 6
-        + [pl.BlockSpec((16, count), lambda i: (16, 0))],
-        out_specs=[
-            pl.BlockSpec((2 * N, HALF), lambda i: (0, 0)),
-            pl.BlockSpec((16, count), lambda i: (16, 0)),
-        ],
-        input_output_aliases={7: 1},
+        out_shape=[jax.ShapeDtypeStruct((320, count), F32)],
+        in_specs=[smem] + [vmem] * 7 + [walls_spec],
+        out_specs=[walls_spec],
+        input_output_aliases={8: 0},
         compiler_params=pltpu.CompilerParams(vmem_limit_bytes=40 << 20),
-    )(where, got3, Q_HALVES, trace1, elem, owner, patch, fluid2)
+    )(where, mine, far_row, Q_HALVES, slots, trace1, elem, patch, fluid2)
     return fluid2.reshape(fluid_state.shape), solid_out.reshape(solid_temp.shape)
 
 

time: 118 us -> 112 us (0.949)
  blocking collectives: 50.6 us -> 22.6 us
  starting transfers between devices: 18.1 us -> 30.7 us
  local copies, waits for them, and re-layouts: 2.75 us -> 11.2 us
  waiting for transfers between devices: 15.1 us -> 18 us
  Pallas kernels: 29.7 us -> 28.3 us
    all_to_all x2 -> x1, blocking collectives: 50.6 us -> 22.6 us  [exchange(): lax.all_to_all(chunks, axes, split_axis=0, concat_axis=0, tiled=True)]
    all_to_all x1 -> x2, starting transfers between devices: 5.41 us -> 18.9 us  [exchange(): lax.all_to_all(chunks, axes, split_axis=0, concat_axis=0, tiled=True)]
    unnamed x42 -> x53, local copies, waits for them, and re-layouts: 2.63 us -> 10.9 us
    ppermute x1, waiting for transfers between devices: 0.01 us -> 2.03 us  [on_device(): after = lax.ppermute(first, ALL, [(i + 1, i) for i in range(255)])]
    pallas_call x9 -> x10, Pallas kernels: 29.7 us -> 28.3 us  [the longest x9 26 us: call(): pl.pallas_call(kernel, out_shape=[jax.ShapeDtypeStruct(*(out if isinstanc...]
    all_to_all x1 -> x2, waiting for transfers between devices: 13.8 us -> 14.7 us  [exchange(): lax.all_to_all(chunks, axes, split_axis=0, concat_axis=0, tiled=True)]
  transfers between devices with their start and end apart: 5 -> 7, of which waited for: 2 -> 4; matrix products, arithmetic and copies ran while one was open for 1% -> 1% of each run, Pallas kernels for 16% -> 16%
where the time goes in v3:
time: 112 us
  starting transfers between devices  30.7 us (27%)
  Pallas kernels  28.3 us (25%)
  blocking collectives  22.6 us (20%)
  waiting for transfers between devices  18 us (16%)
  local copies, waits for them, and re-layouts  11.2 us (10%)
    pallas_call x9, Pallas kernels, call(): pl.pallas_call(kernel, out_shape=[jax.ShapeDtypeStruct(*(out if isinstanc...  26 us
    all_to_all x1, blocking collectives, exchange(): lax.all_to_all(chunks, axes, split_axis=0, concat_axis=0, tiled=True)  22.6 us
    all_to_all x2, starting transfers between devices, exchange(): lax.all_to_all(chunks, axes, split_axis=0, concat_axis=0, tiled=True)  18.9 us
    all_to_all x2, waiting for transfers between devices, exchange(): lax.all_to_all(chunks, axes, split_axis=0, concat_axis=0, tiled=True)  14.7 us
    unnamed x53, local copies, waits for them, and re-layouts  10.9 us
    ppermute x1, starting transfers between devices, on_device(): far = lax.ppermute(solid, 'g', [(0, 1), (1, 0)])  3.83 us
    ppermute x1, starting transfers between devices, on_device(): before = lax.ppermute(last, ALL, [(i, i + 1) for i in range(255)])  3.54 us
    ppermute x1, starting transfers between devices, on_device(): other = lax.ppermute(got2, 'c', [(0, 1), (1, 0)])  2.42 us
  transfers between devices with their start and end apart: 7, of which 4 were waited for; matrix products, arithmetic and copies ran while one was open for 1% of the time, Pallas kernels for 16%

profile of v3, /device:TPU:1, one launch (start us, length us, event | category | flops | bytes accessed | tf_op | source)
XLA Modules:
  0.0 111.7 jit_solution(9612845698080002931)
XLA Ops:
  0.6 3.8 %collective-permute-start = (f32[512,128]{1,0:T(8,128)}, f32[512,128]{1,0:T(8,128)S(1)}, u32[]{:S(2)}, u32[]{:S(2)}) collective-permute-start(f32[512,128]{1,0:T(8,128)} %bitcast.35), channel_id=1, source_target_pairs={{0,128},{128,0},{1,129},{129,1},{2,130},{130,2},{3,131},{131,3},{4... | collective-permute-start | bytes 786440 | tf_op jit(solution)/shard_map/ppermute | solution.py:589
  4.5 0.7 copy.27.jac_hbm
  5.2 0.9 copy-done
  6.2 1.3 %copy-done.3 = f32[5,64,1024]{2,1,0:T(8,128)S(1)} copy-done((f32[5,64,1024]{2,1,0:T(8,128)S(1)}, f32[5,64,1024]{2,1,0:T(8,128)}, u32[]{:S(2)}) %copy-start.3) | copy-done | bytes 1310744
  7.5 0.9 copy-done.5
  8.5 0.9 copy-done.9
  9.4 0.7 copy-done.16
  11.4 2.2 %shard_map.185 = (f32[640,128]{1,0:T(8,128)S(1)}, f32[16,128]{1,0:T(8,128)S(1)}, f32[2,128]{1,0:T(2,128)S(1)}, f32[8,384]{1,0:T(8,128)S(1)}, f32[8,384]{1,0:T(8,...) custom-call(s32[3]{0:T(128)S(1)} %pad_add_fusion.where_ref, f32[3,5,5]{2,1,0:T(8,128)S(1)} %copy.27.jac_hbm, ...), custom_call_target="tpu_custom_call" | custom-call | flops 100000000 | bytes 1048576 | tf_op jit(solution)/shard_map/pallas_call | solution.py:559
  13.7 1.0 shard_map.186
  14.7 13.5 %all-to-all-start = ((f32[640,1,128]{2,1,0:T(1,128)}), f32[640,1,128]{2,1,0:T(1,128)S(1)}, u32[]{:S(2)}, u32[]{:S(2)}) async-start(f32[640,1,128]{2,1,0:T(1,128)} %bitcast.9), calls=%async_computation | async-start | bytes 655360 | tf_op jit(solution)/shard_map/all_to_all | solution.py:575
  28.1 3.5 %collective-permute-start.1 = (f32[8,384]{1,0:T(8,128)S(1)}, f32[8,384]{1,0:T(8,128)S(1)}, u32[]{:S(2)}, u32[]{:S(2)}) collective-permute-start(f32[8,384]{1,0:T(8,128)S(1)} %get-tuple-element.34), channel_id=1, source_target_pairs={{0,1},{1,2},{2,3},{3,4},{4,5},{5,6},{6,7},{7,8},{8,9},{9,10},{10,1... | collective-permute-start | bytes 36872 | tf_op jit(solution)/shard_map/ppermute | solution.py:603
  31.7 1.9 %collective-permute-start.2 = (f32[8,384]{1,0:T(8,128)S(1)}, f32[8,384]{1,0:T(8,128)S(1)}, u32[]{:S(2)}, u32[]{:S(2)}) collective-permute-start(f32[8,384]{1,0:T(8,128)S(1)} %get-tuple-element.35), channel_id=1, source_target_pairs={{1,0},{2,1},{3,2},{4,3},{5,4},{6,5},{7,6},{8,7},{9,8},{10,9},{11,1... | collective-permute-start | bytes 36872 | tf_op jit(solution)/shard_map/ppermute | solution.py:604
  33.7 0.9 shard_map.187
  34.5 0.7 copy-done.7
  35.2 2.0 %collective-permute-done.2.after_ref = f32[8,384]{1,0:T(8,128)S(1)} collective-permute-done((f32[8,384]{1,0:T(8,128)S(1)}, f32[8,384]{1,0:T(8,128)S(1)}, u32[]{:S(2)}, u32[]{:S(2)}) %collective-permute-start.2) | collective-permute-done | bytes 12320 | tf_op jit(solution)/shard_map/ppermute | solution.py:604
  37.3 5.5 %all-to-all-done = f32[640,1,128]{2,1,0:T(1,128)S(1)} async-done(((f32[640,1,128]{2,1,0:T(1,128)}), f32[640,1,128]{2,1,0:T(1,128)S(1)}, u32[]{:S(2)}, u32[]{:S(2)}) %all-to-all-start) | async-done | bytes 327712 | tf_op jit(solution)/shard_map/all_to_all | solution.py:575
  42.8 2.4 %shard_map.188 = (f32[256,256]{1,0:T(8,128)S(1)}, f32[640,128]{1,0:T(8,128)S(1)}) custom-call(s32[3]{0:T(128)S(1)} %pad_add_fusion.where_ref, f32[640,128]{1,0:T(8,128)S(1)} %bitcast.27, f32[2,128]{1,0:T(2,128)S(1)} %get-tuple-element.28.order_ref.surface_ref, bf16[2,256,256]{2,1,0:T(8,128)(2,1)S(1)} %get-tuple-element.29.sine_ref.pair_ref, ...), custom_call_target="tpu_custom_call" | custom-call | flops 100000000 | bytes 1048576 | tf_op jit(solution)/shard_map/pallas_call | solution.py:559
  45.2 22.6 %all_to_all.15 = f32[640,1,128]{2,1,0:T(1,128)S(1)} all-to-all(f32[640,1,128]{2,1,0:T(1,128)S(1)} %bitcast.34), channel_id=1, replica_groups=mesh['g'=2,'yl'=2,'x'=4,'z'=8,'c'=2] {'g','yl','x','z'}, dimensions={0} | all-to-all | bytes 655360 | tf_op jit(solution)/shard_map/all_to_all | solution.py:575
  67.8 2.4 %collective-permute-start.3 = (f32[640,128]{1,0:T(8,128)S(1)}, f32[640,128]{1,0:T(8,128)S(1)}, u32[]{:S(2)}, u32[]{:S(2)}) collective-permute-start(f32[640,128]{1,0:T(8,128)S(1)} %bitcast.30), channel_id=1, source_target_pairs={{0,1},{1,0},{2,3},{3,2},{4,5},{5,4},{6,7},{7,6},{8,9},{9,8},{10,11... | collective-permute-start | bytes 983048 | tf_op jit(solution)/shard_map/ppermute | solution.py:635
  70.2 1.3 %collective-permute-done.3.other_ref = f32[640,128]{1,0:T(8,128)S(1)} collective-permute-done((f32[640,128]{1,0:T(8,128)S(1)}, f32[640,128]{1,0:T(8,128)S(1)}, u32[]{:S(2)}, u32[]{:S(2)}) %collective-permute-start.3) | collective-permute-done | bytes 327712 | tf_op jit(solution)/shard_map/ppermute | solution.py:635
  71.5 0.9 copy-done.12
  72.4 4.6 %shard_map.189 = (f32[256,256]{1,0:T(8,128)S(1)}, f32[1280,128]{1,0:T(8,128)}) custom-call(s32[3]{0:T(128)S(1)} %pad_add_fusion.where_ref, f32[640,128]{1,0:T(8,128)S(1)} %bitcast.31, f32[640,128]{1,0:T(8,128)S(1)} %collective-permute-done.3.other_ref, f32[256,256]{1,0:T(8,128)S(1)} %get-tuple-element.37.modes_ref, f32[256,256]{1,0:T(8,128)S(1)} %copy-done.6, ...), custom_call_target="tpu_custom_call" | custom-call | flops 100000000 | bytes 1048576 | tf_op jit(solution)/shard_map/pallas_call | solution.py:559
  77.0 0.7 copy-done.24
  77.7 5.4 %all-to-all-start.2 = ((f32[1280,1,128]{2,1,0:T(1,128)}), f32[1280,1,128]{2,1,0:T(1,128)S(1)}, u32[]{:S(2)}, u32[]{:S(2)}) async-start(f32[1280,1,128]{2,1,0:T(1,128)} %bitcast.15), calls=%async_computation.2 | async-start | bytes 1310720 | tf_op jit(solution)/shard_map/all_to_all | solution.py:575
  83.1 0.9 copy-done.13
  84.0 0.9 copy-done.14
  84.9 2.3 %shard_map.190.matrix_ref = f32[960,320]{1,0:T(8,128)S(1)} custom-call(f32[3,8,8]{2,1,0:T(8,128)S(1)} %pad.4.jac_ref, bf16[320,8]{1,0:T(8,128)(2,1)S(1)} %copy-done.13, bf16[320,64]{1,0:T(8,128)(2,1)S(1)} %copy-done.14, f32[3,320,320]{2,1,0:T(8,128)S(1)} %copy-done.2, f32[5,64,64]{2,1,0:T(8,128)S(1)} %copy-done.10), custom_call_target="tpu_custom_call" | custom-call | flops 100000000 | bytes 1048576 | tf_op jit(solution)/shard_map/pallas_call | solution.py:559
  87.3 4.6 %shard_map.191.fluid_ref = f32[320,1152]{1,0:T(8,128)S(1)} custom-call(s32[3]{0:T(128)S(1)} %pad_add_fusion.where_ref, f32[320,1024]{1,0:T(8,128)S(1)} %bitcast.29, f32[960,320]{1,0:T(8,128)S(1)} %shard_map.190.matrix_ref, f32[8,384]{1,0:T(8,128)S(1)} %collective-permute-done.1.before_ref, f32[8,384]{1,0:T(8,128)S(1)} %collective-permute-done.2.after_ref), custom_call_target="tpu_custom_call" | custom-call | flops 2000000000 | bytes 1048576 | tf_op jit(solution)/shard_map/pallas_call | solution.py:559
  91.9 6.3 %shard_map.192 = (f32[320,1024]{1,0:T(8,128)}, f32[16,128]{1,0:T(8,128)S(1)}, f32[256,128]{1,0:T(8,128)S(1)}) custom-call(s32[3]{0:T(128)S(1)} %pad_add_fusion.where_ref, f32[320,1152]{1,0:T(8,128)S(1)} %shard_map.191.fluid_ref, f32[256,256]{1,0:T(8,128)S(1)} %copy-done.25, f32[16,128]{1,0:T(8,128)S(1)} %get-tuple-element.42.trace_ref, ...), custom_call_target="tpu_custom_call" | custom-call | flops 2000000000 | bytes 1048576 | tf_op jit(solution)/shard_map/pallas_call | solution.py:559
  98.1 9.2 %all-to-all-done.2 = f32[1280,1,128]{2,1,0:T(1,128)S(1)} async-done(((f32[1280,1,128]{2,1,0:T(1,128)}), f32[1280,1,128]{2,1,0:T(1,128)S(1)}, u32[]{:S(2)}, u32[]{:S(2)}) %all-to-all-start.2) | async-done | bytes 655392 | tf_op jit(solution)/shard_map/all_to_all | solution.py:575
  107.7 1.7 %shard_map.194 = f32[512,128]{1,0:T(8,128)} custom-call(s32[3]{0:T(128)S(1)} %pad_add_fusion.where_ref, f32[1280,128]{1,0:T(8,128)S(1)} %bitcast.26, f32[512,128]{1,0:T(8,128)S(1)} %copy-done.1), custom_call_target="tpu_custom_call" | custom-call | flops 100000000 | bytes 1048576 | tf_op jit(solution)/shard_map/pallas_call | solution.py:559
  109.4 2.3 %shard_map.193 = f32[320,1024]{1,0:T(8,128)} custom-call(s32[3]{0:T(128)S(1)} %pad_add_fusion.where_ref, f32[256,128]{1,0:T(8,128)S(1)} %bitcast.33, f32[256,128]{1,0:T(8,128)S(1)} %collective-permute-done.4.other_ref, f32[512,128]{1,0:T(8,128)S(1)} %copy-done.1, f32[256,128]{1,0:T(8,128)S(1)} %get-tuple-element.47.slots_ref, ...), custom_call_target="tpu_custom_call", output_to_operand_aliasing={{}: (8, {})} | custom-call | tf_op jit(solution)/shard_map/pallas_call | solution.py:657
  (50 shorter events, 1.9 us)
Async XLA Ops:
  0.6 13.0 %collective-permute-start = (f32[512,128]{1,0:T(8,128)}, f32[512,128]{1,0:T(8,128)S(1)}, u32[]{:S(2)}, u32[]{:S(2)}) collective-permute-start(f32[512,128]{1,0:T(8,128)} %bitcast.35), channel_id=1, source_target_pairs={{0,128},{128,0},{1,129},{129,1},{2,130},{130,2},{3,131},{131,3},{4... | collective-permute-start | bytes 786440 | tf_op jit(solution)/shard_map/ppermute | solution.py:589
  5.2 1.0 copy-start
  6.2 1.3 %copy-start.3 = (f32[5,64,1024]{2,1,0:T(8,128)S(1)}, f32[5,64,1024]{2,1,0:T(8,128)}, u32[]{:S(2)}) copy-start(f32[5,64,1024]{2,1,0:T(8,128)} %param.18) | copy-start | bytes 3932164
  7.5 0.9 copy-start.5
  8.5 0.9 copy-start.9
  9.4 0.7 copy-start.16
  10.0 0.7 copy-start.18
  11.4 22.3 %copy-start.1 = (f32[512,128]{1,0:T(8,128)S(1)}, f32[512,128]{1,0:T(8,128)}, u32[]{:S(2)}) copy-start(f32[512,128]{1,0:T(8,128)} %constant.80.clone.sine_hbm.sine_ref) | copy-start | bytes 786436
  11.4 22.3 %copy-start.11 = (f32[256,1]{1,0:T(8,128)S(1)}, f32[256,1]{1,0:T(8,128)}, u32[]{:S(2)}) copy-start(f32[256,1]{1,0:T(8,128)} %constant.84.clone.rate_col_ref) | copy-start | bytes 3076
  11.4 22.3 %copy-start.22 = (f32[256]{0:T(256)S(1)}, f32[256]{0:T(256)}, u32[]{:S(2)}) copy-start(f32[256]{0:T(256)} %constant.82.clone.rate_ref) | copy-start | bytes 3076
  11.4 22.3 %copy-start.23 = (f32[1,256]{1,0:T(1,128)S(1)}, f32[1,256]{1,0:T(1,128)}, u32[]{:S(2)}) copy-start(f32[1,256]{1,0:T(1,128)} %constant.83.clone.rate_row_ref) | copy-start | bytes 3076
  13.6 29.2 %copy-start.15 = (f32[8,256]{1,0:T(8,128)S(1)}, f32[8,256]{1,0:T(8,128)}, u32[]{:S(2)}) copy-start(f32[8,256]{1,0:T(8,128)} %constant.89.clone.row_ref) | copy-start | bytes 24580
  13.6 29.1 %copy-start.17 = (s32[128]{0:T(128)S(1)}, s32[128]{0:T(128)}, u32[]{:S(2)}) copy-start(s32[128]{0:T(128)} %param.21) | copy-start | bytes 1540
  13.6 29.1 %copy-start.19 = (s32[128]{0:T(128)S(1)}, s32[128]{0:T(128)}, u32[]{:S(2)}) copy-start(s32[128]{0:T(128)} %param.23) | copy-start | bytes 1540
  13.7 29.1 %copy-start.21 = (s32[128,1]{0,1:T(1,128)S(1)}, s32[128,1]{0,1:T(1,128)}, u32[]{:S(2)}) copy-start(s32[128,1]{0,1:T(1,128)} %param.22) | copy-start | bytes 1540
  14.7 56.8 %copy-start.6 = (f32[256,256]{1,0:T(8,128)S(1)}, f32[256,256]{1,0:T(8,128)}, u32[]{:S(2)}) copy-start(f32[256,256]{1,0:T(8,128)} %constant.90.clone.response_ref) | copy-start | bytes 786436
  14.7 28.1 %all-to-all-start = ((f32[640,1,128]{2,1,0:T(1,128)}), f32[640,1,128]{2,1,0:T(1,128)S(1)}, u32[]{:S(2)}, u32[]{:S(2)}) async-start(f32[640,1,128]{2,1,0:T(1,128)} %bitcast.9), calls=%async_computation | async-start | bytes 655360 | tf_op jit(solution)/shard_map/all_to_all | solution.py:575
  28.1 7.1 %collective-permute-start.1 = (f32[8,384]{1,0:T(8,128)S(1)}, f32[8,384]{1,0:T(8,128)S(1)}, u32[]{:S(2)}, u32[]{:S(2)}) collective-permute-start(f32[8,384]{1,0:T(8,128)S(1)} %get-tuple-element.34), channel_id=1, source_target_pairs={{0,1},{1,2},{2,3},{3,4},{4,5},{5,6},{6,7},{7,8},{8,9},{9,10},{10,1... | collective-permute-start | bytes 36872 | tf_op jit(solution)/shard_map/ppermute | solution.py:603
  31.7 5.6 %collective-permute-start.2 = (f32[8,384]{1,0:T(8,128)S(1)}, f32[8,384]{1,0:T(8,128)S(1)}, u32[]{:S(2)}, u32[]{:S(2)}) collective-permute-start(f32[8,384]{1,0:T(8,128)S(1)} %get-tuple-element.35), channel_id=1, source_target_pairs={{1,0},{2,1},{3,2},{4,3},{5,4},{6,5},{7,6},{8,7},{9,8},{10,9},{11,1... | collective-permute-start | bytes 36872 | tf_op jit(solution)/shard_map/ppermute | solution.py:604
  34.5 0.7 copy-start.7
  42.8 28.7 %copy-start.8 = (bf16[2,256,256]{2,1,0:T(8,128)(2,1)S(1)}, bf16[2,256,256]{2,1,0:T(8,128)(2,1)}, u32[]{:S(2)}) copy-start(bf16[2,256,256]{2,1,0:T(8,128)(2,1)} %copy-done.7) | copy-start | bytes 786436
  67.8 3.7 %collective-permute-start.3 = (f32[640,128]{1,0:T(8,128)S(1)}, f32[640,128]{1,0:T(8,128)S(1)}, u32[]{:S(2)}, u32[]{:S(2)}) collective-permute-start(f32[640,128]{1,0:T(8,128)S(1)} %bitcast.30), channel_id=1, source_target_pairs={{0,1},{1,0},{2,3},{3,2},{4,5},{5,4},{6,7},{7,6},{8,9},{9,8},{10,11... | collective-permute-start | bytes 983048 | tf_op jit(solution)/shard_map/ppermute | solution.py:635
  71.5 0.9 copy-start.12
  72.4 10.7 %copy-start.2 = (f32[3,320,320]{2,1,0:T(8,128)S(1)}, f32[3,320,320]{2,1,0:T(8,128)}, u32[]{:S(2)}) copy-start(f32[3,320,320]{2,1,0:T(8,128)} %constant.87.clone.fixed_ref) | copy-start | bytes 3686404
  72.4 10.7 %copy-start.10 = (f32[5,64,64]{2,1,0:T(8,128)S(1)}, f32[5,64,64]{2,1,0:T(8,128)}, u32[]{:S(2)}) copy-start(f32[5,64,64]{2,1,0:T(8,128)} %constant.88.clone.operators_ref) | copy-start | bytes 245764
  77.0 0.7 copy-start.24
  77.7 29.6 %all-to-all-start.2 = ((f32[1280,1,128]{2,1,0:T(1,128)}), f32[1280,1,128]{2,1,0:T(1,128)S(1)}, u32[]{:S(2)}, u32[]{:S(2)}) async-start(f32[1280,1,128]{2,1,0:T(1,128)} %bitcast.15), calls=%async_computation.2 | async-start | bytes 1310720 | tf_op jit(solution)/shard_map/all_to_all | solution.py:575
  83.1 0.9 copy-start.13
  84.0 0.9 copy-start.14
  84.9 2.4 %copy-start.4 = (f32[5,64,1024]{2,1,0:T(8,128)S(1)}, f32[5,64,1024]{2,1,0:T(8,128)}, u32[]{:S(2)}) copy-start(f32[5,64,1024]{2,1,0:T(8,128)} %param.18) | copy-start | bytes 3932164
  87.3 4.6 %copy-start.25 = (f32[256,256]{1,0:T(8,128)S(1)}, f32[256,256]{1,0:T(8,128)}, u32[]{:S(2)}) copy-start(f32[256,256]{1,0:T(8,128)} %copy-done.24) | copy-start | bytes 786436
  107.6 1.8 %collective-permute-start.4 = (f32[256,128]{1,0:T(8,128)S(1)}, f32[256,128]{1,0:T(8,128)S(1)}, u32[]{:S(2)}, u32[]{:S(2)}) collective-permute-start(f32[256,128]{1,0:T(8,128)S(1)} %bitcast.32), channel_id=1, source_target_pairs={{0,1},{1,0},{2,3},{3,2},{4,5},{5,4},{6,7},{7,6},{8,9},{9,8},{10,11... | collective-permute-start | bytes 393224 | tf_op jit(solution)/shard_map/ppermute | solution.py:654
  (1 other events, 0.7 us)

commit v4 on v3

--- a/solution.py
+++ b/solution.py
@@ -114,7 +114,6 @@
 RATE_ROW = (1.0 + 64.0 * RATES)[None, :].astype(np.float32)
 RATE_COLUMN = (64.0 * RATES)[:, None].astype(np.float32)
 SURFACE_ROW = np.broadcast_to(Q[:1], (8, N)).copy()
-SURFACE_COLUMN = Q[:, :1].copy()
 FIELD_HOT = np.pad(np.kron(np.eye(5), np.ones((64, 1))), ((0, 0), (0, 3))).astype(ml_dtypes.bfloat16)
 TILE_HOT = np.kron(np.ones((5, 1)), np.eye(64)).astype(ml_dtypes.bfloat16)
 OPERATORS = np.stack([BY_X, BY_Y, BY_Z, NEXT_X, PREV_X])
@@ -175,9 +174,9 @@
 
 
 def near_kernel(
-    where_ref, jac_hbm, fluid_hbm, solid_hbm, sine_hbm, table_ref, elem_ref, owner_ref, patch_ref,
+    where_ref, jac_hbm, fluid_hbm, solid_hbm, sine_hbm, table_hbm, elem_hbm, owner_hbm, patch_hbm,
     out_ref, trace_ref, surface_ref, first_ref, last_ref, matrix_ref, far_table_ref,
-    jac_ref, fluid_ref, solid_ref, sine_ref, sems
+    jac_ref, fluid_ref, solid_ref, sine_ref, table_ref, elem_ref, owner_ref, patch_ref, sems
 ):
     group = where_ref[0]
     count = fluid_ref.shape[1]
@@ -185,13 +184,17 @@
         pltpu.make_async_copy(jac_hbm, jac_ref, sems.at[0]),
         pltpu.make_async_copy(solid_hbm, solid_ref, sems.at[1]),
         pltpu.make_async_copy(sine_hbm, sine_ref, sems.at[2]),
+        pltpu.make_async_copy(table_hbm, table_ref, sems.at[3]),
+        pltpu.make_async_copy(elem_hbm, elem_ref, sems.at[4]),
+        pltpu.make_async_copy(owner_hbm, owner_ref, sems.at[5]),
+        pltpu.make_async_copy(patch_hbm, patch_ref, sems.at[6]),
     ]
     for i in range(5):
         at = pl.ds(64 * i, 64)
-        copies.append(pltpu.make_async_copy(fluid_hbm.at[at, :], fluid_ref.at[at, :], sems.at[3 + i]))
+        copies.append(pltpu.make_async_copy(fluid_hbm.at[at, :], fluid_ref.at[at, :], sems.at[7 + i]))
     for copy in copies:
         copy.start()
-    for copy in copies[:3]:
+    for copy in copies[:7]:
         copy.wait()
 
     near, far = [
@@ -227,7 +230,7 @@
     place = jnp.sum(jnp.where(same, 1.0, 0.0), axis=0, keepdims=True)
     elem_hot = hot_of(column_of(elem) == iota((HALF, count), 1))
 
-    for copy in copies[3:]:
+    for copy in copies[7:]:
         copy.wait()
     lane = iota((1, 384), 1)
     gap = jnp.zeros((1, 64), F32)
@@ -382,7 +385,7 @@
 
 def solve_kernel(
     where_ref, got_ref, other_ref, modes_ref, response_ref, sine_ref, pair_ref, x_ref, by_modes_ref,
-    from_modes_ref, split_ref, decay_ref, row_ref, column_ref, surface_ref, out_ref, heat_ref
+    from_modes_ref, split_ref, decay_ref, row_ref, surface_hbm, out_ref, heat_ref, surface_ref, sem
 ):
     core, me = where_ref[1], where_ref[2]
     first = jnp.full((HALF, HALF), core, jnp.int32) == 0
@@ -413,6 +416,8 @@
     surface = dot3((from_modes_ref[0], from_modes_ref[1]), given + response_ref[...] * heat_modes)
     surface = dot3(surface, by_x, NT)
     surface_ref[...] = surface
+    copy = pltpu.make_async_copy(surface_ref, surface_hbm, sem)
+    copy.start()
     square = (HALF, HALF)
     tails = [block(g, 4) for g in range(2)]
     tail_pairs = [tail.astype(BF16) for tail in tails]
@@ -441,7 +446,7 @@
     heat1 = dot3(later - 0.7 * reduced, by_x)[0:1]
     heat0 = heat_ref[pl.ds(core * HALF + me // 2, 1), :]
     decay = decay_ref[...]
-    column = column_ref[...]
+    column = sine_ref[pl.ds(0, N), 0:1]
     final = decay * (decay * (modes_ref[...] + column * heat0) + column * heat1)
     final_row = dot3(row_ref[...], final)[0:1]
     final = split(final)
@@ -455,6 +460,7 @@
         out_ref[pl.ds(4 + 5 * k, HALF, 10), :] = jnp.broadcast_to(
             final_row[:, k * HALF : (k + 1) * HALF], (HALF, HALF)
         )
+    copy.wait()
 
 
 def met_values(surface, owner, patch):
@@ -500,7 +506,7 @@
 
 def second_kernel(
     where_ref, fluid_ref, surface_ref, trace_ref, matrix_ref, before_ref, after_ref, elem_ref,
-    owner_ref, patch_ref, sine_ref, out_ref, later_ref, slots_ref
+    owner_ref, patch_ref, sine_ref, out_ref, later_ref, slots_ref, walls_ref
 ):
     group, me = where_ref[0], where_ref[2]
     width = fluid_ref.shape[1]
@@ -527,20 +533,28 @@
     walls = fluid_ref[256:272] + jnp.concatenate([source, edge], axis=1)
     later_ref[...] = dot_hot(walls[:, :count] - fluid_ref[0:16, :count], elem_hot, NT)
     extended = jnp.concatenate([fluid_ref[0:256], walls, fluid_ref[272:320]], axis=0)
-    out_ref[...] = stepped(extended, matrix_ref)[:, :count]
-
-
-def solid_kernel(where_ref, got_ref, sine_ref, solid_ref):
+    result = stepped(extended, matrix_ref)[:, :count]
+    out_ref[...] = result
+    walls_ref[...] = result[256:272]
+
+
+def solid_kernel(where_ref, got_ref, sine_ref, solid_hbm, solid_ref, sems):
     by_y = split(sine_ref[pl.ds(pl.multiple_of(where_ref[0] * N, N), N), :])
-    for xl in range(2):
-        for h in range(2):
+    copies = []
+    for h in range(2):
+        for xl in range(2):
             part = rows(got_ref, 2 * xl + h, N, 5)
             solid_ref[pl.ds(h * N + xl, HALF, 2), :] = dot3(part, by_y, TN)
+        at = pl.ds(h * N, N)
+        copies.append(pltpu.make_async_copy(solid_ref.at[at, :], solid_hbm.at[at, :], sems.at[h]))
+        copies[h].start()
+    for copy in copies:
+        copy.wait()
 
 
 def last_kernel(
-    where_ref, mine_ref, other_ref, sine_ref, slots_ref, later_ref, elem_ref, patch_ref, fluid_ref,
-    out_ref
+    where_ref, mine_ref, other_ref, sine_ref, slots_ref, later_ref, elem_ref, patch_ref, walls_ref,
+    fluid_hbm, out_hbm, out_ref, sem
 ):
     group, core = where_ref[0], where_ref[1]
     first = jnp.full((N, HALF), core, jnp.int32) == 0
@@ -549,11 +563,14 @@
     own_rows = sine_rows(sine_ref, pl.multiple_of(group * HALF, HALF), HALF, 1)
     met = dot3(own_rows, dot3(given, slots_ref[...]))
     met = folded(jnp.where(iota((HALF, HALF), 0) // 16 == patch_ref[...] % 8, met, 0.0))
-    elem_hot = hot_of(column_of(elem_ref[...]) == iota((HALF, fluid_ref.shape[1]), 1))
-    out_ref[...] = fluid_ref[...] + GAIN * dot_hot(met - later_ref[...], elem_hot)
-
-
-def call(kernel, outs, args, scalars=0, scratch=(), aliases=None, specs=None, out_specs=None, cost=None):
+    elem_hot = hot_of(column_of(elem_ref[...]) == iota((HALF, walls_ref.shape[1]), 1))
+    out_ref[...] = walls_ref[...] + GAIN * dot_hot(met - later_ref[...], elem_hot)
+    copy = pltpu.make_async_copy(out_ref, out_hbm.at[pl.ds(256, 16), :], sem)
+    copy.start()
+    copy.wait()
+
+
+def call(kernel, outs, args, scalars=0, scratch=(), aliases=None, specs=None, out_specs=None, cost=None, limit=40):
     whole = pl.BlockSpec(memory_space=pltpu.VMEM)
     given = [pl.BlockSpec(memory_space=pltpu.SMEM)] * scalars + [whole] * (len(args) - scalars)
     return pl.pallas_call(
@@ -566,7 +583,7 @@
         scratch_shapes=list(scratch),
         input_output_aliases=aliases or {},
         cost_estimate=pl.CostEstimate(flops=int(cost or 1e8), bytes_accessed=1 << 20, transcendentals=0),
-        compiler_params=pltpu.CompilerParams(vmem_limit_bytes=40 << 20),
+        compiler_params=pltpu.CompilerParams(vmem_limit_bytes=limit << 20),
     )(*args)
 
 
@@ -584,20 +601,25 @@
     elem, owner, patch = iface_elem[None, :], iface_owner.reshape(1, HALF), iface_patch[None, :]
     smem = pl.BlockSpec(memory_space=pltpu.SMEM)
     vmem = pl.BlockSpec(memory_space=pltpu.VMEM)
-    anywhere = pl.BlockSpec(memory_space=pl.ANY)
+    hbm = pl.BlockSpec(memory_space=pltpu.HBM)
 
     far = lax.ppermute(solid, "g", [(0, 1), (1, 0)])
     near, trace0, surface0, first, last, wall_matrix, far_table = call(
         near_kernel,
         [(5 * HALF, HALF), (16, HALF), (2, HALF), (8, 384), (8, 384), (48, 320), (HALF, HALF)],
         [where, flux_jacobian, fluid0, solid, Q_HALVES, WALL_TABLES, elem, owner, patch],
-        specs=[smem] + [anywhere] * 4 + [vmem] * 4,
+        specs=[smem] + [hbm] * 8,
+        limit=52,
         scratch=[
             pltpu.VMEM(flux_jacobian.shape, F32),
             pltpu.VMEM(fluid0.shape, F32),
             pltpu.VMEM(solid.shape, F32),
             pltpu.VMEM(Q_HALVES.shape, F32),
-            pltpu.SemaphoreType.DMA((8,)),
+            pltpu.VMEM(WALL_TABLES.shape, F32),
+            pltpu.VMEM((1, HALF), jnp.int32),
+            pltpu.VMEM((1, HALF), jnp.int32),
+            pltpu.VMEM((1, HALF), jnp.int32),
+            pltpu.SemaphoreType.DMA((12,)),
         ],
     )
     before = lax.ppermute(last, ALL, [(i, i + 1) for i in range(255)])
@@ -637,32 +659,41 @@
         solve_kernel,
         [(N, N), (5 * N, HALF)],
         [where, got2, other, modes, RESPONSE, Q_HALVES, sine_pair, x_pair, modes_pair, modes_t_pair,
-         split_pair, decay, SURFACE_ROW, SURFACE_COLUMN],
+         split_pair, decay, SURFACE_ROW],
         scalars=1,
-        scratch=[pltpu.VMEM((N, N), F32)],
+        out_specs=[hbm, vmem],
+        scratch=[pltpu.VMEM((N, N), F32), pltpu.VMEM((N, N), F32), pltpu.SemaphoreType.DMA],
     )
     got3 = exchange(pay3, ALL)
-    fluid2, trace1, slots = call(
+    fluid2, trace1, slots, walls2 = call(
         second_kernel,
-        [(320, count), (16, HALF), (N, HALF)],
+        [(320, count), (16, HALF), (N, HALF), (16, count)],
         [where, fluid1, surface1, trace0, matrix, before, after, elem, owner, patch, Q_HALVES],
         scalars=1,
         cost=2e9,
     )
-    got3, fluid2, trace1, slots = lax.optimization_barrier((got3, fluid2, trace1, slots))
+    got3, fluid2, trace1, slots, walls2 = lax.optimization_barrier(
+        (got3, fluid2, trace1, slots, walls2)
+    )
     mine = got3.reshape(N, 5, 1, HALF)[:, 4].reshape(N, HALF)
     far_row = lax.ppermute(mine, "c", [(0, 1), (1, 0)])
-    (solid_out,) = call(solid_kernel, [(2 * N, HALF)], [where, got3, Q_HALVES], scalars=1)
-    walls_spec = pl.BlockSpec((16, count), lambda i: (16, 0))
-    (fluid2,) = pl.pallas_call(
+    (solid_out,) = call(
+        solid_kernel,
+        [(2 * N, HALF)],
+        [where, got3, Q_HALVES],
+        scalars=1,
+        out_specs=[hbm],
+        scratch=[pltpu.VMEM((2 * N, HALF), F32), pltpu.SemaphoreType.DMA((2,))],
+    )
+    (fluid2,) = call(
         last_kernel,
-        grid=(1,),
-        out_shape=[jax.ShapeDtypeStruct((320, count), F32)],
-        in_specs=[smem] + [vmem] * 7 + [walls_spec],
-        out_specs=[walls_spec],
-        input_output_aliases={8: 0},
-        compiler_params=pltpu.CompilerParams(vmem_limit_bytes=40 << 20),
-    )(where, mine, far_row, Q_HALVES, slots, trace1, elem, patch, fluid2)
+        [(320, count)],
+        [where, mine, far_row, Q_HALVES, slots, trace1, elem, patch, walls2, fluid2],
+        specs=[smem] + [vmem] * 8 + [hbm],
+        out_specs=[hbm],
+        aliases={9: 0},
+        scratch=[pltpu.VMEM((16, count), F32), pltpu.SemaphoreType.DMA],
+    )
     return fluid2.reshape(fluid_state.shape), solid_out.reshape(solid_temp.shape)
 
 

time: 112 us -> 111 us (level)
  local copies, waits for them, and re-layouts: 11.2 us -> 8.97 us
    pallas_call x9 -> x10, Pallas kernels: 26 us -> 29.2 us  [call(): pl.pallas_call(kernel, out_shape=[jax.ShapeDtypeStruct(*(out if isinstanc...]
    pallas_call x1 -> x0, Pallas kernels: 2.31 us -> none  [on_device(): pl.pallas_call(last_kernel, grid=(1,), out_shape=[jax.ShapeDtypeStruct((3...]
    unnamed x53 -> x49, local copies, waits for them, and re-layouts: 10.9 us -> 8.72 us
  transfers between devices with their start and end apart: 7 -> 7, of which waited for: 4 -> 4; matrix products, arithmetic and copies ran while one was open for 1% -> 1% of each run, Pallas kernels for 16% -> 17%
where the time goes in v4:
time: 111 us
  starting transfers between devices  30.7 us (28%)
  Pallas kernels  29.2 us (26%)
  blocking collectives  22.6 us (20%)
  waiting for transfers between devices  18 us (16%)
  local copies, waits for them, and re-layouts  8.97 us (8%)
    pallas_call x10, Pallas kernels, call(): pl.pallas_call(kernel, out_shape=[jax.ShapeDtypeStruct(*(out if isinstanc...  29.2 us
    all_to_all x1, blocking collectives, exchange(): lax.all_to_all(chunks, axes, split_axis=0, concat_axis=0, tiled=True)  22.6 us
    all_to_all x2, starting transfers between devices, exchange(): lax.all_to_all(chunks, axes, split_axis=0, concat_axis=0, tiled=True)  18.9 us
    all_to_all x2, waiting for transfers between devices, exchange(): lax.all_to_all(chunks, axes, split_axis=0, concat_axis=0, tiled=True)  14.7 us
    unnamed x49, local copies, waits for them, and re-layouts  8.72 us
    ppermute x1, starting transfers between devices, on_device(): far = lax.ppermute(solid, 'g', [(0, 1), (1, 0)])  3.83 us
    ppermute x1, starting transfers between devices, on_device(): before = lax.ppermute(last, ALL, [(i, i + 1) for i in range(255)])  3.54 us
    ppermute x1, starting transfers between devices, on_device(): other = lax.ppermute(got2, 'c', [(0, 1), (1, 0)])  2.4 us
  transfers between devices with their start and end apart: 7, of which 4 were waited for; matrix products, arithmetic and copies ran while one was open for 1% of the time, Pallas kernels for 17%

profile of v4, /device:TPU:1, one launch (start us, length us, event | category | flops | bytes accessed | tf_op | source)
XLA Modules:
  0.0 110.7 jit_solution(5615620288937088222)
XLA Ops:
  0.6 3.8 %collective-permute-start = (f32[512,128]{1,0:T(8,128)}, f32[512,128]{1,0:T(8,128)S(1)}, u32[]{:S(2)}, u32[]{:S(2)}) collective-permute-start(f32[512,128]{1,0:T(8,128)} %bitcast.35), channel_id=1, source_target_pairs={{0,128},{128,0},{1,129},{129,1},{2,130},{130,2},{3,131},{131,3},{4... | collective-permute-start | bytes 786440 | tf_op jit(solution)/shard_map/ppermute | solution.py:606
  4.5 0.7 copy.26.jac_hbm
  5.2 0.9 copy-done
  6.2 0.9 copy-done.4
  7.1 0.9 copy-done.8
  8.1 0.7 copy-done.14
  8.7 0.7 copy-done.16
  9.4 0.7 copy-done.18
  10.0 3.3 %shard_map.176 = (f32[640,128]{1,0:T(8,128)S(1)}, f32[16,128]{1,0:T(8,128)S(1)}, f32[2,128]{1,0:T(2,128)S(1)}, f32[8,384]{1,0:T(8,128)S(1)}, f32[8,384]{1,0:T(8,...) custom-call(s32[3]{0:T(128)S(1)} %pad_add_fusion.where_ref, f32[3,5,5]{2,1,0:T(8,128)S(1)} %copy.26.jac_hbm, ...), custom_call_target="tpu_custom_call" | custom-call | flops 100000000 | bytes 1048576 | tf_op jit(solution)/shard_map/pallas_call | solution.py:576
  13.5 1.0 shard_map.177
  14.5 13.5 %all-to-all-start = ((f32[640,1,128]{2,1,0:T(1,128)}), f32[640,1,128]{2,1,0:T(1,128)S(1)}, u32[]{:S(2)}, u32[]{:S(2)}) async-start(f32[640,1,128]{2,1,0:T(1,128)} %bitcast.9), calls=%async_computation | async-start | bytes 655360 | tf_op jit(solution)/shard_map/all_to_all | solution.py:592
  27.9 3.5 %collective-permute-start.1 = (f32[8,384]{1,0:T(8,128)S(1)}, f32[8,384]{1,0:T(8,128)S(1)}, u32[]{:S(2)}, u32[]{:S(2)}) collective-permute-start(f32[8,384]{1,0:T(8,128)S(1)} %get-tuple-element.36), channel_id=1, source_target_pairs={{0,1},{1,2},{2,3},{3,4},{4,5},{5,6},{6,7},{7,8},{8,9},{9,10},{10,1... | collective-permute-start | bytes 36872 | tf_op jit(solution)/shard_map/ppermute | solution.py:625
  31.5 1.9 %collective-permute-start.2 = (f32[8,384]{1,0:T(8,128)S(1)}, f32[8,384]{1,0:T(8,128)S(1)}, u32[]{:S(2)}, u32[]{:S(2)}) collective-permute-start(f32[8,384]{1,0:T(8,128)S(1)} %get-tuple-element.37), channel_id=1, source_target_pairs={{1,0},{2,1},{3,2},{4,3},{5,4},{6,5},{7,6},{8,7},{9,8},{10,9},{11,1... | collective-permute-start | bytes 36872 | tf_op jit(solution)/shard_map/ppermute | solution.py:626
  33.4 0.9 shard_map.178
  34.3 0.7 copy-done.6
  35.0 2.0 %collective-permute-done.2.after_ref = f32[8,384]{1,0:T(8,128)S(1)} collective-permute-done((f32[8,384]{1,0:T(8,128)S(1)}, f32[8,384]{1,0:T(8,128)S(1)}, u32[]{:S(2)}, u32[]{:S(2)}) %collective-permute-start.2) | collective-permute-done | bytes 12320 | tf_op jit(solution)/shard_map/ppermute | solution.py:626
  37.0 5.5 %all-to-all-done = f32[640,1,128]{2,1,0:T(1,128)S(1)} async-done(((f32[640,1,128]{2,1,0:T(1,128)}), f32[640,1,128]{2,1,0:T(1,128)S(1)}, u32[]{:S(2)}, u32[]{:S(2)}) %all-to-all-start) | async-done | bytes 327712 | tf_op jit(solution)/shard_map/all_to_all | solution.py:592
  42.6 2.4 %shard_map.179 = (f32[256,256]{1,0:T(8,128)S(1)}, f32[640,128]{1,0:T(8,128)S(1)}) custom-call(s32[3]{0:T(128)S(1)} %pad_add_fusion.where_ref, f32[640,128]{1,0:T(8,128)S(1)} %bitcast.27, f32[2,128]{1,0:T(2,128)S(1)} %get-tuple-element.30.order_ref.surface_ref, bf16[2,256,256]{2,1,0:T(8,128)(2,1)S(1)} %get-tuple-element.31.sine_ref.pair_ref, ...), custom_call_target="tpu_custom_call" | custom-call | flops 100000000 | bytes 1048576 | tf_op jit(solution)/shard_map/pallas_call | solution.py:576
  45.0 22.6 %all_to_all.15 = f32[640,1,128]{2,1,0:T(1,128)S(1)} all-to-all(f32[640,1,128]{2,1,0:T(1,128)S(1)} %bitcast.34), channel_id=1, replica_groups=mesh['g'=2,'yl'=2,'x'=4,'z'=8,'c'=2] {'g','yl','x','z'}, dimensions={0} | all-to-all | bytes 655360 | tf_op jit(solution)/shard_map/all_to_all | solution.py:592
  67.6 2.4 %collective-permute-start.3 = (f32[640,128]{1,0:T(8,128)S(1)}, f32[640,128]{1,0:T(8,128)S(1)}, u32[]{:S(2)}, u32[]{:S(2)}) collective-permute-start(f32[640,128]{1,0:T(8,128)S(1)} %bitcast.28), channel_id=1, source_target_pairs={{0,1},{1,0},{2,3},{3,2},{4,5},{5,4},{6,7},{7,6},{8,9},{9,8},{10,11... | collective-permute-start | bytes 983048 | tf_op jit(solution)/shard_map/ppermute | solution.py:657
  70.0 1.3 %collective-permute-done.3.other_ref = f32[640,128]{1,0:T(8,128)S(1)} collective-permute-done((f32[640,128]{1,0:T(8,128)S(1)}, f32[640,128]{1,0:T(8,128)S(1)}, u32[]{:S(2)}, u32[]{:S(2)}) %collective-permute-start.3) | collective-permute-done | bytes 327712 | tf_op jit(solution)/shard_map/ppermute | solution.py:657
  71.3 4.8 %shard_map.180 = (f32[256,256]{1,0:T(8,128)S(1)}, f32[1280,128]{1,0:T(8,128)}) custom-call(s32[3]{0:T(128)S(1)} %pad_add_fusion.where_ref, f32[640,128]{1,0:T(8,128)S(1)} %bitcast.29, f32[640,128]{1,0:T(8,128)S(1)} %collective-permute-done.3.other_ref, f32[256,256]{1,0:T(8,128)S(1)} %get-tuple-element.39.modes_ref, f32[256,256]{1,0:T(8,128)S(1)} %copy-done.5, ...), custom_call_target="tpu_custom_call" | custom-call | flops 100000000 | bytes 1048576 | tf_op jit(solution)/shard_map/pallas_call | solution.py:576
  76.1 0.7 copy-done.22
  76.8 5.4 %all-to-all-start.2 = ((f32[1280,1,128]{2,1,0:T(1,128)}), f32[1280,1,128]{2,1,0:T(1,128)S(1)}, u32[]{:S(2)}, u32[]{:S(2)}) async-start(f32[1280,1,128]{2,1,0:T(1,128)} %bitcast.15), calls=%async_computation.2 | async-start | bytes 1310720 | tf_op jit(solution)/shard_map/all_to_all | solution.py:592
  82.2 0.9 copy-done.11
  83.1 0.9 copy-done.12
  84.0 2.4 %shard_map.181.matrix_ref = f32[960,320]{1,0:T(8,128)S(1)} custom-call(f32[3,8,8]{2,1,0:T(8,128)S(1)} %pad.4.jac_ref, bf16[320,8]{1,0:T(8,128)(2,1)S(1)} %copy-done.11, bf16[320,64]{1,0:T(8,128)(2,1)S(1)} %copy-done.12, f32[3,320,320]{2,1,0:T(8,128)S(1)} %copy-done.2, f32[5,64,64]{2,1,0:T(8,128)S(1)} %copy-done.9), custom_call_target="tpu_custom_call" | custom-call | flops 100000000 | bytes 1048576 | tf_op jit(solution)/shard_map/pallas_call | solution.py:576
  86.4 4.5 %shard_map.182.fluid_ref = f32[320,1152]{1,0:T(8,128)S(1)} custom-call(s32[3]{0:T(128)S(1)} %pad_add_fusion.where_ref, f32[320,1024]{1,0:T(8,128)S(1)} %bitcast.31, f32[960,320]{1,0:T(8,128)S(1)} %shard_map.181.matrix_ref, f32[8,384]{1,0:T(8,128)S(1)} %collective-permute-done.1.before_ref, f32[8,384]{1,0:T(8,128)S(1)} %collective-permute-done.2.after_ref), custom_call_target="tpu_custom_call" | custom-call | flops 2000000000 | bytes 1048576 | tf_op jit(solution)/shard_map/pallas_call | solution.py:576
  91.0 6.3 %shard_map.183 = (f32[320,1024]{1,0:T(8,128)}, f32[16,128]{1,0:T(8,128)S(1)}, f32[256,128]{1,0:T(8,128)S(1)}, f32[16,1024]{1,0:T(8,128)S(1)}) custom-call(s32[3]{0:T(128)S(1)} %pad_add_fusion.where_ref, f32[320,1152]{1,0:T(8,128)S(1)} %shard_map.182.fluid_ref, f32[256,256]{1,0:T(8,128)S(1)} %copy-done.23, f32[16,128]{1,0:T(8,128)S(1)} %get-tuple-element.44.trace_ref, ...), custom_call_target="tpu_custom_call" | custom-call | flops 2000000000 | bytes 1048576 | tf_op jit(solution)/shard_map/pallas_call | solution.py:576
  97.2 9.2 %all-to-all-done.2 = f32[1280,1,128]{2,1,0:T(1,128)S(1)} async-done(((f32[1280,1,128]{2,1,0:T(1,128)}), f32[1280,1,128]{2,1,0:T(1,128)S(1)}, u32[]{:S(2)}, u32[]{:S(2)}) %all-to-all-start.2) | async-done | bytes 655392 | tf_op jit(solution)/shard_map/all_to_all | solution.py:592
  106.8 1.6 %shard_map.185 = f32[512,128]{1,0:T(8,128)} custom-call(s32[3]{0:T(128)S(1)} %pad_add_fusion.where_ref, f32[1280,128]{1,0:T(8,128)S(1)} %bitcast.26, f32[512,128]{1,0:T(8,128)S(1)} %copy-done.1), custom_call_target="tpu_custom_call" | custom-call | flops 100000000 | bytes 1048576 | tf_op jit(solution)/shard_map/pallas_call | solution.py:576
  108.5 2.0 %shard_map.184 = f32[320,1024]{1,0:T(8,128)} custom-call(s32[3]{0:T(128)S(1)} %pad_add_fusion.where_ref, f32[256,128]{1,0:T(8,128)S(1)} %bitcast.33, f32[256,128]{1,0:T(8,128)S(1)} %collective-permute-done.4.other_ref, f32[512,128]{1,0:T(8,128)S(1)} %copy-done.1, f32[256,128]{1,0:T(8,128)S(1)} %get-tuple-element.50.slots_ref, ...), custom_call_target="tpu_custom_call", output_to_operand_aliasing={{}: (9, {})} | custom-call | flops 100000000 | bytes 1048576 | tf_op jit(solution)/shard_map/pallas_call | solution.py:576
  (46 shorter events, 0.6 us)
Async XLA Ops:
  0.6 12.8 %collective-permute-start = (f32[512,128]{1,0:T(8,128)}, f32[512,128]{1,0:T(8,128)S(1)}, u32[]{:S(2)}, u32[]{:S(2)}) collective-permute-start(f32[512,128]{1,0:T(8,128)} %bitcast.35), channel_id=1, source_target_pairs={{0,128},{128,0},{1,129},{129,1},{2,130},{130,2},{3,131},{131,3},{4... | collective-permute-start | bytes 786440 | tf_op jit(solution)/shard_map/ppermute | solution.py:606
  5.2 1.0 copy-start
  6.2 0.9 copy-start.4
  7.1 0.9 copy-start.8
  8.1 0.7 copy-start.14
  8.7 0.7 copy-start.16
  9.4 0.7 copy-start.18
  10.0 23.4 %copy-start.1 = (f32[512,128]{1,0:T(8,128)S(1)}, f32[512,128]{1,0:T(8,128)}, u32[]{:S(2)}) copy-start(f32[512,128]{1,0:T(8,128)} %constant.78.clone.sine_hbm.sine_ref) | copy-start | bytes 786436
  10.0 23.4 %copy-start.10 = (f32[256,1]{1,0:T(8,128)S(1)}, f32[256,1]{1,0:T(8,128)}, u32[]{:S(2)}) copy-start(f32[256,1]{1,0:T(8,128)} %constant.82.clone.rate_col_ref) | copy-start | bytes 3076
  10.0 23.4 %copy-start.20 = (f32[256]{0:T(256)S(1)}, f32[256]{0:T(256)}, u32[]{:S(2)}) copy-start(f32[256]{0:T(256)} %constant.80.clone.rate_ref) | copy-start | bytes 3076
  10.0 23.4 %copy-start.21 = (f32[1,256]{1,0:T(1,128)S(1)}, f32[1,256]{1,0:T(1,128)}, u32[]{:S(2)}) copy-start(f32[1,256]{1,0:T(1,128)} %constant.81.clone.rate_row_ref) | copy-start | bytes 3076
  13.4 29.1 %copy-start.13 = (f32[8,256]{1,0:T(8,128)S(1)}, f32[8,256]{1,0:T(8,128)}, u32[]{:S(2)}) copy-start(f32[8,256]{1,0:T(8,128)} %constant.87.clone.row_ref) | copy-start | bytes 24580
  13.4 29.1 %copy-start.15 = (s32[128]{0:T(128)S(1)}, s32[128]{0:T(128)}, u32[]{:S(2)}) copy-start(s32[128]{0:T(128)} %param.20) | copy-start | bytes 1540
  13.4 29.1 %copy-start.17 = (s32[128]{0:T(128)S(1)}, s32[128]{0:T(128)}, u32[]{:S(2)}) copy-start(s32[128]{0:T(128)} %param.22) | copy-start | bytes 1540
  13.4 29.1 %copy-start.19 = (s32[128,1]{0,1:T(1,128)S(1)}, s32[128,1]{0,1:T(1,128)}, u32[]{:S(2)}) copy-start(s32[128,1]{0,1:T(1,128)} %param.21) | copy-start | bytes 1540
  14.5 56.8 %copy-start.5 = (f32[256,256]{1,0:T(8,128)S(1)}, f32[256,256]{1,0:T(8,128)}, u32[]{:S(2)}) copy-start(f32[256,256]{1,0:T(8,128)} %constant.88.clone.response_ref) | copy-start | bytes 786436
  14.5 28.1 %all-to-all-start = ((f32[640,1,128]{2,1,0:T(1,128)}), f32[640,1,128]{2,1,0:T(1,128)S(1)}, u32[]{:S(2)}, u32[]{:S(2)}) async-start(f32[640,1,128]{2,1,0:T(1,128)} %bitcast.9), calls=%async_computation | async-start | bytes 655360 | tf_op jit(solution)/shard_map/all_to_all | solution.py:592
  27.9 7.1 %collective-permute-start.1 = (f32[8,384]{1,0:T(8,128)S(1)}, f32[8,384]{1,0:T(8,128)S(1)}, u32[]{:S(2)}, u32[]{:S(2)}) collective-permute-start(f32[8,384]{1,0:T(8,128)S(1)} %get-tuple-element.36), channel_id=1, source_target_pairs={{0,1},{1,2},{2,3},{3,4},{4,5},{5,6},{6,7},{7,8},{8,9},{9,10},{10,1... | collective-permute-start | bytes 36872 | tf_op jit(solution)/shard_map/ppermute | solution.py:625
  31.5 5.6 %collective-permute-start.2 = (f32[8,384]{1,0:T(8,128)S(1)}, f32[8,384]{1,0:T(8,128)S(1)}, u32[]{:S(2)}, u32[]{:S(2)}) collective-permute-start(f32[8,384]{1,0:T(8,128)S(1)} %get-tuple-element.37), channel_id=1, source_target_pairs={{1,0},{2,1},{3,2},{4,3},{5,4},{6,5},{7,6},{8,7},{9,8},{10,9},{11,1... | collective-permute-start | bytes 36872 | tf_op jit(solution)/shard_map/ppermute | solution.py:626
  34.3 0.7 copy-start.6
  42.5 28.7 %copy-start.7 = (bf16[2,256,256]{2,1,0:T(8,128)(2,1)S(1)}, bf16[2,256,256]{2,1,0:T(8,128)(2,1)}, u32[]{:S(2)}) copy-start(bf16[2,256,256]{2,1,0:T(8,128)(2,1)} %copy-done.6) | copy-start | bytes 786436
  67.6 3.7 %collective-permute-start.3 = (f32[640,128]{1,0:T(8,128)S(1)}, f32[640,128]{1,0:T(8,128)S(1)}, u32[]{:S(2)}, u32[]{:S(2)}) collective-permute-start(f32[640,128]{1,0:T(8,128)S(1)} %bitcast.28), channel_id=1, source_target_pairs={{0,1},{1,0},{2,3},{3,2},{4,5},{5,4},{6,7},{7,6},{8,9},{9,8},{10,11... | collective-permute-start | bytes 983048 | tf_op jit(solution)/shard_map/ppermute | solution.py:657
  71.3 10.9 %copy-start.2 = (f32[3,320,320]{2,1,0:T(8,128)S(1)}, f32[3,320,320]{2,1,0:T(8,128)}, u32[]{:S(2)}) copy-start(f32[3,320,320]{2,1,0:T(8,128)} %constant.85.clone.fixed_ref) | copy-start | bytes 3686404
  71.3 10.9 %copy-start.9 = (f32[5,64,64]{2,1,0:T(8,128)S(1)}, f32[5,64,64]{2,1,0:T(8,128)}, u32[]{:S(2)}) copy-start(f32[5,64,64]{2,1,0:T(8,128)} %constant.86.clone.operators_ref) | copy-start | bytes 245764
  76.1 0.7 copy-start.22
  76.8 29.6 %all-to-all-start.2 = ((f32[1280,1,128]{2,1,0:T(1,128)}), f32[1280,1,128]{2,1,0:T(1,128)S(1)}, u32[]{:S(2)}, u32[]{:S(2)}) async-start(f32[1280,1,128]{2,1,0:T(1,128)} %bitcast.15), calls=%async_computation.2 | async-start | bytes 1310720 | tf_op jit(solution)/shard_map/all_to_all | solution.py:592
  82.2 0.9 copy-start.11
  83.1 0.9 copy-start.12
  84.0 2.4 %copy-start.3 = (f32[5,64,1024]{2,1,0:T(8,128)S(1)}, f32[5,64,1024]{2,1,0:T(8,128)}, u32[]{:S(2)}) copy-start(f32[5,64,1024]{2,1,0:T(8,128)} %param.17) | copy-start | bytes 3932164
  86.4 4.6 %copy-start.23 = (f32[256,256]{1,0:T(8,128)S(1)}, f32[256,256]{1,0:T(8,128)}, u32[]{:S(2)}) copy-start(f32[256,256]{1,0:T(8,128)} %copy-done.22) | copy-start | bytes 786436
  106.7 1.8 %collective-permute-start.4 = (f32[256,128]{1,0:T(8,128)S(1)}, f32[256,128]{1,0:T(8,128)S(1)}, u32[]{:S(2)}, u32[]{:S(2)}) collective-permute-start(f32[256,128]{1,0:T(8,128)S(1)} %bitcast.32), channel_id=1, source_target_pairs={{0,1},{1,0},{2,3},{3,2},{4,5},{5,4},{6,7},{7,6},{8,9},{9,8},{10,11... | collective-permute-start | bytes 393224 | tf_op jit(solution)/shard_map/ppermute | solution.py:679

commit v5 on v4

--- a/solution.py
+++ b/solution.py
@@ -268,7 +268,14 @@
     out_ref[pl.ds(4, HALF, 5), :] = arranged
 
 
-def far_kernel(far_ref, table_ref, near_ref, out_ref):
+def send_out(pairs, sems):
+    copies = [pltpu.make_async_copy(a, b, sems.at[i]) for i, (a, b) in enumerate(pairs)]
+    for copy in copies:
+        copy.start()
+    return copies
+
+
+def far_kernel(far_ref, table_ref, near_ref, out_hbm, out_ref, sems):
     table = split(table_ref[...])
     out_ref[pl.ds(4, HALF, 5), :] = rows(near_ref, 4, HALF, 5)
     for i in range(2):
@@ -276,11 +283,14 @@
         for h in range(2):
             part = modes[:, h * HALF : (h + 1) * HALF]
             out_ref[pl.ds(2 * i + h, HALF, 5), :] = rows(near_ref, 2 * i + h, HALF, 5) + part
+    pieces = [pl.ds(160 * i, 160) for i in range(4)]
+    for copy in send_out([(out_ref.at[at, :], out_hbm.at[at, :]) for at in pieces], sems):
+        copy.wait()
 
 
 def tables_kernel(
-    where_ref, rate_ref, sine_ref, rate_row_ref, rate_col_ref, order_ref,
-    sine_out, x_out, modes_out, modes_t_out, split_out, decay_out
+    where_ref, rate_ref, sine_ref, rate_row_ref, rate_col_ref, row_ref, order_ref,
+    sine_out, x_out, modes_out, modes_t_out, split_out, decay_out, once_out, twice_out, rows_out
 ):
     del order_ref
     by_modes = mode_ordered(sine_ref)
@@ -293,7 +303,14 @@
         out[0], out[1] = table
     for i in range(2):
         split_out[2 * i], split_out[2 * i + 1] = split(sine_rows(sine_ref, i, HALF, 2))
-    decay_out[...] = 1.0 / (rate_col_ref[...] + (rate_row_ref[...] + 64.0 * rate_ref[where_ref[2]]))
+    decay = 1.0 / (rate_col_ref[...] + (rate_row_ref[...] + 64.0 * rate_ref[where_ref[2]]))
+    decay_out[...] = decay
+    sine = split(sine_rows(sine_ref, 0, N, 1))
+    response = decay * sine_ref[pl.ds(0, N), 0:1]
+    for k, out in enumerate((once_out, twice_out)):
+        out[0], out[1] = split(dot3(response, sine, TN))
+        rows_out[8 * k : 8 * k + 8] = dot3(row_ref[...], response)
+        response = decay * response
 
 
 def matrices_kernel(jac_ref, field_ref, tile_ref, fixed_ref, operators_ref, out_ref):
@@ -323,8 +340,9 @@
         part = jnp.concatenate([rows(got_ref, 2 * i + h, HALF, 5) for h in range(2)], axis=1)
         by_z = dot3(sine, part, NT)
         modes = modes + dot3(by_z, (split_ref[2 * i], split_ref[2 * i + 1]))
-    modes_ref[...] = modes
-    surface_row = dot3(row_ref[...], decay_ref[...] * modes)[0:1]
+    modes = decay_ref[...] * modes
+    surface_row = dot3(row_ref[...], modes)[0:1]
+    modes_ref[...] = decay_ref[...] * modes
 
     fluid = rows(got_ref, 4, HALF, 5)
     square = (HALF, HALF)
@@ -385,7 +403,8 @@
 
 def solve_kernel(
     where_ref, got_ref, other_ref, modes_ref, response_ref, sine_ref, pair_ref, x_ref, by_modes_ref,
-    from_modes_ref, split_ref, decay_ref, row_ref, surface_hbm, out_ref, heat_ref, surface_ref, sem
+    from_modes_ref, split_ref, once_ref, twice_ref, rows_ref, row_ref,
+    surface_hbm, out_hbm, heat_ref, surface_ref, out_ref, sem, sems
 ):
     core, me = where_ref[1], where_ref[2]
     first = jnp.full((HALF, HALF), core, jnp.int32) == 0
@@ -393,6 +412,13 @@
     for r in range(5):
         mine, theirs = rows(got_ref, r, HALF, 5), rows(other_ref, r, HALF, 5)
         ordered.append((jnp.where(first, mine, theirs), jnp.where(first, theirs, mine)))
+
+    modes = split(modes_ref[...])
+    sine = pair_ref[0], pair_ref[1]
+    back = [
+        dot3(dot3((split_ref[2 * xl], split_ref[2 * xl + 1]), modes, NT), sine) for xl in range(2)
+    ]
+    final_row = dot3(row_ref[...], modes)[0:1]
 
     def block(g, r):
         return jnp.concatenate([ordered[r][k][g * 64 : (g + 1) * 64] for k in range(2)], axis=0)
@@ -445,21 +471,22 @@
             later = later + jnp.sum(jnp.where(met, value, 0.0), axis=0, keepdims=True)
     heat1 = dot3(later - 0.7 * reduced, by_x)[0:1]
     heat0 = heat_ref[pl.ds(core * HALF + me // 2, 1), :]
-    decay = decay_ref[...]
-    column = sine_ref[pl.ds(0, N), 0:1]
-    final = decay * (decay * (modes_ref[...] + column * heat0) + column * heat1)
-    final_row = dot3(row_ref[...], final)[0:1]
-    final = split(final)
-    sine = pair_ref[0], pair_ref[1]
+    final_row = final_row + heat0 * rows_ref[8:9] + heat1 * rows_ref[0:1]
     for xl in range(2):
-        back = dot3(dot3((split_ref[2 * xl], split_ref[2 * xl + 1]), final, NT), sine)
-        for g in range(2):
-            for h in range(2):
-                out_ref[pl.ds(g * 640 + 2 * xl + h, HALF, 5), :] = back[:, h * HALF : (h + 1) * HALF]
+        table = sine_rows(sine_ref, xl, HALF, 2)
+        part = back[xl] + dot3(table * heat0, (twice_ref[0], twice_ref[1]))
+        part = part + dot3(table * heat1, (once_ref[0], once_ref[1]))
+        for h in range(2):
+            out_ref[pl.ds(2 * xl + h, HALF, 5), :] = part[:, h * HALF : (h + 1) * HALF]
     for k in range(2):
-        out_ref[pl.ds(4 + 5 * k, HALF, 10), :] = jnp.broadcast_to(
-            final_row[:, k * HALF : (k + 1) * HALF], (HALF, HALF)
+        out_ref[pl.ds(4 + 5 * k, 64, 10), :] = jnp.broadcast_to(
+            final_row[:, k * HALF : (k + 1) * HALF], (64, HALF)
         )
+    pieces = [(160 * i, 640 * g + 160 * i) for i in range(4) for g in range(2)]
+    for sending in send_out(
+        [(out_ref.at[pl.ds(a, 160), :], out_hbm.at[pl.ds(b, 160), :]) for a, b in pieces], sems
+    ):
+        sending.wait()
     copy.wait()
 
 
@@ -538,25 +565,26 @@
     walls_ref[...] = result[256:272]
 
 
-def solid_kernel(where_ref, got_ref, sine_ref, solid_hbm, solid_ref, sems):
+def solid_half(h, where_ref, got_ref, sine_ref, solid_hbm, solid_ref, sem):
     by_y = split(sine_ref[pl.ds(pl.multiple_of(where_ref[0] * N, N), N), :])
-    copies = []
-    for h in range(2):
-        for xl in range(2):
-            part = rows(got_ref, 2 * xl + h, N, 5)
-            solid_ref[pl.ds(h * N + xl, HALF, 2), :] = dot3(part, by_y, TN)
-        at = pl.ds(h * N, N)
-        copies.append(pltpu.make_async_copy(solid_ref.at[at, :], solid_hbm.at[at, :], sems.at[h]))
-        copies[h].start()
-    for copy in copies:
-        copy.wait()
+    for xl in range(2):
+        part = rows(got_ref, 2 * xl + h, N, 5)
+        solid_ref[pl.ds(xl, HALF, 2), :] = dot3(part, by_y, TN)
+    copy = pltpu.make_async_copy(solid_ref, solid_hbm.at[pl.ds(h * N, N), :], sem)
+    copy.start()
+    return copy
+
+
+def solid_kernel(where_ref, got_ref, sine_ref, solid_hbm, solid_ref, sem):
+    solid_half(0, where_ref, got_ref, sine_ref, solid_hbm, solid_ref, sem).wait()
 
 
 def last_kernel(
-    where_ref, mine_ref, other_ref, sine_ref, slots_ref, later_ref, elem_ref, patch_ref, walls_ref,
-    fluid_hbm, out_hbm, out_ref, sem
+    where_ref, got_ref, mine_ref, other_ref, sine_ref, slots_ref, later_ref, elem_ref, patch_ref,
+    walls_ref, fluid_hbm, half_hbm, out_hbm, solid_hbm, out_ref, solid_ref, sem, solid_sem
 ):
     group, core = where_ref[0], where_ref[1]
+    solid = solid_half(1, where_ref, got_ref, sine_ref, solid_hbm, solid_ref, solid_sem)
     first = jnp.full((N, HALF), core, jnp.int32) == 0
     mine, other = mine_ref[...], other_ref[...]
     given = jnp.concatenate([jnp.where(first, mine, other), jnp.where(first, other, mine)], axis=1)
@@ -567,6 +595,7 @@
     out_ref[...] = walls_ref[...] + GAIN * dot_hot(met - later_ref[...], elem_hot)
     copy = pltpu.make_async_copy(out_ref, out_hbm.at[pl.ds(256, 16), :], sem)
     copy.start()
+    solid.wait()
     copy.wait()
 
 
@@ -624,15 +653,22 @@
     )
     before = lax.ppermute(last, ALL, [(i, i + 1) for i in range(255)])
     after = lax.ppermute(first, ALL, [(i + 1, i) for i in range(255)])
-    (pay1,) = call(far_kernel, [(5 * HALF, HALF)], [far, far_table, near])
+    (pay1,) = call(
+        far_kernel,
+        [(5 * HALF, HALF)],
+        [far, far_table, near],
+        out_specs=[hbm],
+        scratch=[pltpu.VMEM((5 * HALF, HALF), F32), pltpu.SemaphoreType.DMA((4,))],
+    )
     got1 = exchange(pay1, SUB)
     tables = call(
         tables_kernel,
-        [((2, N, N), BF16)] * 4 + [((4, HALF, N), BF16), (N, N)],
-        [where, RATE_LIST, Q_HALVES, RATE_ROW, RATE_COLUMN, surface0],
+        [((2, N, N), BF16)] * 4
+        + [((4, HALF, N), BF16), (N, N), ((2, N, N), BF16), ((2, N, N), BF16), (16, N)],
+        [where, RATE_LIST, Q_HALVES, RATE_ROW, RATE_COLUMN, SURFACE_ROW, surface0],
         scalars=2,
     )
-    sine_pair, x_pair, modes_pair, modes_t_pair, split_pair, decay = tables
+    sine_pair, x_pair, modes_pair, modes_t_pair, split_pair, decay, once, twice, heat_rows = tables
     jacobian = jnp.pad(flux_jacobian, ((0, 0), (0, 3), (0, 3)))
     (matrix,) = call(
         matrices_kernel,
@@ -659,10 +695,16 @@
         solve_kernel,
         [(N, N), (5 * N, HALF)],
         [where, got2, other, modes, RESPONSE, Q_HALVES, sine_pair, x_pair, modes_pair, modes_t_pair,
-         split_pair, decay, SURFACE_ROW],
+         split_pair, once, twice, heat_rows, SURFACE_ROW],
         scalars=1,
-        out_specs=[hbm, vmem],
-        scratch=[pltpu.VMEM((N, N), F32), pltpu.VMEM((N, N), F32), pltpu.SemaphoreType.DMA],
+        out_specs=[hbm, hbm],
+        scratch=[
+            pltpu.VMEM((N, N), F32),
+            pltpu.VMEM((N, N), F32),
+            pltpu.VMEM((5 * HALF, HALF), F32),
+            pltpu.SemaphoreType.DMA,
+            pltpu.SemaphoreType.DMA((8,)),
+        ],
     )
     got3 = exchange(pay3, ALL)
     fluid2, trace1, slots, walls2 = call(
@@ -683,16 +725,21 @@
         [where, got3, Q_HALVES],
         scalars=1,
         out_specs=[hbm],
-        scratch=[pltpu.VMEM((2 * N, HALF), F32), pltpu.SemaphoreType.DMA((2,))],
-    )
-    (fluid2,) = call(
+        scratch=[pltpu.VMEM((N, HALF), F32), pltpu.SemaphoreType.DMA],
+    )
+    fluid2, solid_out = call(
         last_kernel,
-        [(320, count)],
-        [where, mine, far_row, Q_HALVES, slots, trace1, elem, patch, walls2, fluid2],
-        specs=[smem] + [vmem] * 8 + [hbm],
-        out_specs=[hbm],
-        aliases={9: 0},
-        scratch=[pltpu.VMEM((16, count), F32), pltpu.SemaphoreType.DMA],
+        [(320, count), (2 * N, HALF)],
+        [where, got3, mine, far_row, Q_HALVES, slots, trace1, elem, patch, walls2, fluid2, solid_out],
+        specs=[smem] + [vmem] * 9 + [hbm] * 2,
+        out_specs=[hbm] * 2,
+        aliases={10: 0, 11: 1},
+        scratch=[
+            pltpu.VMEM((16, count), F32),
+            pltpu.VMEM((N, HALF), F32),
+            pltpu.SemaphoreType.DMA,
+            pltpu.SemaphoreType.DMA,
+        ],
     )
     return fluid2.reshape(fluid_state.shape), solid_out.reshape(solid_temp.shape)
 

time: 111 us -> 113 us (1.018)
  local copies, waits for them, and re-layouts: 8.97 us -> 10.2 us
    unnamed x49 -> x57, local copies, waits for them, and re-layouts: 8.72 us -> 9.94 us
where the time goes in v5:
time: 113 us
  starting transfers between devices  30.7 us (27%)
  Pallas kernels  29.6 us (26%)
  blocking collectives  22.6 us (20%)
  waiting for transfers between devices  18.2 us (16%)
  local copies, waits for them, and re-layouts  10.2 us (9%)
    pallas_call x10, Pallas kernels, call(): pl.pallas_call(kernel, out_shape=[jax.ShapeDtypeStruct(*(out if isinstanc...  29.6 us
    all_to_all x1, blocking collectives, exchange(): lax.all_to_all(chunks, axes, split_axis=0, concat_axis=0, tiled=True)  22.6 us
    all_to_all x2, starting transfers between devices, exchange(): lax.all_to_all(chunks, axes, split_axis=0, concat_axis=0, tiled=True)  18.9 us
    all_to_all x2, waiting for transfers between devices, exchange(): lax.all_to_all(chunks, axes, split_axis=0, concat_axis=0, tiled=True)  14.7 us
    unnamed x57, local copies, waits for them, and re-layouts  9.94 us
    ppermute x1, starting transfers between devices, on_device(): far = lax.ppermute(solid, 'g', [(0, 1), (1, 0)])  3.83 us
    ppermute x1, starting transfers between devices, on_device(): before = lax.ppermute(last, ALL, [(i, i + 1) for i in range(255)])  3.54 us
    ppermute x1, starting transfers between devices, on_device(): other = lax.ppermute(got2, 'c', [(0, 1), (1, 0)])  2.38 us
  transfers between devices with their start and end apart: 7, of which 4 were waited for; matrix products, arithmetic and copies ran while one was open for 1% of the time, Pallas kernels for 17%

profile of v5, /device:TPU:1, one launch (start us, length us, event | category | flops | bytes accessed | tf_op | source)
XLA Modules:
  0.0 112.5 jit_solution(17840405387046264313)
XLA Ops:
  0.6 3.8 %collective-permute-start = (f32[512,128]{1,0:T(8,128)}, f32[512,128]{1,0:T(8,128)S(1)}, u32[]{:S(2)}, u32[]{:S(2)}) collective-permute-start(f32[512,128]{1,0:T(8,128)} %bitcast.36), channel_id=1, source_target_pairs={{0,128},{128,0},{1,129},{129,1},{2,130},{130,2},{3,131},{131,3},{4... | collective-permute-start | bytes 786440 | tf_op jit(solution)/shard_map/ppermute | solution.py:635
  4.5 0.7 copy.26.jac_hbm
  5.2 0.9 copy-done
  6.2 0.9 copy-done.4
  7.1 0.9 copy-done.10
  8.1 0.7 copy-done.16
  8.7 0.7 copy-done.18
  10.1 3.3 %shard_map.176 = (f32[640,128]{1,0:T(8,128)S(1)}, f32[16,128]{1,0:T(8,128)S(1)}, f32[2,128]{1,0:T(2,128)S(1)}, f32[8,384]{1,0:T(8,128)S(1)}, f32[8,384]{1,0:T(8,...) custom-call(s32[3]{0:T(128)S(1)} %pad_add_fusion.where_ref, f32[3,5,5]{2,1,0:T(8,128)S(1)} %copy.26.jac_hbm, ...), custom_call_target="tpu_custom_call" | custom-call | flops 100000000 | bytes 1048576 | tf_op jit(solution)/shard_map/pallas_call | solution.py:605
  13.5 1.0 shard_map.177
  14.5 13.5 %all-to-all-start = ((f32[640,1,128]{2,1,0:T(1,128)}), f32[640,1,128]{2,1,0:T(1,128)S(1)}, u32[]{:S(2)}, u32[]{:S(2)}) async-start(f32[640,1,128]{2,1,0:T(1,128)} %bitcast.9), calls=%async_computation | async-start | bytes 655360 | tf_op jit(solution)/shard_map/all_to_all | solution.py:621
  28.0 3.5 %collective-permute-start.1 = (f32[8,384]{1,0:T(8,128)S(1)}, f32[8,384]{1,0:T(8,128)S(1)}, u32[]{:S(2)}, u32[]{:S(2)}) collective-permute-start(f32[8,384]{1,0:T(8,128)S(1)} %get-tuple-element.41), channel_id=1, source_target_pairs={{0,1},{1,2},{2,3},{3,4},{4,5},{5,6},{6,7},{7,8},{8,9},{9,10},{10,1... | collective-permute-start | bytes 36872 | tf_op jit(solution)/shard_map/ppermute | solution.py:654
  31.6 1.9 %collective-permute-start.2 = (f32[8,384]{1,0:T(8,128)S(1)}, f32[8,384]{1,0:T(8,128)S(1)}, u32[]{:S(2)}, u32[]{:S(2)}) collective-permute-start(f32[8,384]{1,0:T(8,128)S(1)} %get-tuple-element.42), channel_id=1, source_target_pairs={{1,0},{2,1},{3,2},{4,3},{5,4},{6,5},{7,6},{8,7},{9,8},{10,9},{11,1... | collective-permute-start | bytes 36872 | tf_op jit(solution)/shard_map/ppermute | solution.py:655
  33.5 1.3 %shard_map.178 = (bf16[2,256,256]{2,1,0:T(8,128)(2,1)S(1)}, bf16[2,256,256]{2,1,0:T(8,128)(2,1)S(1)}, bf16[2,256,256]{2,1,0:T(8,128)(2,1)S(1)}, bf16[2,256,256]{...) custom-call(s32[3]{0:T(128)S(1)} %pad_add_fusion.where_ref, ...), custom_call_target="tpu_custom_call" | custom-call | flops 100000000 | bytes 1048576 | tf_op jit(solution)/shard_map/pallas_call | solution.py:605
  34.9 2.3 %collective-permute-done.2.after_ref = f32[8,384]{1,0:T(8,128)S(1)} collective-permute-done((f32[8,384]{1,0:T(8,128)S(1)}, f32[8,384]{1,0:T(8,128)S(1)}, u32[]{:S(2)}, u32[]{:S(2)}) %collective-permute-start.2) | collective-permute-done | bytes 12320 | tf_op jit(solution)/shard_map/ppermute | solution.py:655
  37.1 5.5 %all-to-all-done = f32[640,1,128]{2,1,0:T(1,128)S(1)} async-done(((f32[640,1,128]{2,1,0:T(1,128)}), f32[640,1,128]{2,1,0:T(1,128)S(1)}, u32[]{:S(2)}, u32[]{:S(2)}) %all-to-all-start) | async-done | bytes 327712 | tf_op jit(solution)/shard_map/all_to_all | solution.py:621
  42.6 2.4 %shard_map.179 = (f32[256,256]{1,0:T(8,128)S(1)}, f32[640,128]{1,0:T(8,128)S(1)}) custom-call(s32[3]{0:T(128)S(1)} %pad_add_fusion.where_ref, f32[640,128]{1,0:T(8,128)S(1)} %bitcast.28, f32[2,128]{1,0:T(2,128)S(1)} %get-tuple-element.35.order_ref.surface_ref, bf16[2,256,256]{2,1,0:T(8,128)(2,1)S(1)} %get-tuple-element.36.sine_ref.pair_ref, ...), custom_call_target="tpu_custom_call" | custom-call | flops 100000000 | bytes 1048576 | tf_op jit(solution)/shard_map/pallas_call | solution.py:605
  45.1 22.6 %all_to_all.15 = f32[640,1,128]{2,1,0:T(1,128)S(1)} all-to-all(f32[640,1,128]{2,1,0:T(1,128)S(1)} %bitcast.35), channel_id=1, replica_groups=mesh['g'=2,'yl'=2,'x'=4,'z'=8,'c'=2] {'g','yl','x','z'}, dimensions={0} | all-to-all | bytes 655360 | tf_op jit(solution)/shard_map/all_to_all | solution.py:621
  67.7 2.4 %collective-permute-start.3 = (f32[640,128]{1,0:T(8,128)S(1)}, f32[640,128]{1,0:T(8,128)S(1)}, u32[]{:S(2)}, u32[]{:S(2)}) collective-permute-start(f32[640,128]{1,0:T(8,128)S(1)} %bitcast.31), channel_id=1, source_target_pairs={{0,1},{1,0},{2,3},{3,2},{4,5},{5,4},{6,7},{7,6},{8,9},{9,8},{10,11... | collective-permute-start | bytes 983048 | tf_op jit(solution)/shard_map/ppermute | solution.py:693
  70.1 1.3 %collective-permute-done.3.other_ref = f32[640,128]{1,0:T(8,128)S(1)} collective-permute-done((f32[640,128]{1,0:T(8,128)S(1)}, f32[640,128]{1,0:T(8,128)S(1)}, u32[]{:S(2)}, u32[]{:S(2)}) %collective-permute-start.3) | collective-permute-done | bytes 327712 | tf_op jit(solution)/shard_map/ppermute | solution.py:693
  71.4 0.9 copy-done.7
  72.3 0.9 copy-done.9
  73.3 4.6 %shard_map.180 = (f32[256,256]{1,0:T(8,128)S(1)}, f32[1280,128]{1,0:T(8,128)}) custom-call(s32[3]{0:T(128)S(1)} %pad_add_fusion.where_ref, f32[640,128]{1,0:T(8,128)S(1)} %bitcast.32, f32[640,128]{1,0:T(8,128)S(1)} %collective-permute-done.3.other_ref, f32[256,256]{1,0:T(8,128)S(1)} %get-tuple-element.44.modes_ref, f32[256,256]{1,0:T(8,128)S(1)} %copy-done.5, ...), custom_call_target="tpu_custom_call" | custom-call | flops 100000000 | bytes 1048576 | tf_op jit(solution)/shard_map/pallas_call | solution.py:605
  77.9 0.7 copy-done.24
  78.6 5.4 %all-to-all-start.2 = ((f32[1280,1,128]{2,1,0:T(1,128)}), f32[1280,1,128]{2,1,0:T(1,128)S(1)}, u32[]{:S(2)}, u32[]{:S(2)}) async-start(f32[1280,1,128]{2,1,0:T(1,128)} %bitcast.15), calls=%async_computation.2 | async-start | bytes 1310720 | tf_op jit(solution)/shard_map/all_to_all | solution.py:621
  84.1 0.9 copy-done.13
  84.9 0.9 copy-done.14
  85.8 2.3 %shard_map.181.matrix_ref = f32[960,320]{1,0:T(8,128)S(1)} custom-call(f32[3,8,8]{2,1,0:T(8,128)S(1)} %pad.4.jac_ref, bf16[320,8]{1,0:T(8,128)(2,1)S(1)} %copy-done.13, bf16[320,64]{1,0:T(8,128)(2,1)S(1)} %copy-done.14, f32[3,320,320]{2,1,0:T(8,128)S(1)} %copy-done.2, f32[5,64,64]{2,1,0:T(8,128)S(1)} %copy-done.11), custom_call_target="tpu_custom_call" | custom-call | flops 100000000 | bytes 1048576 | tf_op jit(solution)/shard_map/pallas_call | solution.py:605
  88.2 4.5 %shard_map.182.fluid_ref = f32[320,1152]{1,0:T(8,128)S(1)} custom-call(s32[3]{0:T(128)S(1)} %pad_add_fusion.where_ref, f32[320,1024]{1,0:T(8,128)S(1)} %bitcast.30, f32[960,320]{1,0:T(8,128)S(1)} %shard_map.181.matrix_ref, f32[8,384]{1,0:T(8,128)S(1)} %collective-permute-done.1.before_ref, f32[8,384]{1,0:T(8,128)S(1)} %collective-permute-done.2.after_ref), custom_call_target="tpu_custom_call" | custom-call | flops 2000000000 | bytes 1048576 | tf_op jit(solution)/shard_map/pallas_call | solution.py:605
  92.8 6.3 %shard_map.183 = (f32[320,1024]{1,0:T(8,128)}, f32[16,128]{1,0:T(8,128)S(1)}, f32[256,128]{1,0:T(8,128)S(1)}, f32[16,1024]{1,0:T(8,128)S(1)}) custom-call(s32[3]{0:T(128)S(1)} %pad_add_fusion.where_ref, f32[320,1152]{1,0:T(8,128)S(1)} %shard_map.182.fluid_ref, f32[256,256]{1,0:T(8,128)S(1)} %copy-done.25, f32[16,128]{1,0:T(8,128)S(1)} %copy-done.27, ...), custom_call_target="tpu_custom_call" | custom-call | flops 2000000000 | bytes 1048576 | tf_op jit(solution)/shard_map/pallas_call | solution.py:605
  99.0 9.2 %all-to-all-done.2 = f32[1280,1,128]{2,1,0:T(1,128)S(1)} async-done(((f32[1280,1,128]{2,1,0:T(1,128)}), f32[1280,1,128]{2,1,0:T(1,128)S(1)}, u32[]{:S(2)}, u32[]{:S(2)}) %all-to-all-start.2) | async-done | bytes 655392 | tf_op jit(solution)/shard_map/all_to_all | solution.py:621
  108.6 1.5 %shard_map.184.half_hbm = f32[512,128]{1,0:T(8,128)} custom-call(s32[3]{0:T(128)S(1)} %pad_add_fusion.where_ref, f32[1280,128]{1,0:T(8,128)S(1)} %bitcast.26, f32[512,128]{1,0:T(8,128)S(1)} %copy-done.1), custom_call_target="tpu_custom_call" | custom-call | flops 100000000 | bytes 1048576 | tf_op jit(solution)/shard_map/pallas_call | solution.py:605
  110.2 2.2 %shard_map.185 = (f32[320,1024]{1,0:T(8,128)}, f32[512,128]{1,0:T(8,128)}) custom-call(s32[3]{0:T(128)S(1)} %pad_add_fusion.where_ref, f32[1280,128]{1,0:T(8,128)S(1)} %bitcast.27, f32[256,128]{1,0:T(8,128)S(1)} %bitcast.34, f32[256,128]{1,0:T(8,128)S(1)} %collective-permute-done.4.other_ref, ...), custom_call_target="tpu_custom_call", output_to_operand_aliasing={{0}: (10, {}), {1}: (11, {})} | custom-call | flops 100000000 | bytes 1048576 | tf_op jit(solution)/shard_map/pallas_call | solution.py:605
  (54 shorter events, 1.2 us)
Async XLA Ops:
  0.6 12.8 %collective-permute-start = (f32[512,128]{1,0:T(8,128)}, f32[512,128]{1,0:T(8,128)S(1)}, u32[]{:S(2)}, u32[]{:S(2)}) collective-permute-start(f32[512,128]{1,0:T(8,128)} %bitcast.36), channel_id=1, source_target_pairs={{0,128},{128,0},{1,129},{129,1},{2,130},{130,2},{3,131},{131,3},{4... | collective-permute-start | bytes 786440 | tf_op jit(solution)/shard_map/ppermute | solution.py:635
  5.2 1.0 copy-start
  6.2 0.9 copy-start.4
  7.1 0.9 copy-start.10
  10.0 23.5 %copy-start.1 = (f32[512,128]{1,0:T(8,128)S(1)}, f32[512,128]{1,0:T(8,128)}, u32[]{:S(2)}) copy-start(f32[512,128]{1,0:T(8,128)} %constant.78.clone.sine_hbm.sine_ref) | copy-start | bytes 786436
  10.0 23.5 %copy-start.12 = (f32[256,1]{1,0:T(8,128)S(1)}, f32[256,1]{1,0:T(8,128)}, u32[]{:S(2)}) copy-start(f32[256,1]{1,0:T(8,128)} %constant.82.clone.rate_col_ref) | copy-start | bytes 3076
  10.0 23.5 %copy-start.15 = (f32[8,256]{1,0:T(8,128)S(1)}, f32[8,256]{1,0:T(8,128)}, u32[]{:S(2)}) copy-start(f32[8,256]{1,0:T(8,128)} %constant.83.clone.row_ref) | copy-start | bytes 24580
  10.0 23.5 %copy-start.22 = (f32[256]{0:T(256)S(1)}, f32[256]{0:T(256)}, u32[]{:S(2)}) copy-start(f32[256]{0:T(256)} %constant.80.clone.rate_ref) | copy-start | bytes 3076
  10.0 23.5 %copy-start.23 = (f32[1,256]{1,0:T(1,128)S(1)}, f32[1,256]{1,0:T(1,128)}, u32[]{:S(2)}) copy-start(f32[1,256]{1,0:T(1,128)} %constant.81.clone.rate_row_ref) | copy-start | bytes 3076
  13.4 1.1 copy-start.26
  13.4 29.2 %copy-start.17 = (s32[128]{0:T(128)S(1)}, s32[128]{0:T(128)}, u32[]{:S(2)}) copy-start(s32[128]{0:T(128)} %param.20) | copy-start | bytes 1540
  13.4 29.2 %copy-start.19 = (s32[128]{0:T(128)S(1)}, s32[128]{0:T(128)}, u32[]{:S(2)}) copy-start(s32[128]{0:T(128)} %param.22) | copy-start | bytes 1540
  13.4 29.2 %copy-start.21 = (s32[128,1]{0,1:T(1,128)S(1)}, s32[128,1]{0,1:T(1,128)}, u32[]{:S(2)}) copy-start(s32[128,1]{0,1:T(1,128)} %param.21) | copy-start | bytes 1540
  14.5 56.8 %copy-start.5 = (f32[256,256]{1,0:T(8,128)S(1)}, f32[256,256]{1,0:T(8,128)}, u32[]{:S(2)}) copy-start(f32[256,256]{1,0:T(8,128)} %constant.88.clone.response_ref) | copy-start | bytes 786436
  14.5 28.1 %all-to-all-start = ((f32[640,1,128]{2,1,0:T(1,128)}), f32[640,1,128]{2,1,0:T(1,128)S(1)}, u32[]{:S(2)}, u32[]{:S(2)}) async-start(f32[640,1,128]{2,1,0:T(1,128)} %bitcast.9), calls=%async_computation | async-start | bytes 655360 | tf_op jit(solution)/shard_map/all_to_all | solution.py:621
  28.0 6.8 %collective-permute-start.1 = (f32[8,384]{1,0:T(8,128)S(1)}, f32[8,384]{1,0:T(8,128)S(1)}, u32[]{:S(2)}, u32[]{:S(2)}) collective-permute-start(f32[8,384]{1,0:T(8,128)S(1)} %get-tuple-element.41), channel_id=1, source_target_pairs={{0,1},{1,2},{2,3},{3,4},{4,5},{5,6},{6,7},{7,8},{8,9},{9,10},{10,1... | collective-permute-start | bytes 36872 | tf_op jit(solution)/shard_map/ppermute | solution.py:654
  31.6 5.6 %collective-permute-start.2 = (f32[8,384]{1,0:T(8,128)S(1)}, f32[8,384]{1,0:T(8,128)S(1)}, u32[]{:S(2)}, u32[]{:S(2)}) collective-permute-start(f32[8,384]{1,0:T(8,128)S(1)} %get-tuple-element.42), channel_id=1, source_target_pairs={{1,0},{2,1},{3,2},{4,3},{5,4},{6,5},{7,6},{8,7},{9,8},{10,9},{11,1... | collective-permute-start | bytes 36872 | tf_op jit(solution)/shard_map/ppermute | solution.py:655
  34.8 36.5 %copy-start.6 = (bf16[2,256,256]{2,1,0:T(8,128)(2,1)}, bf16[2,256,256]{2,1,0:T(8,128)(2,1)S(1)}, u32[]{:S(2)}) copy-start(bf16[2,256,256]{2,1,0:T(8,128)(2,1)S(1)} %get-tuple-element.47.once_ref) | copy-start | bytes 786436
  34.8 36.5 %copy-start.8 = (bf16[2,256,256]{2,1,0:T(8,128)(2,1)}, bf16[2,256,256]{2,1,0:T(8,128)(2,1)S(1)}, u32[]{:S(2)}) copy-start(bf16[2,256,256]{2,1,0:T(8,128)(2,1)S(1)} %get-tuple-element.48.twice_ref) | copy-start | bytes 786436
  67.7 3.6 %collective-permute-start.3 = (f32[640,128]{1,0:T(8,128)S(1)}, f32[640,128]{1,0:T(8,128)S(1)}, u32[]{:S(2)}, u32[]{:S(2)}) collective-permute-start(f32[640,128]{1,0:T(8,128)S(1)} %bitcast.31), channel_id=1, source_target_pairs={{0,1},{1,0},{2,3},{3,2},{4,5},{5,4},{6,7},{7,6},{8,9},{9,8},{10,11... | collective-permute-start | bytes 983048 | tf_op jit(solution)/shard_map/ppermute | solution.py:693
  71.3 1.0 copy-start.7
  72.3 0.9 copy-start.9
  73.3 10.8 %copy-start.2 = (f32[3,320,320]{2,1,0:T(8,128)S(1)}, f32[3,320,320]{2,1,0:T(8,128)}, u32[]{:S(2)}) copy-start(f32[3,320,320]{2,1,0:T(8,128)} %constant.86.clone.fixed_ref) | copy-start | bytes 3686404
  73.3 10.8 %copy-start.11 = (f32[5,64,64]{2,1,0:T(8,128)S(1)}, f32[5,64,64]{2,1,0:T(8,128)}, u32[]{:S(2)}) copy-start(f32[5,64,64]{2,1,0:T(8,128)} %constant.87.clone.operators_ref) | copy-start | bytes 245764
  77.9 0.7 copy-start.24
  78.6 29.6 %all-to-all-start.2 = ((f32[1280,1,128]{2,1,0:T(1,128)}), f32[1280,1,128]{2,1,0:T(1,128)S(1)}, u32[]{:S(2)}, u32[]{:S(2)}) async-start(f32[1280,1,128]{2,1,0:T(1,128)} %bitcast.15), calls=%async_computation.2 | async-start | bytes 1310720 | tf_op jit(solution)/shard_map/all_to_all | solution.py:621
  84.0 0.9 copy-start.13
  84.9 0.9 copy-start.14
  85.8 2.4 %copy-start.3 = (f32[5,64,1024]{2,1,0:T(8,128)S(1)}, f32[5,64,1024]{2,1,0:T(8,128)}, u32[]{:S(2)}) copy-start(f32[5,64,1024]{2,1,0:T(8,128)} %param.17) | copy-start | bytes 3932164
  88.2 4.6 %copy-start.25 = (f32[256,256]{1,0:T(8,128)S(1)}, f32[256,256]{1,0:T(8,128)}, u32[]{:S(2)}) copy-start(f32[256,256]{1,0:T(8,128)} %copy-done.24) | copy-start | bytes 786436
  88.2 4.6 %copy-start.27 = (f32[16,128]{1,0:T(8,128)S(1)}, f32[16,128]{1,0:T(8,128)}, u32[]{:S(2)}) copy-start(f32[16,128]{1,0:T(8,128)} %copy-done.26) | copy-start | bytes 24580
  108.5 1.7 %collective-permute-start.4 = (f32[256,128]{1,0:T(8,128)S(1)}, f32[256,128]{1,0:T(8,128)S(1)}, u32[]{:S(2)}, u32[]{:S(2)}) collective-permute-start(f32[256,128]{1,0:T(8,128)S(1)} %bitcast.33), channel_id=1, source_target_pairs={{0,1},{1,0},{2,3},{3,2},{4,5},{5,4},{6,7},{7,6},{8,9},{9,8},{10,11... | collective-permute-start | bytes 393224 | tf_op jit(solution)/shard_map/ppermute | solution.py:721
  (3 other events, 2.0 us)

commit v6 on v5

--- a/solution.py
+++ b/solution.py
@@ -131,7 +131,9 @@
 def dot3(a, b, dims=NN):
     a = split(a) if not isinstance(a, tuple) else a
     b = split(b) if not isinstance(b, tuple) else b
-    return dot(a[0], b[0], dims) + (dot(a[0], b[1], dims) + dot(a[1], b[0], dims))
+    a = jnp.concatenate([a[0], a[1], a[0]], axis=dims[0][0])
+    b = jnp.concatenate([b[0], b[0], b[1]], axis=dims[1][0])
+    return dot(a, b, dims)
 
 
 def hot_dot(hot, b, dims=NN):
@@ -289,8 +291,8 @@
 
 
 def tables_kernel(
-    where_ref, rate_ref, sine_ref, rate_row_ref, rate_col_ref, row_ref, order_ref,
-    sine_out, x_out, modes_out, modes_t_out, split_out, decay_out, once_out, twice_out, rows_out
+    where_ref, rate_ref, sine_ref, rate_row_ref, rate_col_ref, order_ref,
+    sine_out, x_out, modes_out, modes_t_out, split_out, decay_out
 ):
     del order_ref
     by_modes = mode_ordered(sine_ref)
@@ -303,14 +305,7 @@
         out[0], out[1] = table
     for i in range(2):
         split_out[2 * i], split_out[2 * i + 1] = split(sine_rows(sine_ref, i, HALF, 2))
-    decay = 1.0 / (rate_col_ref[...] + (rate_row_ref[...] + 64.0 * rate_ref[where_ref[2]]))
-    decay_out[...] = decay
-    sine = split(sine_rows(sine_ref, 0, N, 1))
-    response = decay * sine_ref[pl.ds(0, N), 0:1]
-    for k, out in enumerate((once_out, twice_out)):
-        out[0], out[1] = split(dot3(response, sine, TN))
-        rows_out[8 * k : 8 * k + 8] = dot3(row_ref[...], response)
-        response = decay * response
+    decay_out[...] = 1.0 / (rate_col_ref[...] + (rate_row_ref[...] + 64.0 * rate_ref[where_ref[2]]))
 
 
 def matrices_kernel(jac_ref, field_ref, tile_ref, fixed_ref, operators_ref, out_ref):
@@ -340,9 +335,8 @@
         part = jnp.concatenate([rows(got_ref, 2 * i + h, HALF, 5) for h in range(2)], axis=1)
         by_z = dot3(sine, part, NT)
         modes = modes + dot3(by_z, (split_ref[2 * i], split_ref[2 * i + 1]))
-    modes = decay_ref[...] * modes
-    surface_row = dot3(row_ref[...], modes)[0:1]
-    modes_ref[...] = decay_ref[...] * modes
+    modes_ref[...] = modes
+    surface_row = dot3(row_ref[...], decay_ref[...] * modes)[0:1]
 
     fluid = rows(got_ref, 4, HALF, 5)
     square = (HALF, HALF)
@@ -403,7 +397,7 @@
 
 def solve_kernel(
     where_ref, got_ref, other_ref, modes_ref, response_ref, sine_ref, pair_ref, x_ref, by_modes_ref,
-    from_modes_ref, split_ref, once_ref, twice_ref, rows_ref, row_ref,
+    from_modes_ref, split_ref, decay_ref, row_ref,
     surface_hbm, out_hbm, heat_ref, surface_ref, out_ref, sem, sems
 ):
     core, me = where_ref[1], where_ref[2]
@@ -412,13 +406,6 @@
     for r in range(5):
         mine, theirs = rows(got_ref, r, HALF, 5), rows(other_ref, r, HALF, 5)
         ordered.append((jnp.where(first, mine, theirs), jnp.where(first, theirs, mine)))
-
-    modes = split(modes_ref[...])
-    sine = pair_ref[0], pair_ref[1]
-    back = [
-        dot3(dot3((split_ref[2 * xl], split_ref[2 * xl + 1]), modes, NT), sine) for xl in range(2)
-    ]
-    final_row = dot3(row_ref[...], modes)[0:1]
 
     def block(g, r):
         return jnp.concatenate([ordered[r][k][g * 64 : (g + 1) * 64] for k in range(2)], axis=0)
@@ -471,11 +458,14 @@
             later = later + jnp.sum(jnp.where(met, value, 0.0), axis=0, keepdims=True)
     heat1 = dot3(later - 0.7 * reduced, by_x)[0:1]
     heat0 = heat_ref[pl.ds(core * HALF + me // 2, 1), :]
-    final_row = final_row + heat0 * rows_ref[8:9] + heat1 * rows_ref[0:1]
+    decay = decay_ref[...]
+    column = sine_ref[pl.ds(0, N), 0:1]
+    final = decay * (decay * (modes_ref[...] + column * heat0) + column * heat1)
+    final_row = dot3(row_ref[...], final)[0:1]
+    final = split(final)
+    sine = pair_ref[0], pair_ref[1]
     for xl in range(2):
-        table = sine_rows(sine_ref, xl, HALF, 2)
-        part = back[xl] + dot3(table * heat0, (twice_ref[0], twice_ref[1]))
-        part = part + dot3(table * heat1, (once_ref[0], once_ref[1]))
+        part = dot3(dot3((split_ref[2 * xl], split_ref[2 * xl + 1]), final, NT), sine)
         for h in range(2):
             out_ref[pl.ds(2 * xl + h, HALF, 5), :] = part[:, h * HALF : (h + 1) * HALF]
     for k in range(2):
@@ -664,11 +654,11 @@
     tables = call(
         tables_kernel,
         [((2, N, N), BF16)] * 4
-        + [((4, HALF, N), BF16), (N, N), ((2, N, N), BF16), ((2, N, N), BF16), (16, N)],
-        [where, RATE_LIST, Q_HALVES, RATE_ROW, RATE_COLUMN, SURFACE_ROW, surface0],
+        + [((4, HALF, N), BF16), (N, N)],
+        [where, RATE_LIST, Q_HALVES, RATE_ROW, RATE_COLUMN, surface0],
         scalars=2,
     )
-    sine_pair, x_pair, modes_pair, modes_t_pair, split_pair, decay, once, twice, heat_rows = tables
+    sine_pair, x_pair, modes_pair, modes_t_pair, split_pair, decay = tables
     jacobian = jnp.pad(flux_jacobian, ((0, 0), (0, 3), (0, 3)))
     (matrix,) = call(
         matrices_kernel,
@@ -695,7 +685,7 @@
         solve_kernel,
         [(N, N), (5 * N, HALF)],
         [where, got2, other, modes, RESPONSE, Q_HALVES, sine_pair, x_pair, modes_pair, modes_t_pair,
-         split_pair, once, twice, heat_rows, SURFACE_ROW],
+         split_pair, decay, SURFACE_ROW],
         scalars=1,
         out_specs=[hbm, hbm],
         scratch=[

time: 113 us -> 111 us (0.982)
  Pallas kernels: 29.6 us -> 26.3 us
  waiting for transfers between devices: 18.2 us -> 20.2 us
  local copies, waits for them, and re-layouts: 10.2 us -> 8.97 us
    pallas_call x10, Pallas kernels: 29.6 us -> 26.3 us  [call(): pl.pallas_call(kernel, out_shape=[jax.ShapeDtypeStruct(*(out if isinstanc...]
    all_to_all x2, waiting for transfers between devices: 14.7 us -> 16.9 us  [exchange(): lax.all_to_all(chunks, axes, split_axis=0, concat_axis=0, tiled=True)]
    unnamed x57 -> x49, local copies, waits for them, and re-layouts: 9.94 us -> 8.73 us
  transfers between devices with their start and end apart: 7 -> 7, of which waited for: 4 -> 4; matrix products, arithmetic and copies ran while one was open for 1% -> 1% of each run, Pallas kernels for 17% -> 15%
where the time goes in v6:
time: 111 us; the launch traced here: 110 us
  starting transfers between devices  30.7 us (28%)
  Pallas kernels  26.3 us (24%)
  blocking collectives  22.6 us (20%)
  waiting for transfers between devices  20.2 us (18%)
  local copies, waits for them, and re-layouts  8.97 us (8%)
    pallas_call x10, Pallas kernels, call(): pl.pallas_call(kernel, out_shape=[jax.ShapeDtypeStruct(*(out if isinstanc...  26.3 us
    all_to_all x1, blocking collectives, exchange(): lax.all_to_all(chunks, axes, split_axis=0, concat_axis=0, tiled=True)  22.6 us
    all_to_all x2, starting transfers between devices, exchange(): lax.all_to_all(chunks, axes, split_axis=0, concat_axis=0, tiled=True)  18.9 us
    all_to_all x2, waiting for transfers between devices, exchange(): lax.all_to_all(chunks, axes, split_axis=0, concat_axis=0, tiled=True)  16.9 us
    unnamed x49, local copies, waits for them, and re-layouts  8.73 us
    ppermute x1, starting transfers between devices, on_device(): far = lax.ppermute(solid, 'g', [(0, 1), (1, 0)])  3.83 us
    ppermute x1, starting transfers between devices, on_device(): before = lax.ppermute(last, ALL, [(i, i + 1) for i in range(255)])  3.54 us
    ppermute x1, starting transfers between devices, on_device(): other = lax.ppermute(got2, 'c', [(0, 1), (1, 0)])  2.42 us
  transfers between devices with their start and end apart: 7, of which 4 were waited for; matrix products, arithmetic and copies ran while one was open for 1% of the time, Pallas kernels for 15%

profile of v6, /device:TPU:1, one launch (start us, length us, event | category | flops | bytes accessed | tf_op | source)
XLA Modules:
  0.0 110.0 jit_solution(6223960190831264652)
XLA Ops:
  0.6 3.8 %collective-permute-start = (f32[512,128]{1,0:T(8,128)}, f32[512,128]{1,0:T(8,128)S(1)}, u32[]{:S(2)}, u32[]{:S(2)}) collective-permute-start(f32[512,128]{1,0:T(8,128)} %bitcast.36), channel_id=1, source_target_pairs={{0,128},{128,0},{1,129},{129,1},{2,130},{130,2},{3,131},{131,3},{4... | collective-permute-start | bytes 786440 | tf_op jit(solution)/shard_map/ppermute | solution.py:625
  4.5 0.7 copy.26.jac_hbm
  5.2 0.9 copy-done
  6.2 0.9 copy-done.4
  7.1 0.9 copy-done.8
  8.1 0.7 copy-done.14
  8.7 0.7 copy-done.16
  9.4 0.7 copy-done.18
  10.0 3.3 %shard_map.176 = (f32[640,128]{1,0:T(8,128)S(1)}, f32[16,128]{1,0:T(8,128)S(1)}, f32[2,128]{1,0:T(2,128)S(1)}, f32[8,384]{1,0:T(8,128)S(1)}, f32[8,384]{1,0:T(8,...) custom-call(s32[3]{0:T(128)S(1)} %pad_add_fusion.where_ref, f32[3,5,5]{2,1,0:T(8,128)S(1)} %copy.26.jac_hbm, ...), custom_call_target="tpu_custom_call" | custom-call | flops 100000000 | bytes 1048576 | tf_op jit(solution)/shard_map/pallas_call | solution.py:595
  13.4 1.0 shard_map.177
  14.5 13.5 %all-to-all-start = ((f32[640,1,128]{2,1,0:T(1,128)}), f32[640,1,128]{2,1,0:T(1,128)S(1)}, u32[]{:S(2)}, u32[]{:S(2)}) async-start(f32[640,1,128]{2,1,0:T(1,128)} %bitcast.9), calls=%async_computation | async-start | bytes 655360 | tf_op jit(solution)/shard_map/all_to_all | solution.py:611
  27.9 3.5 %collective-permute-start.1 = (f32[8,384]{1,0:T(8,128)S(1)}, f32[8,384]{1,0:T(8,128)S(1)}, u32[]{:S(2)}, u32[]{:S(2)}) collective-permute-start(f32[8,384]{1,0:T(8,128)S(1)} %get-tuple-element.38), channel_id=1, source_target_pairs={{0,1},{1,2},{2,3},{3,4},{4,5},{5,6},{6,7},{7,8},{8,9},{9,10},{10,1... | collective-permute-start | bytes 36872 | tf_op jit(solution)/shard_map/ppermute | solution.py:644
  31.5 1.9 %collective-permute-start.2 = (f32[8,384]{1,0:T(8,128)S(1)}, f32[8,384]{1,0:T(8,128)S(1)}, u32[]{:S(2)}, u32[]{:S(2)}) collective-permute-start(f32[8,384]{1,0:T(8,128)S(1)} %get-tuple-element.39), channel_id=1, source_target_pairs={{1,0},{2,1},{3,2},{4,3},{5,4},{6,5},{7,6},{8,7},{9,8},{10,9},{11,1... | collective-permute-start | bytes 36872 | tf_op jit(solution)/shard_map/ppermute | solution.py:645
  33.5 0.9 shard_map.178
  34.3 0.7 copy-done.6
  35.0 2.0 %collective-permute-done.2.after_ref = f32[8,384]{1,0:T(8,128)S(1)} collective-permute-done((f32[8,384]{1,0:T(8,128)S(1)}, f32[8,384]{1,0:T(8,128)S(1)}, u32[]{:S(2)}, u32[]{:S(2)}) %collective-permute-start.2) | collective-permute-done | bytes 12320 | tf_op jit(solution)/shard_map/ppermute | solution.py:645
  37.1 5.5 %all-to-all-done = f32[640,1,128]{2,1,0:T(1,128)S(1)} async-done(((f32[640,1,128]{2,1,0:T(1,128)}), f32[640,1,128]{2,1,0:T(1,128)S(1)}, u32[]{:S(2)}, u32[]{:S(2)}) %all-to-all-start) | async-done | bytes 327712 | tf_op jit(solution)/shard_map/all_to_all | solution.py:611
  42.6 2.0 %shard_map.179 = (f32[256,256]{1,0:T(8,128)S(1)}, f32[640,128]{1,0:T(8,128)S(1)}) custom-call(s32[3]{0:T(128)S(1)} %pad_add_fusion.where_ref, f32[640,128]{1,0:T(8,128)S(1)} %bitcast.28, f32[2,128]{1,0:T(2,128)S(1)} %get-tuple-element.32.order_ref.surface_ref, bf16[2,256,256]{2,1,0:T(8,128)(2,1)S(1)} %get-tuple-element.33.sine_ref.pair_ref, ...), custom_call_target="tpu_custom_call" | custom-call | flops 100000000 | bytes 1048576 | tf_op jit(solution)/shard_map/pallas_call | solution.py:595
  44.6 22.6 %all_to_all.15 = f32[640,1,128]{2,1,0:T(1,128)S(1)} all-to-all(f32[640,1,128]{2,1,0:T(1,128)S(1)} %bitcast.35), channel_id=1, replica_groups=mesh['g'=2,'yl'=2,'x'=4,'z'=8,'c'=2] {'g','yl','x','z'}, dimensions={0} | all-to-all | bytes 655360 | tf_op jit(solution)/shard_map/all_to_all | solution.py:611
  67.2 2.4 %collective-permute-start.3 = (f32[640,128]{1,0:T(8,128)S(1)}, f32[640,128]{1,0:T(8,128)S(1)}, u32[]{:S(2)}, u32[]{:S(2)}) collective-permute-start(f32[640,128]{1,0:T(8,128)S(1)} %bitcast.29), channel_id=1, source_target_pairs={{0,1},{1,0},{2,3},{3,2},{4,5},{5,4},{6,7},{7,6},{8,9},{9,8},{10,11... | collective-permute-start | bytes 983048 | tf_op jit(solution)/shard_map/ppermute | solution.py:683
  69.6 1.3 %collective-permute-done.3.other_ref = f32[640,128]{1,0:T(8,128)S(1)} collective-permute-done((f32[640,128]{1,0:T(8,128)S(1)}, f32[640,128]{1,0:T(8,128)S(1)}, u32[]{:S(2)}, u32[]{:S(2)}) %collective-permute-start.3) | collective-permute-done | bytes 327712 | tf_op jit(solution)/shard_map/ppermute | solution.py:683
  70.9 4.5 %shard_map.180 = (f32[256,256]{1,0:T(8,128)S(1)}, f32[1280,128]{1,0:T(8,128)}) custom-call(s32[3]{0:T(128)S(1)} %pad_add_fusion.where_ref, f32[640,128]{1,0:T(8,128)S(1)} %bitcast.30, f32[640,128]{1,0:T(8,128)S(1)} %collective-permute-done.3.other_ref, f32[256,256]{1,0:T(8,128)S(1)} %get-tuple-element.41.modes_ref, f32[256,256]{1,0:T(8,128)S(1)} %copy-done.5, ...), custom_call_target="tpu_custom_call" | custom-call | flops 100000000 | bytes 1048576 | tf_op jit(solution)/shard_map/pallas_call | solution.py:595
  75.4 0.7 copy-done.22
  76.1 5.4 %all-to-all-start.2 = ((f32[1280,1,128]{2,1,0:T(1,128)}), f32[1280,1,128]{2,1,0:T(1,128)S(1)}, u32[]{:S(2)}, u32[]{:S(2)}) async-start(f32[1280,1,128]{2,1,0:T(1,128)} %bitcast.15), calls=%async_computation.2 | async-start | bytes 1310720 | tf_op jit(solution)/shard_map/all_to_all | solution.py:611
  81.6 0.9 copy-done.11
  82.4 0.9 copy-done.12
  83.3 2.4 %shard_map.181.matrix_ref = f32[960,320]{1,0:T(8,128)S(1)} custom-call(f32[3,8,8]{2,1,0:T(8,128)S(1)} %pad.4.jac_ref, bf16[320,8]{1,0:T(8,128)(2,1)S(1)} %copy-done.11, bf16[320,64]{1,0:T(8,128)(2,1)S(1)} %copy-done.12, f32[3,320,320]{2,1,0:T(8,128)S(1)} %copy-done.2, f32[5,64,64]{2,1,0:T(8,128)S(1)} %copy-done.9), custom_call_target="tpu_custom_call" | custom-call | flops 100000000 | bytes 1048576 | tf_op jit(solution)/shard_map/pallas_call | solution.py:595
  85.7 3.4 %shard_map.182.fluid_ref = f32[320,1152]{1,0:T(8,128)S(1)} custom-call(s32[3]{0:T(128)S(1)} %pad_add_fusion.where_ref, f32[320,1024]{1,0:T(8,128)S(1)} %bitcast.32, f32[960,320]{1,0:T(8,128)S(1)} %shard_map.181.matrix_ref, f32[8,384]{1,0:T(8,128)S(1)} %collective-permute-done.1.before_ref, f32[8,384]{1,0:T(8,128)S(1)} %collective-permute-done.2.after_ref), custom_call_target="tpu_custom_call" | custom-call | flops 2000000000 | bytes 1048576 | tf_op jit(solution)/shard_map/pallas_call | solution.py:595
  89.2 5.2 %shard_map.183 = (f32[320,1024]{1,0:T(8,128)}, f32[16,128]{1,0:T(8,128)S(1)}, f32[256,128]{1,0:T(8,128)S(1)}, f32[16,1024]{1,0:T(8,128)S(1)}) custom-call(s32[3]{0:T(128)S(1)} %pad_add_fusion.where_ref, f32[320,1152]{1,0:T(8,128)S(1)} %shard_map.182.fluid_ref, f32[256,256]{1,0:T(8,128)S(1)} %copy-done.23, f32[16,128]{1,0:T(8,128)S(1)} %get-tuple-element.46.trace_ref, ...), custom_call_target="tpu_custom_call" | custom-call | flops 2000000000 | bytes 1048576 | tf_op jit(solution)/shard_map/pallas_call | solution.py:595
  94.3 11.4 %all-to-all-done.2 = f32[1280,1,128]{2,1,0:T(1,128)S(1)} async-done(((f32[1280,1,128]{2,1,0:T(1,128)}), f32[1280,1,128]{2,1,0:T(1,128)S(1)}, u32[]{:S(2)}, u32[]{:S(2)}) %all-to-all-start.2) | async-done | bytes 655392 | tf_op jit(solution)/shard_map/all_to_all | solution.py:611
  106.2 1.5 %shard_map.184.half_hbm = f32[512,128]{1,0:T(8,128)} custom-call(s32[3]{0:T(128)S(1)} %pad_add_fusion.where_ref, f32[1280,128]{1,0:T(8,128)S(1)} %bitcast.26, f32[512,128]{1,0:T(8,128)S(1)} %copy-done.1), custom_call_target="tpu_custom_call" | custom-call | flops 100000000 | bytes 1048576 | tf_op jit(solution)/shard_map/pallas_call | solution.py:595
  107.7 2.2 %shard_map.185 = (f32[320,1024]{1,0:T(8,128)}, f32[512,128]{1,0:T(8,128)}) custom-call(s32[3]{0:T(128)S(1)} %pad_add_fusion.where_ref, f32[1280,128]{1,0:T(8,128)S(1)} %bitcast.27, f32[256,128]{1,0:T(8,128)S(1)} %bitcast.34, f32[256,128]{1,0:T(8,128)S(1)} %collective-permute-done.4.other_ref, ...), custom_call_target="tpu_custom_call", output_to_operand_aliasing={{0}: (10, {}), {1}: (11, {})} | custom-call | flops 100000000 | bytes 1048576 | tf_op jit(solution)/shard_map/pallas_call | solution.py:595
  (46 shorter events, 0.6 us)
Async XLA Ops:
  0.6 12.8 %collective-permute-start = (f32[512,128]{1,0:T(8,128)}, f32[512,128]{1,0:T(8,128)S(1)}, u32[]{:S(2)}, u32[]{:S(2)}) collective-permute-start(f32[512,128]{1,0:T(8,128)} %bitcast.36), channel_id=1, source_target_pairs={{0,128},{128,0},{1,129},{129,1},{2,130},{130,2},{3,131},{131,3},{4... | collective-permute-start | bytes 786440 | tf_op jit(solution)/shard_map/ppermute | solution.py:625
  5.2 1.0 copy-start
  6.2 0.9 copy-start.4
  7.1 0.9 copy-start.8
  8.1 0.7 copy-start.14
  8.7 0.7 copy-start.16
  9.4 0.7 copy-start.18
  10.0 23.4 %copy-start.1 = (f32[512,128]{1,0:T(8,128)S(1)}, f32[512,128]{1,0:T(8,128)}, u32[]{:S(2)}) copy-start(f32[512,128]{1,0:T(8,128)} %constant.78.clone.sine_hbm.sine_ref) | copy-start | bytes 786436
  10.0 23.4 %copy-start.10 = (f32[256,1]{1,0:T(8,128)S(1)}, f32[256,1]{1,0:T(8,128)}, u32[]{:S(2)}) copy-start(f32[256,1]{1,0:T(8,128)} %constant.82.clone.rate_col_ref) | copy-start | bytes 3076
  10.0 23.4 %copy-start.20 = (f32[256]{0:T(256)S(1)}, f32[256]{0:T(256)}, u32[]{:S(2)}) copy-start(f32[256]{0:T(256)} %constant.80.clone.rate_ref) | copy-start | bytes 3076
  10.0 23.4 %copy-start.21 = (f32[1,256]{1,0:T(1,128)S(1)}, f32[1,256]{1,0:T(1,128)}, u32[]{:S(2)}) copy-start(f32[1,256]{1,0:T(1,128)} %constant.81.clone.rate_row_ref) | copy-start | bytes 3076
  13.4 29.2 %copy-start.13 = (f32[8,256]{1,0:T(8,128)S(1)}, f32[8,256]{1,0:T(8,128)}, u32[]{:S(2)}) copy-start(f32[8,256]{1,0:T(8,128)} %constant.87.clone.row_ref) | copy-start | bytes 24580
  13.4 29.2 %copy-start.15 = (s32[128]{0:T(128)S(1)}, s32[128]{0:T(128)}, u32[]{:S(2)}) copy-start(s32[128]{0:T(128)} %param.20) | copy-start | bytes 1540
  13.4 29.2 %copy-start.17 = (s32[128]{0:T(128)S(1)}, s32[128]{0:T(128)}, u32[]{:S(2)}) copy-start(s32[128]{0:T(128)} %param.22) | copy-start | bytes 1540
  13.4 29.2 %copy-start.19 = (s32[128,1]{0,1:T(1,128)S(1)}, s32[128,1]{0,1:T(1,128)}, u32[]{:S(2)}) copy-start(s32[128,1]{0,1:T(1,128)} %param.21) | copy-start | bytes 1540
  14.4 56.4 %copy-start.5 = (f32[256,256]{1,0:T(8,128)S(1)}, f32[256,256]{1,0:T(8,128)}, u32[]{:S(2)}) copy-start(f32[256,256]{1,0:T(8,128)} %constant.88.clone.response_ref) | copy-start | bytes 786436
  14.5 28.1 %all-to-all-start = ((f32[640,1,128]{2,1,0:T(1,128)}), f32[640,1,128]{2,1,0:T(1,128)S(1)}, u32[]{:S(2)}, u32[]{:S(2)}) async-start(f32[640,1,128]{2,1,0:T(1,128)} %bitcast.9), calls=%async_computation | async-start | bytes 655360 | tf_op jit(solution)/shard_map/all_to_all | solution.py:611
  27.9 7.1 %collective-permute-start.1 = (f32[8,384]{1,0:T(8,128)S(1)}, f32[8,384]{1,0:T(8,128)S(1)}, u32[]{:S(2)}, u32[]{:S(2)}) collective-permute-start(f32[8,384]{1,0:T(8,128)S(1)} %get-tuple-element.38), channel_id=1, source_target_pairs={{0,1},{1,2},{2,3},{3,4},{4,5},{5,6},{6,7},{7,8},{8,9},{9,10},{10,1... | collective-permute-start | bytes 36872 | tf_op jit(solution)/shard_map/ppermute | solution.py:644
  31.5 5.6 %collective-permute-start.2 = (f32[8,384]{1,0:T(8,128)S(1)}, f32[8,384]{1,0:T(8,128)S(1)}, u32[]{:S(2)}, u32[]{:S(2)}) collective-permute-start(f32[8,384]{1,0:T(8,128)S(1)} %get-tuple-element.39), channel_id=1, source_target_pairs={{1,0},{2,1},{3,2},{4,3},{5,4},{6,5},{7,6},{8,7},{9,8},{10,9},{11,1... | collective-permute-start | bytes 36872 | tf_op jit(solution)/shard_map/ppermute | solution.py:645
  34.3 0.7 copy-start.6
  42.6 28.3 %copy-start.7 = (bf16[2,256,256]{2,1,0:T(8,128)(2,1)S(1)}, bf16[2,256,256]{2,1,0:T(8,128)(2,1)}, u32[]{:S(2)}) copy-start(bf16[2,256,256]{2,1,0:T(8,128)(2,1)} %copy-done.6) | copy-start | bytes 786436
  67.2 3.7 %collective-permute-start.3 = (f32[640,128]{1,0:T(8,128)S(1)}, f32[640,128]{1,0:T(8,128)S(1)}, u32[]{:S(2)}, u32[]{:S(2)}) collective-permute-start(f32[640,128]{1,0:T(8,128)S(1)} %bitcast.29), channel_id=1, source_target_pairs={{0,1},{1,0},{2,3},{3,2},{4,5},{5,4},{6,7},{7,6},{8,9},{9,8},{10,11... | collective-permute-start | bytes 983048 | tf_op jit(solution)/shard_map/ppermute | solution.py:683
  70.9 10.7 %copy-start.2 = (f32[3,320,320]{2,1,0:T(8,128)S(1)}, f32[3,320,320]{2,1,0:T(8,128)}, u32[]{:S(2)}) copy-start(f32[3,320,320]{2,1,0:T(8,128)} %constant.85.clone.fixed_ref) | copy-start | bytes 3686404
  70.9 10.7 %copy-start.9 = (f32[5,64,64]{2,1,0:T(8,128)S(1)}, f32[5,64,64]{2,1,0:T(8,128)}, u32[]{:S(2)}) copy-start(f32[5,64,64]{2,1,0:T(8,128)} %constant.86.clone.operators_ref) | copy-start | bytes 245764
  75.4 0.7 copy-start.22
  76.1 29.6 %all-to-all-start.2 = ((f32[1280,1,128]{2,1,0:T(1,128)}), f32[1280,1,128]{2,1,0:T(1,128)S(1)}, u32[]{:S(2)}, u32[]{:S(2)}) async-start(f32[1280,1,128]{2,1,0:T(1,128)} %bitcast.15), calls=%async_computation.2 | async-start | bytes 1310720 | tf_op jit(solution)/shard_map/all_to_all | solution.py:611
  81.5 0.9 copy-start.11
  82.4 0.9 copy-start.12
  83.3 2.4 %copy-start.3 = (f32[5,64,1024]{2,1,0:T(8,128)S(1)}, f32[5,64,1024]{2,1,0:T(8,128)}, u32[]{:S(2)}) copy-start(f32[5,64,1024]{2,1,0:T(8,128)} %param.17) | copy-start | bytes 3932164
  85.7 3.5 %copy-start.23 = (f32[256,256]{1,0:T(8,128)S(1)}, f32[256,256]{1,0:T(8,128)}, u32[]{:S(2)}) copy-start(f32[256,256]{1,0:T(8,128)} %copy-done.22) | copy-start | bytes 786436
  106.0 1.7 %collective-permute-start.4 = (f32[256,128]{1,0:T(8,128)S(1)}, f32[256,128]{1,0:T(8,128)S(1)}, u32[]{:S(2)}, u32[]{:S(2)}) collective-permute-start(f32[256,128]{1,0:T(8,128)S(1)} %bitcast.33), channel_id=1, source_target_pairs={{0,1},{1,0},{2,3},{3,2},{4,5},{5,4},{6,7},{7,6},{8,9},{9,8},{10,11... | collective-permute-start | bytes 393224 | tf_op jit(solution)/shard_map/ppermute | solution.py:711

commit v7 on v6

--- a/solution.py
+++ b/solution.py
@@ -17,6 +17,7 @@
 DT = 0.05
 VISC = 0.05
 GAIN = 0.3
+SURFACE_ROWS = 20480
 F32 = jnp.float32
 BF16 = jnp.bfloat16
 NN = ((1,), (0,))
@@ -429,7 +430,7 @@
     surface = dot3((from_modes_ref[0], from_modes_ref[1]), given + response_ref[...] * heat_modes)
     surface = dot3(surface, by_x, NT)
     surface_ref[...] = surface
-    copy = pltpu.make_async_copy(surface_ref, surface_hbm, sem)
+    copy = pltpu.make_async_copy(surface_ref, surface_hbm.at[pl.ds(0, N), :], sem)
     copy.start()
     square = (HALF, HALF)
     tails = [block(g, 4) for g in range(2)]
@@ -522,9 +523,12 @@
 
 
 def second_kernel(
-    where_ref, fluid_ref, surface_ref, trace_ref, matrix_ref, before_ref, after_ref, elem_ref,
-    owner_ref, patch_ref, sine_ref, out_ref, later_ref, slots_ref, walls_ref
+    where_ref, surface_hbm, fluid_ref, trace_ref, matrix_ref, before_ref, after_ref, elem_ref,
+    owner_ref, patch_ref, sine_ref, out_ref, later_ref, slots_ref, walls_ref, surface_ref, sem
 ):
+    copy = pltpu.make_async_copy(surface_hbm.at[pl.ds(0, N), :], surface_ref, sem)
+    copy.start()
+    copy.wait()
     group, me = where_ref[0], where_ref[2]
     width = fluid_ref.shape[1]
     count = width - HALF
@@ -555,26 +559,21 @@
     walls_ref[...] = result[256:272]
 
 
-def solid_half(h, where_ref, got_ref, sine_ref, solid_hbm, solid_ref, sem):
+def solid_kernel(where_ref, got_ref, sine_ref, solid_ref):
     by_y = split(sine_ref[pl.ds(pl.multiple_of(where_ref[0] * N, N), N), :])
     for xl in range(2):
-        part = rows(got_ref, 2 * xl + h, N, 5)
-        solid_ref[pl.ds(xl, HALF, 2), :] = dot3(part, by_y, TN)
-    copy = pltpu.make_async_copy(solid_ref, solid_hbm.at[pl.ds(h * N, N), :], sem)
-    copy.start()
-    return copy
-
-
-def solid_kernel(where_ref, got_ref, sine_ref, solid_hbm, solid_ref, sem):
-    solid_half(0, where_ref, got_ref, sine_ref, solid_hbm, solid_ref, sem).wait()
+        for h in range(2):
+            part = rows(got_ref, 2 * xl + h, N, 5)
+            solid_ref[pl.ds(h * N + xl, HALF, 2), :] = dot3(part, by_y, TN)
 
 
 def last_kernel(
-    where_ref, got_ref, mine_ref, other_ref, sine_ref, slots_ref, later_ref, elem_ref, patch_ref,
-    walls_ref, fluid_hbm, half_hbm, out_hbm, solid_hbm, out_ref, solid_ref, sem, solid_sem
+    where_ref, solid_ref, mine_ref, other_ref, sine_ref, slots_ref, later_ref, elem_ref, patch_ref,
+    walls_ref, fluid_hbm, out_hbm, solid_hbm, out_ref, sem, solid_sems
 ):
     group, core = where_ref[0], where_ref[1]
-    solid = solid_half(1, where_ref, got_ref, sine_ref, solid_hbm, solid_ref, solid_sem)
+    pieces = [pl.ds(HALF * i, HALF) for i in range(4)]
+    solid = send_out([(solid_ref.at[at, :], solid_hbm.at[at, :]) for at in pieces], solid_sems)
     first = jnp.full((N, HALF), core, jnp.int32) == 0
     mine, other = mine_ref[...], other_ref[...]
     given = jnp.concatenate([jnp.where(first, mine, other), jnp.where(first, other, mine)], axis=1)
@@ -585,7 +584,8 @@
     out_ref[...] = walls_ref[...] + GAIN * dot_hot(met - later_ref[...], elem_hot)
     copy = pltpu.make_async_copy(out_ref, out_hbm.at[pl.ds(256, 16), :], sem)
     copy.start()
-    solid.wait()
+    for sending in solid:
+        sending.wait()
     copy.wait()
 
 
@@ -683,7 +683,7 @@
     other = lax.ppermute(got2, "c", [(0, 1), (1, 0)])
     surface1, pay3 = call(
         solve_kernel,
-        [(N, N), (5 * N, HALF)],
+        [(SURFACE_ROWS, N), (5 * N, HALF)],
         [where, got2, other, modes, RESPONSE, Q_HALVES, sine_pair, x_pair, modes_pair, modes_t_pair,
          split_pair, decay, SURFACE_ROW],
         scalars=1,
@@ -700,8 +700,9 @@
     fluid2, trace1, slots, walls2 = call(
         second_kernel,
         [(320, count), (16, HALF), (N, HALF), (16, count)],
-        [where, fluid1, surface1, trace0, matrix, before, after, elem, owner, patch, Q_HALVES],
-        scalars=1,
+        [where, surface1, fluid1, trace0, matrix, before, after, elem, owner, patch, Q_HALVES],
+        specs=[smem, hbm] + [vmem] * 9,
+        scratch=[pltpu.VMEM((N, N), F32), pltpu.SemaphoreType.DMA],
         cost=2e9,
     )
     got3, fluid2, trace1, slots, walls2 = lax.optimization_barrier(
@@ -709,26 +710,18 @@
     )
     mine = got3.reshape(N, 5, 1, HALF)[:, 4].reshape(N, HALF)
     far_row = lax.ppermute(mine, "c", [(0, 1), (1, 0)])
-    (solid_out,) = call(
-        solid_kernel,
-        [(2 * N, HALF)],
-        [where, got3, Q_HALVES],
-        scalars=1,
-        out_specs=[hbm],
-        scratch=[pltpu.VMEM((N, HALF), F32), pltpu.SemaphoreType.DMA],
-    )
+    (solid_new,) = call(solid_kernel, [(2 * N, HALF)], [where, got3, Q_HALVES], scalars=1)
     fluid2, solid_out = call(
         last_kernel,
         [(320, count), (2 * N, HALF)],
-        [where, got3, mine, far_row, Q_HALVES, slots, trace1, elem, patch, walls2, fluid2, solid_out],
-        specs=[smem] + [vmem] * 9 + [hbm] * 2,
+        [where, solid_new, mine, far_row, Q_HALVES, slots, trace1, elem, patch, walls2, fluid2],
+        specs=[smem] + [vmem] * 9 + [hbm],
         out_specs=[hbm] * 2,
-        aliases={10: 0, 11: 1},
+        aliases={10: 0},
         scratch=[
             pltpu.VMEM((16, count), F32),
-            pltpu.VMEM((N, HALF), F32),
             pltpu.SemaphoreType.DMA,
-            pltpu.SemaphoreType.DMA,
+            pltpu.SemaphoreType.DMA((4,)),
         ],
     )
     return fluid2.reshape(fluid_state.shape), solid_out.reshape(solid_temp.shape)

time: 111 us -> 109 us (0.982)
    unnamed x49 -> x45, local copies, waits for them, and re-layouts: 8.73 us -> 8.02 us
  transfers between devices with their start and end apart: 7 -> 7, of which waited for: 4 -> 5; matrix products, arithmetic and copies ran while one was open for 1% -> 1% of each run, Pallas kernels for 15% -> 16%
where the time goes in v7:
time: 109 us
  starting transfers between devices  30.7 us (28%)
  Pallas kernels  26.2 us (24%)
  blocking collectives  22.6 us (21%)
  waiting for transfers between devices  19.6 us (18%)
  local copies, waits for them, and re-layouts  8.27 us (8%)
    pallas_call x10, Pallas kernels, call(): pl.pallas_call(kernel, out_shape=[jax.ShapeDtypeStruct(*(out if isinstanc...  26.2 us
    all_to_all x1, blocking collectives, exchange(): lax.all_to_all(chunks, axes, split_axis=0, concat_axis=0, tiled=True)  22.6 us
    all_to_all x2, starting transfers between devices, exchange(): lax.all_to_all(chunks, axes, split_axis=0, concat_axis=0, tiled=True)  18.9 us
    all_to_all x2, waiting for transfers between devices, exchange(): lax.all_to_all(chunks, axes, split_axis=0, concat_axis=0, tiled=True)  16 us
    unnamed x45, local copies, waits for them, and re-layouts  8.02 us
    ppermute x1, starting transfers between devices, on_device(): far = lax.ppermute(solid, 'g', [(0, 1), (1, 0)])  3.83 us
    ppermute x1, starting transfers between devices, on_device(): before = lax.ppermute(last, ALL, [(i, i + 1) for i in range(255)])  3.54 us
    ppermute x1, starting transfers between devices, on_device(): other = lax.ppermute(got2, 'c', [(0, 1), (1, 0)])  2.42 us
  transfers between devices with their start and end apart: 7, of which 5 were waited for; matrix products, arithmetic and copies ran while one was open for 1% of the time, Pallas kernels for 16%

profile of v7, /device:TPU:1, one launch (start us, length us, event | category | flops | bytes accessed | tf_op | source)
XLA Modules:
  0.0 108.6 jit_solution(16847682200180572000)
XLA Ops:
  0.6 3.8 %collective-permute-start = (f32[512,128]{1,0:T(8,128)}, f32[512,128]{1,0:T(8,128)S(1)}, u32[]{:S(2)}, u32[]{:S(2)}) collective-permute-start(f32[512,128]{1,0:T(8,128)} %bitcast.35), channel_id=1, source_target_pairs={{0,128},{128,0},{1,129},{129,1},{2,130},{130,2},{3,131},{131,3},{4... | collective-permute-start | bytes 786440 | tf_op jit(solution)/shard_map/ppermute | solution.py:625
  4.5 0.7 copy.25.jac_hbm
  5.2 0.9 copy-done
  6.2 0.9 copy-done.4
  7.1 0.9 copy-done.8
  8.1 0.7 copy-done.14
  8.7 0.7 copy-done.16
  9.4 0.7 copy-done.18
  10.0 3.3 %shard_map.176 = (f32[640,128]{1,0:T(8,128)S(1)}, f32[16,128]{1,0:T(8,128)S(1)}, f32[2,128]{1,0:T(2,128)S(1)}, f32[8,384]{1,0:T(8,128)S(1)}, f32[8,384]{1,0:T(8,...) custom-call(s32[3]{0:T(128)S(1)} %pad_add_fusion.where_ref, f32[3,5,5]{2,1,0:T(8,128)S(1)} %copy.25.jac_hbm, ...), custom_call_target="tpu_custom_call" | custom-call | flops 100000000 | bytes 1048576 | tf_op jit(solution)/shard_map/pallas_call | solution.py:595
  13.4 1.0 shard_map.177
  14.5 13.5 %all-to-all-start = ((f32[640,1,128]{2,1,0:T(1,128)}), f32[640,1,128]{2,1,0:T(1,128)S(1)}, u32[]{:S(2)}, u32[]{:S(2)}) async-start(f32[640,1,128]{2,1,0:T(1,128)} %bitcast.9), calls=%async_computation | async-start | bytes 655360 | tf_op jit(solution)/shard_map/all_to_all | solution.py:611
  27.9 3.5 %collective-permute-start.1 = (f32[8,384]{1,0:T(8,128)S(1)}, f32[8,384]{1,0:T(8,128)S(1)}, u32[]{:S(2)}, u32[]{:S(2)}) collective-permute-start(f32[8,384]{1,0:T(8,128)S(1)} %get-tuple-element.38), channel_id=1, source_target_pairs={{0,1},{1,2},{2,3},{3,4},{4,5},{5,6},{6,7},{7,8},{8,9},{9,10},{10,1... | collective-permute-start | bytes 36872 | tf_op jit(solution)/shard_map/ppermute | solution.py:644
  31.5 1.9 %collective-permute-start.2 = (f32[8,384]{1,0:T(8,128)S(1)}, f32[8,384]{1,0:T(8,128)S(1)}, u32[]{:S(2)}, u32[]{:S(2)}) collective-permute-start(f32[8,384]{1,0:T(8,128)S(1)} %get-tuple-element.39), channel_id=1, source_target_pairs={{1,0},{2,1},{3,2},{4,3},{5,4},{6,5},{7,6},{8,7},{9,8},{10,9},{11,1... | collective-permute-start | bytes 36872 | tf_op jit(solution)/shard_map/ppermute | solution.py:645
  33.5 0.9 shard_map.178
  34.3 0.7 copy-done.6
  35.0 2.0 %collective-permute-done.2.after_ref = f32[8,384]{1,0:T(8,128)S(1)} collective-permute-done((f32[8,384]{1,0:T(8,128)S(1)}, f32[8,384]{1,0:T(8,128)S(1)}, u32[]{:S(2)}, u32[]{:S(2)}) %collective-permute-start.2) | collective-permute-done | bytes 12320 | tf_op jit(solution)/shard_map/ppermute | solution.py:645
  37.1 5.5 %all-to-all-done = f32[640,1,128]{2,1,0:T(1,128)S(1)} async-done(((f32[640,1,128]{2,1,0:T(1,128)}), f32[640,1,128]{2,1,0:T(1,128)S(1)}, u32[]{:S(2)}, u32[]{:S(2)}) %all-to-all-start) | async-done | bytes 327712 | tf_op jit(solution)/shard_map/all_to_all | solution.py:611
  42.6 2.0 %shard_map.179 = (f32[256,256]{1,0:T(8,128)S(1)}, f32[640,128]{1,0:T(8,128)S(1)}) custom-call(s32[3]{0:T(128)S(1)} %pad_add_fusion.where_ref, f32[640,128]{1,0:T(8,128)S(1)} %bitcast.27, f32[2,128]{1,0:T(2,128)S(1)} %get-tuple-element.32.order_ref.surface_ref, bf16[2,256,256]{2,1,0:T(8,128)(2,1)S(1)} %get-tuple-element.33.sine_ref.pair_ref, ...), custom_call_target="tpu_custom_call" | custom-call | flops 100000000 | bytes 1048576 | tf_op jit(solution)/shard_map/pallas_call | solution.py:595
  44.6 22.6 %all_to_all.15 = f32[640,1,128]{2,1,0:T(1,128)S(1)} all-to-all(f32[640,1,128]{2,1,0:T(1,128)S(1)} %bitcast.34), channel_id=1, replica_groups=mesh['g'=2,'yl'=2,'x'=4,'z'=8,'c'=2] {'g','yl','x','z'}, dimensions={0} | all-to-all | bytes 655360 | tf_op jit(solution)/shard_map/all_to_all | solution.py:611
  67.2 2.4 %collective-permute-start.3 = (f32[640,128]{1,0:T(8,128)S(1)}, f32[640,128]{1,0:T(8,128)S(1)}, u32[]{:S(2)}, u32[]{:S(2)}) collective-permute-start(f32[640,128]{1,0:T(8,128)S(1)} %bitcast.28), channel_id=1, source_target_pairs={{0,1},{1,0},{2,3},{3,2},{4,5},{5,4},{6,7},{7,6},{8,9},{9,8},{10,11... | collective-permute-start | bytes 983048 | tf_op jit(solution)/shard_map/ppermute | solution.py:683
  69.6 1.3 %collective-permute-done.3.other_ref = f32[640,128]{1,0:T(8,128)S(1)} collective-permute-done((f32[640,128]{1,0:T(8,128)S(1)}, f32[640,128]{1,0:T(8,128)S(1)}, u32[]{:S(2)}, u32[]{:S(2)}) %collective-permute-start.3) | collective-permute-done | bytes 327712 | tf_op jit(solution)/shard_map/ppermute | solution.py:683
  70.9 4.2 %shard_map.180 = (f32[20480,256]{1,0:T(8,128)}, f32[1280,128]{1,0:T(8,128)}) custom-call(s32[3]{0:T(128)S(1)} %pad_add_fusion.where_ref, f32[640,128]{1,0:T(8,128)S(1)} %bitcast.29, f32[640,128]{1,0:T(8,128)S(1)} %collective-permute-done.3.other_ref, f32[256,256]{1,0:T(8,128)S(1)} %get-tuple-element.41.modes_ref, f32[256,256]{1,0:T(8,128)S(1)} %copy-done.5, ...), custom_call_target="tpu_custom_call" | custom-call | flops 100000000 | bytes 1048576 | tf_op jit(solution)/shard_map/pallas_call | solution.py:595
  75.1 5.4 %all-to-all-start.2 = ((f32[1280,1,128]{2,1,0:T(1,128)}), f32[1280,1,128]{2,1,0:T(1,128)S(1)}, u32[]{:S(2)}, u32[]{:S(2)}) async-start(f32[1280,1,128]{2,1,0:T(1,128)} %bitcast.15), calls=%async_computation.2 | async-start | bytes 1310720 | tf_op jit(solution)/shard_map/all_to_all | solution.py:611
  80.6 0.9 copy-done.11
  81.4 0.9 copy-done.12
  82.3 2.4 %shard_map.181.matrix_ref = f32[960,320]{1,0:T(8,128)S(1)} custom-call(f32[3,8,8]{2,1,0:T(8,128)S(1)} %pad.4.jac_ref, bf16[320,8]{1,0:T(8,128)(2,1)S(1)} %copy-done.11, bf16[320,64]{1,0:T(8,128)(2,1)S(1)} %copy-done.12, f32[3,320,320]{2,1,0:T(8,128)S(1)} %copy-done.2, f32[5,64,64]{2,1,0:T(8,128)S(1)} %copy-done.9), custom_call_target="tpu_custom_call" | custom-call | flops 100000000 | bytes 1048576 | tf_op jit(solution)/shard_map/pallas_call | solution.py:595
  84.7 3.4 %shard_map.182.fluid_ref = f32[320,1152]{1,0:T(8,128)S(1)} custom-call(s32[3]{0:T(128)S(1)} %pad_add_fusion.where_ref, f32[320,1024]{1,0:T(8,128)S(1)} %bitcast.31, f32[960,320]{1,0:T(8,128)S(1)} %shard_map.181.matrix_ref, f32[8,384]{1,0:T(8,128)S(1)} %collective-permute-done.1.before_ref, f32[8,384]{1,0:T(8,128)S(1)} %collective-permute-done.2.after_ref), custom_call_target="tpu_custom_call" | custom-call | flops 2000000000 | bytes 1048576 | tf_op jit(solution)/shard_map/pallas_call | solution.py:595
  88.1 6.1 %shard_map.183 = (f32[320,1024]{1,0:T(8,128)}, f32[16,128]{1,0:T(8,128)S(1)}, f32[256,128]{1,0:T(8,128)S(1)}, f32[16,1024]{1,0:T(8,128)S(1)}) custom-call(s32[3]{0:T(128)S(1)} %pad_add_fusion.where_ref, f32[20480,256]{1,0:T(8,128)} %get-tuple-element.45.surface_hbm, f32[320,1152]{1,0:T(8,128)S(1)} %shard_map.182.fluid_ref, ...), custom_call_target="tpu_custom_call" | custom-call | flops 2000000000 | bytes 1048576 | tf_op jit(solution)/shard_map/pallas_call | solution.py:595
  94.2 10.5 %all-to-all-done.2 = f32[1280,1,128]{2,1,0:T(1,128)S(1)} async-done(((f32[1280,1,128]{2,1,0:T(1,128)}), f32[1280,1,128]{2,1,0:T(1,128)S(1)}, u32[]{:S(2)}, u32[]{:S(2)}) %all-to-all-start.2) | async-done | bytes 655392 | tf_op jit(solution)/shard_map/all_to_all | solution.py:611
  105.1 0.9 shard_map.184.solid_ref
  106.1 0.3 collective-permute-done.4.other_ref
  106.4 2.0 %shard_map.185 = (f32[320,1024]{1,0:T(8,128)}, f32[512,128]{1,0:T(8,128)}) custom-call(s32[3]{0:T(128)S(1)} %pad_add_fusion.where_ref, f32[512,128]{1,0:T(8,128)S(1)} %shard_map.184.solid_ref, f32[256,128]{1,0:T(8,128)S(1)} %bitcast.33, f32[256,128]{1,0:T(8,128)S(1)} %collective-permute-done.4.other_ref, ...), custom_call_target="tpu_custom_call", output_to_operand_aliasing={{0}: (10, {})} | custom-call | flops 100000000 | bytes 1048576 | tf_op jit(solution)/shard_map/pallas_call | solution.py:595
  (42 shorter events, 0.6 us)
Async XLA Ops:
  0.6 12.8 %collective-permute-start = (f32[512,128]{1,0:T(8,128)}, f32[512,128]{1,0:T(8,128)S(1)}, u32[]{:S(2)}, u32[]{:S(2)}) collective-permute-start(f32[512,128]{1,0:T(8,128)} %bitcast.35), channel_id=1, source_target_pairs={{0,128},{128,0},{1,129},{129,1},{2,130},{130,2},{3,131},{131,3},{4... | collective-permute-start | bytes 786440 | tf_op jit(solution)/shard_map/ppermute | solution.py:625
  5.2 1.0 copy-start
  6.2 0.9 copy-start.4
  7.1 0.9 copy-start.8
  8.1 0.7 copy-start.14
  8.7 0.7 copy-start.16
  9.4 0.7 copy-start.18
  10.0 23.4 %copy-start.1 = (f32[512,128]{1,0:T(8,128)S(1)}, f32[512,128]{1,0:T(8,128)}, u32[]{:S(2)}) copy-start(f32[512,128]{1,0:T(8,128)} %constant.78.clone.sine_hbm.sine_ref) | copy-start | bytes 786436
  10.0 23.4 %copy-start.10 = (f32[256,1]{1,0:T(8,128)S(1)}, f32[256,1]{1,0:T(8,128)}, u32[]{:S(2)}) copy-start(f32[256,1]{1,0:T(8,128)} %constant.82.clone.rate_col_ref) | copy-start | bytes 3076
  10.0 23.4 %copy-start.20 = (f32[256]{0:T(256)S(1)}, f32[256]{0:T(256)}, u32[]{:S(2)}) copy-start(f32[256]{0:T(256)} %constant.80.clone.rate_ref) | copy-start | bytes 3076
  10.0 23.4 %copy-start.21 = (f32[1,256]{1,0:T(1,128)S(1)}, f32[1,256]{1,0:T(1,128)}, u32[]{:S(2)}) copy-start(f32[1,256]{1,0:T(1,128)} %constant.81.clone.rate_row_ref) | copy-start | bytes 3076
  13.4 29.2 %copy-start.13 = (f32[8,256]{1,0:T(8,128)S(1)}, f32[8,256]{1,0:T(8,128)}, u32[]{:S(2)}) copy-start(f32[8,256]{1,0:T(8,128)} %constant.87.clone.row_ref) | copy-start | bytes 24580
  13.4 29.2 %copy-start.15 = (s32[128]{0:T(128)S(1)}, s32[128]{0:T(128)}, u32[]{:S(2)}) copy-start(s32[128]{0:T(128)} %param.20) | copy-start | bytes 1540
  13.4 29.2 %copy-start.17 = (s32[128]{0:T(128)S(1)}, s32[128]{0:T(128)}, u32[]{:S(2)}) copy-start(s32[128]{0:T(128)} %param.22) | copy-start | bytes 1540
  13.4 29.2 %copy-start.19 = (s32[128,1]{0,1:T(1,128)S(1)}, s32[128,1]{0,1:T(1,128)}, u32[]{:S(2)}) copy-start(s32[128,1]{0,1:T(1,128)} %param.21) | copy-start | bytes 1540
  14.4 56.4 %copy-start.5 = (f32[256,256]{1,0:T(8,128)S(1)}, f32[256,256]{1,0:T(8,128)}, u32[]{:S(2)}) copy-start(f32[256,256]{1,0:T(8,128)} %constant.88.clone.response_ref) | copy-start | bytes 786436
  14.5 28.1 %all-to-all-start = ((f32[640,1,128]{2,1,0:T(1,128)}), f32[640,1,128]{2,1,0:T(1,128)S(1)}, u32[]{:S(2)}, u32[]{:S(2)}) async-start(f32[640,1,128]{2,1,0:T(1,128)} %bitcast.9), calls=%async_computation | async-start | bytes 655360 | tf_op jit(solution)/shard_map/all_to_all | solution.py:611
  27.9 7.1 %collective-permute-start.1 = (f32[8,384]{1,0:T(8,128)S(1)}, f32[8,384]{1,0:T(8,128)S(1)}, u32[]{:S(2)}, u32[]{:S(2)}) collective-permute-start(f32[8,384]{1,0:T(8,128)S(1)} %get-tuple-element.38), channel_id=1, source_target_pairs={{0,1},{1,2},{2,3},{3,4},{4,5},{5,6},{6,7},{7,8},{8,9},{9,10},{10,1... | collective-permute-start | bytes 36872 | tf_op jit(solution)/shard_map/ppermute | solution.py:644
  31.5 5.6 %collective-permute-start.2 = (f32[8,384]{1,0:T(8,128)S(1)}, f32[8,384]{1,0:T(8,128)S(1)}, u32[]{:S(2)}, u32[]{:S(2)}) collective-permute-start(f32[8,384]{1,0:T(8,128)S(1)} %get-tuple-element.39), channel_id=1, source_target_pairs={{1,0},{2,1},{3,2},{4,3},{5,4},{6,5},{7,6},{8,7},{9,8},{10,9},{11,1... | collective-permute-start | bytes 36872 | tf_op jit(solution)/shard_map/ppermute | solution.py:645
  34.3 0.7 copy-start.6
  42.6 28.3 %copy-start.7 = (bf16[2,256,256]{2,1,0:T(8,128)(2,1)S(1)}, bf16[2,256,256]{2,1,0:T(8,128)(2,1)}, u32[]{:S(2)}) copy-start(bf16[2,256,256]{2,1,0:T(8,128)(2,1)} %copy-done.6) | copy-start | bytes 786436
  67.2 3.7 %collective-permute-start.3 = (f32[640,128]{1,0:T(8,128)S(1)}, f32[640,128]{1,0:T(8,128)S(1)}, u32[]{:S(2)}, u32[]{:S(2)}) collective-permute-start(f32[640,128]{1,0:T(8,128)S(1)} %bitcast.28), channel_id=1, source_target_pairs={{0,1},{1,0},{2,3},{3,2},{4,5},{5,4},{6,7},{7,6},{8,9},{9,8},{10,11... | collective-permute-start | bytes 983048 | tf_op jit(solution)/shard_map/ppermute | solution.py:683
  70.9 9.7 %copy-start.2 = (f32[3,320,320]{2,1,0:T(8,128)S(1)}, f32[3,320,320]{2,1,0:T(8,128)}, u32[]{:S(2)}) copy-start(f32[3,320,320]{2,1,0:T(8,128)} %constant.85.clone.fixed_ref) | copy-start | bytes 3686404
  70.9 9.7 %copy-start.9 = (f32[5,64,64]{2,1,0:T(8,128)S(1)}, f32[5,64,64]{2,1,0:T(8,128)}, u32[]{:S(2)}) copy-start(f32[5,64,64]{2,1,0:T(8,128)} %constant.86.clone.operators_ref) | copy-start | bytes 245764
  75.1 29.6 %all-to-all-start.2 = ((f32[1280,1,128]{2,1,0:T(1,128)}), f32[1280,1,128]{2,1,0:T(1,128)S(1)}, u32[]{:S(2)}, u32[]{:S(2)}) async-start(f32[1280,1,128]{2,1,0:T(1,128)} %bitcast.15), calls=%async_computation.2 | async-start | bytes 1310720 | tf_op jit(solution)/shard_map/all_to_all | solution.py:611
  80.5 0.9 copy-start.11
  81.4 0.9 copy-start.12
  82.3 2.4 %copy-start.3 = (f32[5,64,1024]{2,1,0:T(8,128)S(1)}, f32[5,64,1024]{2,1,0:T(8,128)}, u32[]{:S(2)}) copy-start(f32[5,64,1024]{2,1,0:T(8,128)} %param.17) | copy-start | bytes 3932164
  105.0 1.4 %collective-permute-start.4 = (f32[256,128]{1,0:T(8,128)S(1)}, f32[256,128]{1,0:T(8,128)S(1)}, u32[]{:S(2)}, u32[]{:S(2)}) collective-permute-start(f32[256,128]{1,0:T(8,128)S(1)} %bitcast.32), channel_id=1, source_target_pairs={{0,1},{1,0},{2,3},{3,2},{4,5},{5,4},{6,7},{7,6},{8,9},{9,8},{10,11... | collective-permute-start | bytes 393224 | tf_op jit(solution)/shard_map/ppermute | solution.py:712

commit v8 on v7

--- a/solution.py
+++ b/solution.py
@@ -304,8 +304,8 @@
         (modes_t_out, split(by_modes.T)),
     ):
         out[0], out[1] = table
-    for i in range(2):
-        split_out[2 * i], split_out[2 * i + 1] = split(sine_rows(sine_ref, i, HALF, 2))
+    columns = [sine_rows(sine_ref, i, HALF, 2) for i in range(2)]
+    split_out[0], split_out[1] = split(jnp.concatenate(columns, axis=0))
     decay_out[...] = 1.0 / (rate_col_ref[...] + (rate_row_ref[...] + 64.0 * rate_ref[where_ref[2]]))
 
 
@@ -331,11 +331,12 @@
 ):
     group = where_ref[0]
     sine = sine_ref[0], sine_ref[1]
-    modes = 0.0
-    for i in range(2):
-        part = jnp.concatenate([rows(got_ref, 2 * i + h, HALF, 5) for h in range(2)], axis=1)
-        by_z = dot3(sine, part, NT)
-        modes = modes + dot3(by_z, (split_ref[2 * i], split_ref[2 * i + 1]))
+    parts = [
+        jnp.concatenate([rows(got_ref, 2 * i + h, HALF, 5) for h in range(2)], axis=1)
+        for i in range(2)
+    ]
+    by_z = dot3(sine, jnp.concatenate(parts, axis=0), NT)
+    modes = dot3(by_z, (split_ref[0], split_ref[1]))
     modes_ref[...] = modes
     surface_row = dot3(row_ref[...], decay_ref[...] * modes)[0:1]
 
@@ -411,18 +412,11 @@
     def block(g, r):
         return jnp.concatenate([ordered[r][k][g * 64 : (g + 1) * 64] for k in range(2)], axis=0)
 
-    halves = [
-        tuple(by_modes_ref[part, :, g * HALF : (g + 1) * HALF] for part in range(2))
-        for g in range(2)
-    ]
     by_x = x_ref[0], x_ref[1]
-    heat_modes = 0.0
-    for xl in range(2):
-        by_y = 0.0
-        for g in range(2):
-            by_y = by_y + dot3(halves[g], block(g, 2 + xl), NT)
-        at = slice(xl * HALF, (xl + 1) * HALF)
-        heat_modes = heat_modes + dot3(by_y, (by_x[0][at], by_x[1][at]))
+    heat = jnp.concatenate(
+        [jnp.concatenate([block(g, 2 + xl) for g in range(2)], axis=1) for xl in range(2)], axis=0
+    )
+    heat_modes = dot3(dot3((by_modes_ref[0], by_modes_ref[1]), heat, NT), by_x)
     heat_ref[...] = heat_modes
     given = jnp.concatenate(
         [jnp.concatenate([ordered[h][k] for h in range(2)], axis=1) for k in range(2)], axis=0
@@ -465,10 +459,11 @@
     final_row = dot3(row_ref[...], final)[0:1]
     final = split(final)
     sine = pair_ref[0], pair_ref[1]
+    back = dot3(dot3((split_ref[0], split_ref[1]), final, NT), sine)
     for xl in range(2):
-        part = dot3(dot3((split_ref[2 * xl], split_ref[2 * xl + 1]), final, NT), sine)
         for h in range(2):
-            out_ref[pl.ds(2 * xl + h, HALF, 5), :] = part[:, h * HALF : (h + 1) * HALF]
+            part = back[xl * HALF : (xl + 1) * HALF, h * HALF : (h + 1) * HALF]
+            out_ref[pl.ds(2 * xl + h, HALF, 5), :] = part
     for k in range(2):
         out_ref[pl.ds(4 + 5 * k, 64, 10), :] = jnp.broadcast_to(
             final_row[:, k * HALF : (k + 1) * HALF], (64, HALF)
@@ -561,10 +556,12 @@
 
 def solid_kernel(where_ref, got_ref, sine_ref, solid_ref):
     by_y = split(sine_ref[pl.ds(pl.multiple_of(where_ref[0] * N, N), N), :])
+    parts = jnp.concatenate([rows(got_ref, i, N, 5) for i in range(4)], axis=1)
+    solid = dot3(parts, by_y, TN)
     for xl in range(2):
         for h in range(2):
-            part = rows(got_ref, 2 * xl + h, N, 5)
-            solid_ref[pl.ds(h * N + xl, HALF, 2), :] = dot3(part, by_y, TN)
+            at = (2 * xl + h) * HALF
+            solid_ref[pl.ds(h * N + xl, HALF, 2), :] = solid[at : at + HALF]
 
 
 def last_kernel(
@@ -654,7 +651,7 @@
     tables = call(
         tables_kernel,
         [((2, N, N), BF16)] * 4
-        + [((4, HALF, N), BF16), (N, N)],
+        + [((2, N, N), BF16), (N, N)],
         [where, RATE_LIST, Q_HALVES, RATE_ROW, RATE_COLUMN, surface0],
         scalars=2,
     )

time: 109 us -> 109 us (level)
  no operation moved by 1% of the time
where the time goes in v8:
time: 109 us; the launch traced here: 108 us
  starting transfers between devices  30.7 us (28%)
  Pallas kernels  25.8 us (24%)
  blocking collectives  22.6 us (21%)
  waiting for transfers between devices  19.6 us (18%)
  local copies, waits for them, and re-layouts  8.27 us (8%)
    pallas_call x10, Pallas kernels, call(): pl.pallas_call(kernel, out_shape=[jax.ShapeDtypeStruct(*(out if isinstanc...  25.8 us
    all_to_all x1, blocking collectives, exchange(): lax.all_to_all(chunks, axes, split_axis=0, concat_axis=0, tiled=True)  22.6 us
    all_to_all x2, starting transfers between devices, exchange(): lax.all_to_all(chunks, axes, split_axis=0, concat_axis=0, tiled=True)  18.9 us
    all_to_all x2, waiting for transfers between devices, exchange(): lax.all_to_all(chunks, axes, split_axis=0, concat_axis=0, tiled=True)  16 us
    unnamed x45, local copies, waits for them, and re-layouts  8.02 us
    ppermute x1, starting transfers between devices, on_device(): far = lax.ppermute(solid, 'g', [(0, 1), (1, 0)])  3.83 us
    ppermute x1, starting transfers between devices, on_device(): before = lax.ppermute(last, ALL, [(i, i + 1) for i in range(255)])  3.54 us
    ppermute x1, starting transfers between devices, on_device(): other = lax.ppermute(got2, 'c', [(0, 1), (1, 0)])  2.42 us
  transfers between devices with their start and end apart: 7, of which 5 were waited for; matrix products, arithmetic and copies ran while one was open for 1% of the time, Pallas kernels for 16%

profile of v8, /device:TPU:1, one launch (start us, length us, event | category | flops | bytes accessed | tf_op | source)
XLA Modules:
  0.0 108.1 jit_solution(5428472286819942989)
XLA Ops:
  0.6 3.8 %collective-permute-start = (f32[512,128]{1,0:T(8,128)}, f32[512,128]{1,0:T(8,128)S(1)}, u32[]{:S(2)}, u32[]{:S(2)}) collective-permute-start(f32[512,128]{1,0:T(8,128)} %bitcast.35), channel_id=1, source_target_pairs={{0,128},{128,0},{1,129},{129,1},{2,130},{130,2},{3,131},{131,3},{4... | collective-permute-start | bytes 786440 | tf_op jit(solution)/shard_map/ppermute | solution.py:622
  4.5 0.7 copy.25.jac_hbm
  5.2 0.9 copy-done
  6.2 0.9 copy-done.4
  7.1 0.9 copy-done.8
  8.1 0.7 copy-done.14
  8.7 0.7 copy-done.16
  9.4 0.7 copy-done.18
  10.0 3.3 %shard_map.176 = (f32[640,128]{1,0:T(8,128)S(1)}, f32[16,128]{1,0:T(8,128)S(1)}, f32[2,128]{1,0:T(2,128)S(1)}, f32[8,384]{1,0:T(8,128)S(1)}, f32[8,384]{1,0:T(8,...) custom-call(s32[3]{0:T(128)S(1)} %pad_add_fusion.where_ref, f32[3,5,5]{2,1,0:T(8,128)S(1)} %copy.25.jac_hbm, ...), custom_call_target="tpu_custom_call" | custom-call | flops 100000000 | bytes 1048576 | tf_op jit(solution)/shard_map/pallas_call | solution.py:592
  13.4 1.0 shard_map.177
  14.5 13.5 %all-to-all-start = ((f32[640,1,128]{2,1,0:T(1,128)}), f32[640,1,128]{2,1,0:T(1,128)S(1)}, u32[]{:S(2)}, u32[]{:S(2)}) async-start(f32[640,1,128]{2,1,0:T(1,128)} %bitcast.9), calls=%async_computation | async-start | bytes 655360 | tf_op jit(solution)/shard_map/all_to_all | solution.py:608
  27.9 3.5 %collective-permute-start.1 = (f32[8,384]{1,0:T(8,128)S(1)}, f32[8,384]{1,0:T(8,128)S(1)}, u32[]{:S(2)}, u32[]{:S(2)}) collective-permute-start(f32[8,384]{1,0:T(8,128)S(1)} %get-tuple-element.38), channel_id=1, source_target_pairs={{0,1},{1,2},{2,3},{3,4},{4,5},{5,6},{6,7},{7,8},{8,9},{9,10},{10,1... | collective-permute-start | bytes 36872 | tf_op jit(solution)/shard_map/ppermute | solution.py:641
  31.5 1.9 %collective-permute-start.2 = (f32[8,384]{1,0:T(8,128)S(1)}, f32[8,384]{1,0:T(8,128)S(1)}, u32[]{:S(2)}, u32[]{:S(2)}) collective-permute-start(f32[8,384]{1,0:T(8,128)S(1)} %get-tuple-element.39), channel_id=1, source_target_pairs={{1,0},{2,1},{3,2},{4,3},{5,4},{6,5},{7,6},{8,7},{9,8},{10,9},{11,1... | collective-permute-start | bytes 36872 | tf_op jit(solution)/shard_map/ppermute | solution.py:642
  33.5 0.9 shard_map.178
  34.4 0.7 copy-done.6
  35.0 2.0 %collective-permute-done.2.after_ref = f32[8,384]{1,0:T(8,128)S(1)} collective-permute-done((f32[8,384]{1,0:T(8,128)S(1)}, f32[8,384]{1,0:T(8,128)S(1)}, u32[]{:S(2)}, u32[]{:S(2)}) %collective-permute-start.2) | collective-permute-done | bytes 12320 | tf_op jit(solution)/shard_map/ppermute | solution.py:642
  37.1 5.5 %all-to-all-done = f32[640,1,128]{2,1,0:T(1,128)S(1)} async-done(((f32[640,1,128]{2,1,0:T(1,128)}), f32[640,1,128]{2,1,0:T(1,128)S(1)}, u32[]{:S(2)}, u32[]{:S(2)}) %all-to-all-start) | async-done | bytes 327712 | tf_op jit(solution)/shard_map/all_to_all | solution.py:608
  42.6 1.8 %shard_map.179 = (f32[256,256]{1,0:T(8,128)S(1)}, f32[640,128]{1,0:T(8,128)S(1)}) custom-call(s32[3]{0:T(128)S(1)} %pad_add_fusion.where_ref, f32[640,128]{1,0:T(8,128)S(1)} %bitcast.27, f32[2,128]{1,0:T(2,128)S(1)} %get-tuple-element.32.order_ref.surface_ref, bf16[2,256,256]{2,1,0:T(8,128)(2,1)S(1)} %get-tuple-element.33.sine_ref.pair_ref, ...), custom_call_target="tpu_custom_call" | custom-call | flops 100000000 | bytes 1048576 | tf_op jit(solution)/shard_map/pallas_call | solution.py:592
  44.4 22.6 %all_to_all.15 = f32[640,1,128]{2,1,0:T(1,128)S(1)} all-to-all(f32[640,1,128]{2,1,0:T(1,128)S(1)} %bitcast.34), channel_id=1, replica_groups=mesh['g'=2,'yl'=2,'x'=4,'z'=8,'c'=2] {'g','yl','x','z'}, dimensions={0} | all-to-all | bytes 655360 | tf_op jit(solution)/shard_map/all_to_all | solution.py:608
  67.0 2.4 %collective-permute-start.3 = (f32[640,128]{1,0:T(8,128)S(1)}, f32[640,128]{1,0:T(8,128)S(1)}, u32[]{:S(2)}, u32[]{:S(2)}) collective-permute-start(f32[640,128]{1,0:T(8,128)S(1)} %bitcast.28), channel_id=1, source_target_pairs={{0,1},{1,0},{2,3},{3,2},{4,5},{5,4},{6,7},{7,6},{8,9},{9,8},{10,11... | collective-permute-start | bytes 983048 | tf_op jit(solution)/shard_map/ppermute | solution.py:680
  69.5 1.3 %collective-permute-done.3.other_ref = f32[640,128]{1,0:T(8,128)S(1)} collective-permute-done((f32[640,128]{1,0:T(8,128)S(1)}, f32[640,128]{1,0:T(8,128)S(1)}, u32[]{:S(2)}, u32[]{:S(2)}) %collective-permute-start.3) | collective-permute-done | bytes 327712 | tf_op jit(solution)/shard_map/ppermute | solution.py:680
  70.7 3.9 %shard_map.180 = (f32[20480,256]{1,0:T(8,128)}, f32[1280,128]{1,0:T(8,128)}) custom-call(s32[3]{0:T(128)S(1)} %pad_add_fusion.where_ref, f32[640,128]{1,0:T(8,128)S(1)} %bitcast.29, f32[640,128]{1,0:T(8,128)S(1)} %collective-permute-done.3.other_ref, f32[256,256]{1,0:T(8,128)S(1)} %get-tuple-element.41.modes_ref, f32[256,256]{1,0:T(8,128)S(1)} %copy-done.5, ...), custom_call_target="tpu_custom_call" | custom-call | flops 100000000 | bytes 1048576 | tf_op jit(solution)/shard_map/pallas_call | solution.py:592
  74.6 5.4 %all-to-all-start.2 = ((f32[1280,1,128]{2,1,0:T(1,128)}), f32[1280,1,128]{2,1,0:T(1,128)S(1)}, u32[]{:S(2)}, u32[]{:S(2)}) async-start(f32[1280,1,128]{2,1,0:T(1,128)} %bitcast.15), calls=%async_computation.2 | async-start | bytes 1310720 | tf_op jit(solution)/shard_map/all_to_all | solution.py:608
  80.0 0.9 copy-done.11
  80.9 0.9 copy-done.12
  81.8 2.4 %shard_map.181.matrix_ref = f32[960,320]{1,0:T(8,128)S(1)} custom-call(f32[3,8,8]{2,1,0:T(8,128)S(1)} %pad.4.jac_ref, bf16[320,8]{1,0:T(8,128)(2,1)S(1)} %copy-done.11, bf16[320,64]{1,0:T(8,128)(2,1)S(1)} %copy-done.12, f32[3,320,320]{2,1,0:T(8,128)S(1)} %copy-done.2, f32[5,64,64]{2,1,0:T(8,128)S(1)} %copy-done.9), custom_call_target="tpu_custom_call" | custom-call | flops 100000000 | bytes 1048576 | tf_op jit(solution)/shard_map/pallas_call | solution.py:592
  84.2 3.4 %shard_map.182.fluid_ref = f32[320,1152]{1,0:T(8,128)S(1)} custom-call(s32[3]{0:T(128)S(1)} %pad_add_fusion.where_ref, f32[320,1024]{1,0:T(8,128)S(1)} %bitcast.31, f32[960,320]{1,0:T(8,128)S(1)} %shard_map.181.matrix_ref, f32[8,384]{1,0:T(8,128)S(1)} %collective-permute-done.1.before_ref, f32[8,384]{1,0:T(8,128)S(1)} %collective-permute-done.2.after_ref), custom_call_target="tpu_custom_call" | custom-call | flops 2000000000 | bytes 1048576 | tf_op jit(solution)/shard_map/pallas_call | solution.py:592
  87.6 6.1 %shard_map.183 = (f32[320,1024]{1,0:T(8,128)}, f32[16,128]{1,0:T(8,128)S(1)}, f32[256,128]{1,0:T(8,128)S(1)}, f32[16,1024]{1,0:T(8,128)S(1)}) custom-call(s32[3]{0:T(128)S(1)} %pad_add_fusion.where_ref, f32[20480,256]{1,0:T(8,128)} %get-tuple-element.45.surface_hbm, f32[320,1152]{1,0:T(8,128)S(1)} %shard_map.182.fluid_ref, ...), custom_call_target="tpu_custom_call" | custom-call | flops 2000000000 | bytes 1048576 | tf_op jit(solution)/shard_map/pallas_call | solution.py:592
  93.7 10.5 %all-to-all-done.2 = f32[1280,1,128]{2,1,0:T(1,128)S(1)} async-done(((f32[1280,1,128]{2,1,0:T(1,128)}), f32[1280,1,128]{2,1,0:T(1,128)S(1)}, u32[]{:S(2)}, u32[]{:S(2)}) %all-to-all-start.2) | async-done | bytes 655392 | tf_op jit(solution)/shard_map/all_to_all | solution.py:608
  104.6 1.0 shard_map.184.solid_ref
  105.6 0.3 collective-permute-done.4.other_ref
  105.9 2.0 %shard_map.185 = (f32[320,1024]{1,0:T(8,128)}, f32[512,128]{1,0:T(8,128)}) custom-call(s32[3]{0:T(128)S(1)} %pad_add_fusion.where_ref, f32[512,128]{1,0:T(8,128)S(1)} %shard_map.184.solid_ref, f32[256,128]{1,0:T(8,128)S(1)} %bitcast.33, f32[256,128]{1,0:T(8,128)S(1)} %collective-permute-done.4.other_ref, ...), custom_call_target="tpu_custom_call", output_to_operand_aliasing={{0}: (10, {})} | custom-call | flops 100000000 | bytes 1048576 | tf_op jit(solution)/shard_map/pallas_call | solution.py:592
  (42 shorter events, 0.6 us)
Async XLA Ops:
  0.6 12.8 %collective-permute-start = (f32[512,128]{1,0:T(8,128)}, f32[512,128]{1,0:T(8,128)S(1)}, u32[]{:S(2)}, u32[]{:S(2)}) collective-permute-start(f32[512,128]{1,0:T(8,128)} %bitcast.35), channel_id=1, source_target_pairs={{0,128},{128,0},{1,129},{129,1},{2,130},{130,2},{3,131},{131,3},{4... | collective-permute-start | bytes 786440 | tf_op jit(solution)/shard_map/ppermute | solution.py:622
  5.2 1.0 copy-start
  6.2 0.9 copy-start.4
  7.1 0.9 copy-start.8
  8.1 0.7 copy-start.14
  8.7 0.7 copy-start.16
  9.4 0.7 copy-start.18
  10.0 23.4 %copy-start.1 = (f32[512,128]{1,0:T(8,128)S(1)}, f32[512,128]{1,0:T(8,128)}, u32[]{:S(2)}) copy-start(f32[512,128]{1,0:T(8,128)} %constant.78.clone.sine_hbm.sine_ref) | copy-start | bytes 786436
  10.0 23.4 %copy-start.10 = (f32[256,1]{1,0:T(8,128)S(1)}, f32[256,1]{1,0:T(8,128)}, u32[]{:S(2)}) copy-start(f32[256,1]{1,0:T(8,128)} %constant.82.clone.rate_col_ref) | copy-start | bytes 3076
  10.0 23.4 %copy-start.20 = (f32[256]{0:T(256)S(1)}, f32[256]{0:T(256)}, u32[]{:S(2)}) copy-start(f32[256]{0:T(256)} %constant.80.clone.rate_ref) | copy-start | bytes 3076
  10.0 23.4 %copy-start.21 = (f32[1,256]{1,0:T(1,128)S(1)}, f32[1,256]{1,0:T(1,128)}, u32[]{:S(2)}) copy-start(f32[1,256]{1,0:T(1,128)} %constant.81.clone.rate_row_ref) | copy-start | bytes 3076
  13.4 29.2 %copy-start.13 = (f32[8,256]{1,0:T(8,128)S(1)}, f32[8,256]{1,0:T(8,128)}, u32[]{:S(2)}) copy-start(f32[8,256]{1,0:T(8,128)} %constant.87.clone.row_ref) | copy-start | bytes 24580
  13.4 29.2 %copy-start.15 = (s32[128]{0:T(128)S(1)}, s32[128]{0:T(128)}, u32[]{:S(2)}) copy-start(s32[128]{0:T(128)} %param.20) | copy-start | bytes 1540
  13.4 29.2 %copy-start.17 = (s32[128]{0:T(128)S(1)}, s32[128]{0:T(128)}, u32[]{:S(2)}) copy-start(s32[128]{0:T(128)} %param.22) | copy-start | bytes 1540
  13.4 29.2 %copy-start.19 = (s32[128,1]{0,1:T(1,128)S(1)}, s32[128,1]{0,1:T(1,128)}, u32[]{:S(2)}) copy-start(s32[128,1]{0,1:T(1,128)} %param.21) | copy-start | bytes 1540
  14.4 56.3 %copy-start.5 = (f32[256,256]{1,0:T(8,128)S(1)}, f32[256,256]{1,0:T(8,128)}, u32[]{:S(2)}) copy-start(f32[256,256]{1,0:T(8,128)} %constant.88.clone.response_ref) | copy-start | bytes 786436
  14.5 28.1 %all-to-all-start = ((f32[640,1,128]{2,1,0:T(1,128)}), f32[640,1,128]{2,1,0:T(1,128)S(1)}, u32[]{:S(2)}, u32[]{:S(2)}) async-start(f32[640,1,128]{2,1,0:T(1,128)} %bitcast.9), calls=%async_computation | async-start | bytes 655360 | tf_op jit(solution)/shard_map/all_to_all | solution.py:608
  27.9 7.1 %collective-permute-start.1 = (f32[8,384]{1,0:T(8,128)S(1)}, f32[8,384]{1,0:T(8,128)S(1)}, u32[]{:S(2)}, u32[]{:S(2)}) collective-permute-start(f32[8,384]{1,0:T(8,128)S(1)} %get-tuple-element.38), channel_id=1, source_target_pairs={{0,1},{1,2},{2,3},{3,4},{4,5},{5,6},{6,7},{7,8},{8,9},{9,10},{10,1... | collective-permute-start | bytes 36872 | tf_op jit(solution)/shard_map/ppermute | solution.py:641
  31.5 5.6 %collective-permute-start.2 = (f32[8,384]{1,0:T(8,128)S(1)}, f32[8,384]{1,0:T(8,128)S(1)}, u32[]{:S(2)}, u32[]{:S(2)}) collective-permute-start(f32[8,384]{1,0:T(8,128)S(1)} %get-tuple-element.39), channel_id=1, source_target_pairs={{1,0},{2,1},{3,2},{4,3},{5,4},{6,5},{7,6},{8,7},{9,8},{10,9},{11,1... | collective-permute-start | bytes 36872 | tf_op jit(solution)/shard_map/ppermute | solution.py:642
  34.3 0.7 copy-start.6
  42.6 28.2 %copy-start.7 = (bf16[2,256,256]{2,1,0:T(8,128)(2,1)S(1)}, bf16[2,256,256]{2,1,0:T(8,128)(2,1)}, u32[]{:S(2)}) copy-start(bf16[2,256,256]{2,1,0:T(8,128)(2,1)} %copy-done.6) | copy-start | bytes 786436
  67.0 3.7 %collective-permute-start.3 = (f32[640,128]{1,0:T(8,128)S(1)}, f32[640,128]{1,0:T(8,128)S(1)}, u32[]{:S(2)}, u32[]{:S(2)}) collective-permute-start(f32[640,128]{1,0:T(8,128)S(1)} %bitcast.28), channel_id=1, source_target_pairs={{0,1},{1,0},{2,3},{3,2},{4,5},{5,4},{6,7},{7,6},{8,9},{9,8},{10,11... | collective-permute-start | bytes 983048 | tf_op jit(solution)/shard_map/ppermute | solution.py:680
  70.7 9.3 %copy-start.2 = (f32[3,320,320]{2,1,0:T(8,128)S(1)}, f32[3,320,320]{2,1,0:T(8,128)}, u32[]{:S(2)}) copy-start(f32[3,320,320]{2,1,0:T(8,128)} %constant.85.clone.fixed_ref) | copy-start | bytes 3686404
  70.7 9.3 %copy-start.9 = (f32[5,64,64]{2,1,0:T(8,128)S(1)}, f32[5,64,64]{2,1,0:T(8,128)}, u32[]{:S(2)}) copy-start(f32[5,64,64]{2,1,0:T(8,128)} %constant.86.clone.operators_ref) | copy-start | bytes 245764
  74.6 29.6 %all-to-all-start.2 = ((f32[1280,1,128]{2,1,0:T(1,128)}), f32[1280,1,128]{2,1,0:T(1,128)S(1)}, u32[]{:S(2)}, u32[]{:S(2)}) async-start(f32[1280,1,128]{2,1,0:T(1,128)} %bitcast.15), calls=%async_computation.2 | async-start | bytes 1310720 | tf_op jit(solution)/shard_map/all_to_all | solution.py:608
  80.0 0.9 copy-start.11
  80.9 0.9 copy-start.12
  81.8 2.4 %copy-start.3 = (f32[5,64,1024]{2,1,0:T(8,128)S(1)}, f32[5,64,1024]{2,1,0:T(8,128)}, u32[]{:S(2)}) copy-start(f32[5,64,1024]{2,1,0:T(8,128)} %param.17) | copy-start | bytes 3932164
  104.5 1.4 %collective-permute-start.4 = (f32[256,128]{1,0:T(8,128)S(1)}, f32[256,128]{1,0:T(8,128)S(1)}, u32[]{:S(2)}, u32[]{:S(2)}) collective-permute-start(f32[256,128]{1,0:T(8,128)S(1)} %bitcast.32), channel_id=1, source_target_pairs={{0,1},{1,0},{2,3},{3,2},{4,5},{5,4},{6,7},{7,6},{8,9},{9,8},{10,11... | collective-permute-start | bytes 393224 | tf_op jit(solution)/shard_map/ppermute | solution.py:709
